TPU v7x, 32 devices: a whole 2x2x4 slice. The times are simulated.
32 devices in a mesh: req: 8 (over y, x, core), tp: 4 (over z).
Axes of the slice: x: 2, y: 2, z: 4, core: 2. Of those that a mesh axis runs over, the one named last changes fastest.
Arguments:
- hidden: bfloat16 [2048, 5120], P('req', 'tp'), may hold values from -8 to 8
- q_new: bfloat16 [2048, 5120], P('req', 'tp'), may hold values from -8 to 8
- k_new: bfloat16 [2048, 5120], P('req', 'tp'), may hold values from -8 to 8
- v_new: bfloat16 [2048, 5120], P('req', 'tp'), may hold values from -8 to 8
- cache_k: bfloat16 [8, 4096, 5120], P('req', None, 'tp'), may hold values from -8 to 8
- cache_v: bfloat16 [8, 4096, 5120], P('req', None, 'tp'), may hold values from -8 to 8
- cache_len: int32 [8], replicated, may hold values from 1 to 4096, 8192 in all
- w_out: bfloat16 [5120, 5120], P('tp', 'req'), may hold values from -0.625 to 0.625
- q_cross: bfloat16 [2048, 5120], P('req', 'tp'), may hold values from -8 to 8
- text_k: bfloat16 [4, 512, 5120], P(None, 'req', 'tp'), may hold values from -8 to 8
- text_v: bfloat16 [4, 512, 5120], P(None, 'req', 'tp'), may hold values from -12 to 12
- prompt_of: int32 [8], P('req'), may hold values from 0 to 3, as said below
Outputs:
- hidden_out: bfloat16 [2048, 5120], P('req', 'tp')
- cross_heads: bfloat16 [2048, 5120], P('req', 'tp')
Inputs may be any that keep to these rules, and one draw needn't show every extreme that they name: `cache_len`: cache rows at or beyond a request's length hold no data; the longest request fills all 4096 rows. `prompt_of`: each of the 4 prompts serves exactly 2 requests.
All inputs are finite; a program needn't handle non-finite values.
Results may differ from a plain program's by a relative error of at most 0.014.
Values may be sent and summed in bfloat16 or wider, within the bound.
No kernel may reach another device: no remote copies, remote signals or barrier semaphores. Data moves between devices by JAX's collectives and lax.ppermute only.
A program may use at most 128 MiB of HBM per device.

v0:
```python
import jax
import jax.numpy as jnp
from jax import lax
from jax.sharding import PartitionSpec as P

HD = 128
BLOCK = 512


NEG_FILL = -1e30


def attend(running, queries, key_block, value_block, visible, score_scale):
    totals, maxima, masses = running
    scores = (
        jnp.einsum("qhd,khd->hqk", queries, key_block, preferred_element_type=jnp.float32)
        * score_scale
    )
    scores = jnp.where(visible[None], scores, NEG_FILL)
    top_new = jnp.maximum(maxima, jnp.max(scores, axis=-1))
    weights = jnp.where(visible[None], jnp.exp(scores - top_new[..., None]), 0.0)
    shrink = jnp.exp(maxima - top_new)
    masses = masses * shrink + jnp.sum(weights, axis=-1)
    totals = totals * shrink[..., None] + jnp.einsum(
        "hqk,khd->hqd",
        weights.astype(jnp.bfloat16),
        value_block,
        preferred_element_type=jnp.float32,
    )
    return (totals, top_new, masses)


def cache_pass(
    running, queries, key_rows, value_rows, block_count, row_limit, block_rows, score_scale
):
    query_rows = queries.shape[0]

    def visit_block(block_index, carried):
        first_row = block_index * block_rows
        key_block = lax.dynamic_slice_in_dim(key_rows, first_row, block_rows, 0)
        value_block = lax.dynamic_slice_in_dim(value_rows, first_row, block_rows, 0)
        live_rows = first_row + jnp.arange(block_rows, dtype=jnp.int32) < row_limit
        visible = jnp.broadcast_to(live_rows[None, :], (query_rows, block_rows))
        return attend(carried, queries, key_block, value_block, visible, score_scale)

    return lax.fori_loop(0, block_count, visit_block, running)


def finish_heads(running):
    totals, maxima, masses = running
    output = totals / masses[..., None]
    return (
        output.transpose(1, 0, 2)
        .reshape(totals.shape[1], totals.shape[0] * totals.shape[2])
        .astype(jnp.bfloat16)
    )


def per_device(
    hidden,
    q_new,
    k_new,
    v_new,
    cache_k,
    cache_v,
    cache_len,
    w_out,
    q_cross,
    text_k,
    text_v,
    prompt_of,
):
    row_count, width_local = q_new.shape
    head_count = width_local // HD
    capacity = cache_k.shape[1]
    score_scale = HD ** (-0.5)
    block_rows = BLOCK
    queries = q_new.reshape(row_count, head_count, HD)
    new_keys = k_new.reshape(row_count, head_count, HD)
    new_values = v_new.reshape(row_count, head_count, HD)
    cached_keys = cache_k[0].reshape(capacity, head_count, HD)
    cached_values = cache_v[0].reshape(capacity, head_count, HD)
    req_place = lax.axis_index("req")
    length = lax.dynamic_index_in_dim(cache_len, req_place, 0, keepdims=False)
    empty_state = (
        jnp.zeros((head_count, row_count, HD), jnp.float32),
        jnp.full((head_count, row_count), NEG_FILL, jnp.float32),
        jnp.zeros((head_count, row_count), jnp.float32),
    )
    blocks_live = (length + block_rows - 1) // block_rows
    running = cache_pass(
        empty_state,
        queries,
        cached_keys,
        cached_values,
        blocks_live,
        length,
        block_rows,
        score_scale,
    )
    row_ids = jnp.arange(row_count, dtype=jnp.int32)
    causal = row_ids[:, None] >= row_ids[None, :]
    running = attend(running, queries, new_keys, new_values, causal, score_scale)
    self_heads = finish_heads(running)
    terms = jnp.dot(
        self_heads,
        lax.all_gather(w_out, "req", axis=1, tiled=True),
        preferred_element_type=jnp.float32,
    )
    summed = lax.psum_scatter(
        terms.astype(jnp.bfloat16), "tp", scatter_dimension=1, tiled=True
    ).astype(jnp.float32)
    hidden_out = (hidden.astype(jnp.float32) + summed).astype(jnp.bfloat16)
    prompt = prompt_of[0]
    cross_queries = q_cross.reshape(row_count, head_count, HD)
    text_keys = lax.dynamic_index_in_dim(
        lax.all_gather(text_k, "req", axis=1, tiled=True), prompt, 0, keepdims=False
    )
    text_values = lax.dynamic_index_in_dim(
        lax.all_gather(text_v, "req", axis=1, tiled=True), prompt, 0, keepdims=False
    )
    piece_rows = text_keys.shape[0]
    text_keys = text_keys.reshape(piece_rows, head_count, HD)
    text_values = text_values.reshape(piece_rows, head_count, HD)
    visible = jnp.ones((row_count, piece_rows), dtype=bool)
    crossed = attend(empty_state, cross_queries, text_keys, text_values, visible, score_scale)
    cross_heads = finish_heads(crossed)
    return (hidden_out, cross_heads)


def solution(mesh):
    placed = (
        P("req", "tp"),
        P("req", "tp"),
        P("req", "tp"),
        P("req", "tp"),
        P("req", None, "tp"),
        P("req", None, "tp"),
        P(),
        P("tp", "req"),
        P("req", "tp"),
        P(None, "req", "tp"),
        P(None, "req", "tp"),
        P("req"),
    )
    return jax.shard_map(
        per_device,
        mesh=mesh,
        in_specs=placed,
        out_specs=(P("req", "tp"), P("req", "tp")),
        check_vma=False,
    )
```

profile of v0, /device:TPU:0, one launch (start us, length us, event | category | flops | bytes accessed | tf_op | source)
XLA Modules:
  0.0 236.4 jit_solution(2130854359876161292)
XLA Ops:
  8.0 2.4 %copy.56 = bf16[4,64,1280]{2,0,1:T(4,128)(2,1)} copy(bf16[4,64,1280]{2,1,0:T(8,128)(2,1)} %param.23) | data formatting | bytes 1310720 | tf_op args[9]
  13.2 14.6 %copy.44 = bf16[1,4096,1280]{1,2,0:T(8,128)(2,1)} copy(bf16[1,4096,1280]{2,1,0:T(8,128)(2,1)} %param.18) | data formatting | bytes 20971520 | tf_op args[4]
  27.7 14.3 %copy.46 = bf16[1,4096,1280]{1,2,0:T(8,128)(2,1)} copy(bf16[1,4096,1280]{2,1,0:T(8,128)(2,1)} %param.19) | data formatting | bytes 20971520 | tf_op args[5]
  42.4 9.4 %while.14 = (s32[]{:T(128)}, f32[10,256,128]{2,1,0:T(8,128)S(1)}, f32[10,256]{1,0:T(8,128)S(1)}, f32[10,256]{1,0:T(8,128)S(1)}, s32[]{:T(128)}, /*index=5*/s32[]...) while((s32[]{:T(128)}, f32[10,256,128]{2,1,0:T(8,128)S(1)}, ...), condition=%wide.region_3.4_spmd, body=%wide.region_0.3_spmd.sunk | while | flops 688789504 | bytes 21805756 | solution.py:46
  43.2 2.6 %bitcast_reduce_fusion.3 = (f32[10,256]{1,0:T(8,128)S(1)}, f32[10,512,256]{2,1,0:T(8,128)S(1)}) fusion(pred[512]{0:T(512)(128)(4,1)S(1)} %add_compare_fusion.2, bf16[256,10,128]{2,0,1:T(8,128)(2,1)S(1)} %get-tuple-element.206, bf16[4096,10,128]{0,2,1:T(8,128)(2,1)} %get-tuple-element.205, s32[]{:T(128)S(6)} %select_n.90), kind=kOutput, calls=%fused_computation.1.clone.1 | convolution fusion | flops 339473920 | bytes 7219716 | tf_op jit(solution)/shard_map/while/body/qhd,khd->hqk/dot_general | solution.py:16
  45.8 1.7 fusion.66
  47.5 4.1 %fusion.67 = f32[10,256,128]{2,1,0:T(8,128)S(1)} fusion(f32[10,512,256]{2,1,0:T(8,128)S(1)} %get-tuple-element.169, f32[10,256]{1,0:T(8,128)S(1)} %max.8, pred[512]{0:T(512)(128)(4,1)S(1)} %add_compare_fusion.2, bf16[4096,10,128]{0,2,1:T(8,128)(2,1)} %get-tuple-element.207, s32[]{:T(128)S(6)} %select_n.90, ...), kind=kOutput, calls=%fused_computation.10.clone.1 | convolution fusion | flops 342753280 | bytes 9208836 | tf_op jit(solution)/shard_map/while/body/hqk,khd->hqd/dot_general | solution.py:24
  51.8 1.5 copy.53
  53.3 1.1 copy.54
  55.9 0.9 fusion.36
  56.7 30.1 %all-gather.4.cloned.1.call-done = bf16[1280,5120]{1,0:T(8,128)(2,1)} async-done(((bf16[1280,640]{1,0:T(8,128)(2,1)}), bf16[1280,5120]{1,0:T(8,128)(2,1)}) %all-gather.4.cloned.1.call-update) | async-done | bytes 13107216 | tf_op jit(solution)/shard_map/all_gather | solution.py:107
  86.8 9.7 %convolution_convert_fusion = bf16[256,5120]{1,0:T(8,128)(2,1)} fusion(bf16[256,1280]{0,1:T(8,128)(2,1)S(1)} %bitcast.84, bf16[1280,5120]{1,0:T(8,128)(2,1)} %all-gather.4.cloned.1.call-done), kind=kOutput, calls=%fused_computation.22 | convolution fusion | flops 3356753920 | bytes 16384000 | tf_op jit(solution)/shard_map/dot_general | solution.py:105
  97.9 32.5 %all-gather.6.cloned.1.call-done = bf16[4,512,1280]{2,0,1:T(4,128)(2,1)} async-done(((bf16[4,64,1280]{2,0,1:T(4,128)(2,1)}), bf16[4,512,1280]{2,0,1:T(4,128)(2,1)}) %all-gather.6.cloned.1.call-update) | async-done | bytes 5242896 | tf_op jit(solution)/shard_map/all_gather | solution.py:117
  130.4 5.2 %constant_dynamic-slice_fusion.1 = bf16[1,512,1280]{2,0,1:T(2,128)(2,1)S(1)} fusion(bf16[4,512,1280]{2,0,1:T(4,128)(2,1)} %all-gather.6.cloned.1.call-done, s32[]{:T(128)S(6)} %select_n.42), kind=kLoop, calls=%fused_computation.55 | loop fusion | bytes 2621444 | tf_op jit(solution)/shard_map/jit(dynamic_index_in_dim)/dynamic_slice | solution.py:116
  135.6 3.8 %copy.73 = bf16[1,512,1280]{1,2,0:T(8,128)(2,1)} copy(bf16[1,512,1280]{2,0,1:T(2,128)(2,1)S(1)} %constant_dynamic-slice_fusion.1) | data formatting | bytes 2621440
  139.4 34.1 %all-gather.8.cloned.1.call-done = bf16[4,512,1280]{2,1,0:T(8,128)(2,1)} async-done(((bf16[4,64,1280]{2,1,0:T(8,128)(2,1)}), bf16[4,512,1280]{2,1,0:T(8,128)(2,1)}) %all-gather.8.cloned.1.call-update) | async-done | bytes 5242896 | tf_op jit(solution)/shard_map/all_gather | solution.py:120
  173.5 1.4 constant_dynamic-slice_fusion
  174.9 1.5 copy.61
  176.4 0.9 bitcast_reduce_fusion.1
  177.3 0.9 fusion.20
  178.6 1.2 divide_convert_fusion
  179.8 1.1 copy.63
  180.9 46.9 %reduce-scatter.2.cloned.1.call-done = bf16[256,1280]{1,0:T(8,128)(2,1)} async-done(((bf16[256,5120]{1,0:T(8,128)(2,1)}), bf16[256,1280]{1,0:T(8,128)(2,1)}) %reduce-scatter.2.cloned.1.call-update) | async-done | bytes 655376 | tf_op jit(solution)/shard_map/reduce_scatter | solution.py:110
  227.8 2.1 add_convert_fusion
  (47 shorter events, 6.4 us)
Async XLA Ops:
  7.2 4.0 %copy-start.9 = (s32[8]{0:T(128)S(1)}, s32[8]{0:T(128)}, u32[]{:S(2)}) copy-start(s32[8]{0:T(128)} %param.20) | copy-start | bytes 100
  7.2 5.4 %copy-start.3 = (bf16[256,1280]{1,0:T(8,128)(2,1)S(1)}, bf16[256,1280]{1,0:T(8,128)(2,1)}, u32[]{:S(2)}) copy-start(bf16[256,1280]{1,0:T(8,128)(2,1)} %param.15) | copy-start | bytes 1966084
  7.2 79.6 %all-gather.4.cloned.1.call-start = ((), (), s32[]{:S(2)}) async-start(), calls=%async_computation.1 | async-start | bytes 14745600 | tf_op jit(solution)/shard_map/all_gather | solution.py:107
  7.9 122.5 %all-gather.6.cloned.1.call-start = ((), (), s32[]{:S(2)}) async-start(), calls=%async_computation.3 | async-start | bytes 5898240 | tf_op jit(solution)/shard_map/all_gather | solution.py:117
  10.4 163.1 %all-gather.8.cloned.1.call-start = ((), (), s32[]{:S(2)}) async-start(), calls=%async_computation.4 | async-start | bytes 5898240 | tf_op jit(solution)/shard_map/all_gather | solution.py:120
  11.2 216.6 %reduce-scatter.2.cloned.1.call-start = ((), (), s32[]{:S(2)}) async-start(), calls=%async_computation.2 | async-start | bytes 3276800 | tf_op jit(solution)/shard_map/reduce_scatter | solution.py:110
  27.7 14.3 %copy-start.4 = (bf16[256,1280]{1,0:T(8,128)(2,1)S(1)}, bf16[256,1280]{1,0:T(8,128)(2,1)}, u32[]{:S(2)}) copy-start(bf16[256,1280]{1,0:T(8,128)(2,1)} %param.16) | copy-start | bytes 1966084
  51.8 1.5 copy-start.5
  54.4 1.3 copy-start.1
  54.4 1.5 copy-start.7
  96.5 1.1 copy-start.6
  139.4 37.0 %copy-start = (bf16[1,512,1280]{1,2,0:T(8,128)(2,1)S(1)}, bf16[1,512,1280]{1,2,0:T(8,128)(2,1)}, u32[]{:S(2)}) copy-start(bf16[1,512,1280]{1,2,0:T(8,128)(2,1)} %copy.73) | copy-start | bytes 3932164
  177.3 1.3 copy-start.2
  178.6 49.2 %copy-start.8 = (bf16[256,1280]{1,0:T(8,128)(2,1)S(1)}, bf16[256,1280]{1,0:T(8,128)(2,1)}, u32[]{:S(2)}) copy-start(bf16[256,1280]{1,0:T(8,128)(2,1)} %param.14) | copy-start | bytes 1966084
Sparse Core Ops, SparseCore 0:
  9.9 76.8 all-gather.3
  89.3 41.1 all-gather.5
  132.3 41.1 all-gather.7
  175.6 52.0 reduce-scatter.1
where the time goes:
time: 238 us; the launch traced here: 236 us
  waiting for transfers between devices  145 us (61%)
  local copies, waits for them, and re-layouts  49.6 us (21%)
  matrix products  19.9 us (8%)
  between operations  15.4 us (6%)
  other arithmetic  6.03 us (3%)
    reduce_scatter x1, waiting for transfers between devices, per_device(): lax.psum_scatter(terms.astype(jnp.bfloat16), 'tp', scatter_dimension=1, t...  46.9 us
    unnamed x29, local copies, waits for them, and re-layouts  39 us
    all_gather x1, waiting for transfers between devices, per_device(): lax.all_gather(text_v, 'req', axis=1, tiled=True)  34.1 us
    all_gather x1, waiting for transfers between devices, per_device(): lax.all_gather(text_k, 'req', axis=1, tiled=True)  32.5 us
    all_gather x1, waiting for transfers between devices, per_device(): lax.all_gather(w_out, 'req', axis=1, tiled=True)  30.1 us
    dot_general x1, matrix products, per_device(): jnp.dot(self_heads, lax.all_gather(w_out, 'req', axis=1, tiled=True), pre...  9.66 us
    dot_general x3, matrix products, attend(): jnp.einsum('hqk,khd->hqd', weights.astype(jnp.bfloat16), value_block, pre...  6.12 us
    dynamic_slice x1, local copies, waits for them, and re-layouts, per_device(): lax.dynamic_index_in_dim(lax.all_gather(text_k, 'req', axis=1, tiled=True...  5.18 us
  transfers between devices with their start and end apart: 4, of which 4 were waited for; matrix products, arithmetic and copies ran while one was open for 31% of the time, Pallas kernels for 0%

commit v1 on v0

v1 whole, which is shorter than its diff:
```python
import functools

import jax
import jax.numpy as jnp
from jax import lax
from jax.experimental import pallas as pl
from jax.experimental.pallas import tpu as pltpu
from jax.sharding import PartitionSpec as P

HD = 128
CACHE_BLOCK = 1024
HEAD_GROUPS = 2
NEG_FILL = -1e30
LOG2E = 1.4426950408889634
VMEM_LIMIT = 48 * 2**20


def attend(queries, keys, values, state, visible):
    top_old, mass, total = state
    scale = HD ** (-0.5) * LOG2E
    scores = lax.dot_general(
        queries, keys, (((1,), (1,)), ((), ())), preferred_element_type=jnp.float32
    )
    if visible is not None:
        scores = jnp.where(visible, scores, NEG_FILL)
    top = jnp.maximum(top_old, jnp.max(scores, axis=1, keepdims=True))
    shrink = jnp.exp2((top_old - top) * scale)
    weights = jnp.exp2(scores * scale - top[:, :1] * scale)
    mass = mass * shrink + jnp.sum(weights, axis=1, keepdims=True)
    total = total * shrink + lax.dot_general(
        weights.astype(jnp.bfloat16),
        values,
        (((1,), (0,)), ((), ())),
        preferred_element_type=jnp.float32,
    )
    return top, mass, total


def self_kernel(
    block_rows, heads, first_query, length_ref, q_ref, kn_ref, vn_ref, kc_ref, vc_ref, o_ref,
    top_ref, mass_ref, total_ref,
):
    step, steps = pl.program_id(0), pl.num_programs(0)
    left = length_ref[0] - step * block_rows
    rows, new_rows = q_ref.shape[0], kn_ref.shape[0]

    @pl.when(step == 0)
    def _():
        top_ref[...] = jnp.full_like(top_ref, NEG_FILL)
        mass_ref[...] = jnp.zeros_like(mass_ref)
        total_ref[...] = jnp.zeros_like(total_ref)

    def visit(head, k_ref, v_ref, visible):
        cols = slice(head * HD, (head + 1) * HD)
        state = (top_ref[head], mass_ref[head], total_ref[head])
        state = attend(q_ref[:, cols], k_ref[:, cols], v_ref[:, cols], state, visible)
        top_ref[head], mass_ref[head], total_ref[head] = state
        return state

    @pl.when(jnp.logical_and(step < steps - 1, left >= block_rows))
    def _():
        for head in range(heads):
            visit(head, kc_ref, vc_ref, None)

    @pl.when(jnp.logical_and(step < steps - 1, jnp.logical_and(left > 0, left < block_rows)))
    def _():
        visible = lax.broadcasted_iota(jnp.int32, (rows, block_rows), 1) < left
        for head in range(heads):
            visit(head, kc_ref, vc_ref, visible)

    @pl.when(step == steps - 1)
    def _():
        key_ids = lax.broadcasted_iota(jnp.int32, (rows, new_rows), 1)
        query_ids = lax.broadcasted_iota(jnp.int32, (rows, new_rows), 0) + first_query
        for head in range(heads):
            _, mass, total = visit(head, kn_ref, vn_ref, key_ids <= query_ids)
            o_ref[:, head * HD : (head + 1) * HD] = (total / mass).astype(o_ref.dtype)


def self_attention(queries, new_keys, new_values, keys, values, length, first_row, rows, group, width):
    new_rows = queries.shape[0]
    capacity = keys.shape[0]
    block_rows = min(CACHE_BLOCK, capacity)
    heads = width // HD
    blocks = capacity // block_rows
    new_spec = pl.BlockSpec((first_row + rows, width), lambda i, n: (0, group))
    cache_spec = pl.BlockSpec(
        (block_rows, width), lambda i, n: (jnp.minimum(i, (n[0] - 1) // block_rows), group)
    )
    return pl.pallas_call(
        functools.partial(self_kernel, block_rows, heads, first_row),
        grid_spec=pltpu.PrefetchScalarGridSpec(
            num_scalar_prefetch=1,
            grid=(blocks + 1,),
            in_specs=[
                pl.BlockSpec((rows, width), lambda i, n: (first_row // rows, group)),
                new_spec,
                new_spec,
                cache_spec,
                cache_spec,
            ],
            out_specs=pl.BlockSpec((rows, width), lambda i, n: (0, 0)),
            scratch_shapes=[
                pltpu.VMEM((heads, rows, HD), jnp.float32),
                pltpu.VMEM((heads, rows, HD), jnp.float32),
                pltpu.VMEM((heads, rows, HD), jnp.float32),
            ],
        ),
        out_shape=jax.ShapeDtypeStruct((rows, width), jnp.bfloat16),
        compiler_params=pltpu.CompilerParams(vmem_limit_bytes=VMEM_LIMIT),
        cost_estimate=pl.CostEstimate(
            flops=4 * rows * (capacity + new_rows) * width,
            bytes_accessed=4 * (capacity + new_rows) * width,
            transcendentals=rows * (capacity + new_rows) * heads,
        ),
        name="self_attention",
    )(length.reshape(1), queries, new_keys, new_values, keys, values)


def cross_kernel(heads, q_ref, *refs):
    pieces, o_ref = refs[:-1], refs[-1]
    rows = q_ref.shape[0]
    for head in range(heads):
        cols = slice(head * HD, (head + 1) * HD)
        keys = jnp.concatenate([piece[0, :, cols] for piece in pieces], axis=0)
        values = jnp.concatenate([piece[1, :, cols] for piece in pieces], axis=0)
        state = (
            jnp.full((rows, HD), NEG_FILL, jnp.float32),
            jnp.zeros((rows, HD), jnp.float32),
            jnp.zeros((rows, HD), jnp.float32),
        )
        _, mass, total = attend(q_ref[:, cols], keys, values, state, None)
        o_ref[:, cols] = (total / mass).astype(o_ref.dtype)


def cross_attention(queries, pieces):
    rows, width = queries.shape
    return pl.pallas_call(
        functools.partial(cross_kernel, width // HD),
        out_shape=jax.ShapeDtypeStruct((rows, width), jnp.bfloat16),
        compiler_params=pltpu.CompilerParams(vmem_limit_bytes=VMEM_LIMIT),
        name="cross_attention",
    )(queries, *pieces)


def pick_kernel(count, place_ref, prompt_ref, k_ref, v_ref, *refs):
    outs, sems = refs[:count], refs[count]
    copies = []
    for step in range(count):
        prompt = prompt_ref[place_ref[0] ^ step]
        copies.append(pltpu.make_async_copy(k_ref.at[prompt], outs[step].at[0], sems.at[2 * step]))
        copies.append(
            pltpu.make_async_copy(v_ref.at[prompt], outs[step].at[1], sems.at[2 * step + 1])
        )
    for copy in copies:
        copy.start()
    for copy in copies:
        copy.wait()


def pick_text(place, prompts, text_k, text_v):
    count = prompts.shape[0]
    _, rows, width = text_k.shape
    scalars = pl.BlockSpec(memory_space=pltpu.SMEM)
    hbm = pl.BlockSpec(memory_space=pl.ANY)
    return pl.pallas_call(
        functools.partial(pick_kernel, count),
        in_specs=[scalars, scalars, hbm, hbm],
        out_specs=[hbm] * count,
        out_shape=[jax.ShapeDtypeStruct((2, rows, width), text_k.dtype)] * count,
        scratch_shapes=[pltpu.SemaphoreType.DMA((2 * count,))],
        name="pick_text",
    )(place.reshape(1), prompts, text_k, text_v)


def project_kernel(count, place_ref, own_ref, near_ref, *refs):
    held, passed = refs[:count], refs[count : 2 * count]
    o_ref, weights, sems = refs[2 * count :]
    chip, holder = place_ref[0], place_ref[1]
    rows = own_ref.shape[0]

    def each(choice, act):
        for step in range(count):
            act(pltpu.make_async_copy(choice[step], weights.at[step], sems.at[step]))

    @pl.when(holder == 1)
    def _():
        each(held, lambda copy: copy.start())

    @pl.when(holder == 0)
    def _():
        each(passed, lambda copy: copy.start())

    for step in range(count):
        pltpu.make_async_copy(held[step], weights.at[step], sems.at[step]).wait()
        at = chip ^ step
        for part, x_ref in enumerate((own_ref, near_ref)):
            o_ref[at, part * rows : (part + 1) * rows, :] = jnp.dot(
                x_ref[...], weights[step], preferred_element_type=jnp.float32
            ).astype(o_ref.dtype)


def project(chip, holder, own, near, held, passed):
    count = len(held)
    rows, depth = own.shape
    columns = held[0].shape[1]
    hbm = pl.BlockSpec(memory_space=pl.ANY)
    vmem = pl.BlockSpec(memory_space=pltpu.VMEM)
    return pl.pallas_call(
        functools.partial(project_kernel, count),
        in_specs=[pl.BlockSpec(memory_space=pltpu.SMEM), vmem, vmem] + [hbm] * (2 * count),
        out_specs=vmem,
        out_shape=jax.ShapeDtypeStruct((count, 2 * rows, columns), jnp.bfloat16),
        scratch_shapes=[
            pltpu.VMEM((count, depth, columns), jnp.bfloat16),
            pltpu.SemaphoreType.DMA((count,)),
        ],
        compiler_params=pltpu.CompilerParams(vmem_limit_bytes=VMEM_LIMIT),
        name="project",
    )(jnp.stack([chip, holder]).astype(jnp.int32), own, near, *held, *passed)


def per_device(
    reqs,
    tps,
    hidden,
    q_new,
    k_new,
    v_new,
    cache_k,
    cache_v,
    cache_len,
    w_out,
    q_cross,
    text_k,
    text_v,
    prompt_of,
):
    rows, width = q_new.shape
    chips = reqs // 2
    place = lax.axis_index("req")
    chip, core = place // 2, place % 2
    side = chip % 2
    holder = core == side
    length = lax.dynamic_index_in_dim(cache_len, place, 0, keepdims=False)

    def swap(array, distance):
        return lax.ppermute(array, "req", [(i, i ^ distance) for i in range(reqs)])

    held = [w_out]
    held.append(
        lax.ppermute(
            w_out,
            "req",
            [(2 * i + 1 - i % 2, 2 * (i ^ 1) + 1 - i % 2) for i in range(chips)],
        )
    )
    bit = 2
    while bit < chips:
        pairs = [(2 * i + i % 2, 2 * (i ^ bit) + i % 2) for i in range(chips)]
        held += [lax.ppermute(block, "req", pairs) for block in held]
        bit *= 2
    across = [(2 * i + i % 2, 2 * i + 1 - i % 2) for i in range(chips)]
    passed = [lax.ppermute(block, "req", across) for block in held]

    prompts = lax.all_gather(prompt_of, "req", axis=0, tiled=True)
    pieces = pick_text(place, prompts, text_k, text_v)
    pieces = [pieces[0]] + [swap(pieces[i], i) for i in range(1, reqs)]

    groups = HEAD_GROUPS if (width // HD) % HEAD_GROUPS == 0 else 1
    group_width = width // groups
    parts = [
        self_attention(
            q_new, k_new, v_new, cache_k[0], cache_v[0], length, 0, rows, group, group_width
        )
        for group in range(groups)
    ]
    own = jnp.concatenate(parts, axis=1)
    near = swap(own, 2)
    terms = project(chip, holder, own, near, held, passed)
    summed = lax.psum_scatter(terms, "tp", scatter_dimension=0, tiled=True)
    kept, given = summed[:, :rows], summed[:, rows:]
    received = swap(given, 2)
    ordered = jnp.where(
        side == 0, jnp.stack([kept, received], axis=1), jnp.stack([received, kept], axis=1)
    )
    ordered = ordered.transpose(2, 0, 1, 3).reshape(rows, -1)
    hidden_out = (hidden.astype(jnp.float32) + ordered.astype(jnp.float32)).astype(jnp.bfloat16)
    cross_heads = cross_attention(q_cross, pieces)
    return (hidden_out, cross_heads)


def solution(mesh):
    placed = (
        P("req", "tp"),
        P("req", "tp"),
        P("req", "tp"),
        P("req", "tp"),
        P("req", None, "tp"),
        P("req", None, "tp"),
        P(),
        P("tp", "req"),
        P("req", "tp"),
        P(None, "req", "tp"),
        P(None, "req", "tp"),
        P("req"),
    )
    return jax.shard_map(
        functools.partial(per_device, mesh.shape["req"], mesh.shape["tp"]),
        mesh=mesh,
        in_specs=placed,
        out_specs=(P("req", "tp"), P("req", "tp")),
        check_vma=False,
    )
```

time: 238 us -> 242 us (1.017)
  Pallas kernels: 0 us -> 109 us
  waiting for transfers between devices: 145 us -> 65.5 us
  local copies, waits for them, and re-layouts: 49.6 us -> 12.2 us
  starting transfers between devices: 0.16 us -> 27.7 us
  matrix products: 19.9 us -> 0 us
  blocking collectives: 0 us -> 9.68 us
  other arithmetic: 6.03 us -> 1.46 us
    pallas_call x0 -> x5, Pallas kernels: none -> 109 us  [the longest x1 81.3 us: pick_text(): pl.pallas_call(functools.partial(pick_kernel, count), in_specs=[scalars,...]
    all_gather x3 -> x0, waiting for transfers between devices: 96.7 us -> none  [the longest x1 34.1 us: per_device(): lax.all_gather(text_v, 'req', axis=1, tiled=True)]
    ppermute x0 -> x16, waiting for transfers between devices: none -> 65.5 us  [the longest x9 36.2 us: swap(): return lax.ppermute(array, 'req', [(i, i ^ distance) for i in range(reqs)])]
    reduce_scatter x1, waiting for transfers between devices: 46.9 us -> 0.01 us  [per_device(): summed = lax.psum_scatter(terms, 'tp', scatter_dimension=0, tiled=True)]
    unnamed x29 -> x23, local copies, waits for them, and re-layouts: 39 us -> 8.55 us
    ppermute x0 -> x16, starting transfers between devices: none -> 27.7 us  [the longest x4 10 us: per_device(): passed = [lax.ppermute(block, 'req', across) for block in held]]
    dot_general x7 -> x0, matrix products: 19.9 us -> none  [the longest x1 9.66 us: per_device(): jnp.dot(self_heads, lax.all_gather(w_out, 'req', axis=1, tiled=True), pre...]
    unnamed x0 -> x1, blocking collectives: none -> 9.68 us
  transfers between devices with their start and end apart: 4 -> 17, of which waited for: 4 -> 6; matrix products, arithmetic and copies ran while one was open for 31% -> 3% of each run, Pallas kernels for 0% -> 42%
where the time goes in v1:
time: 242 us; the launch traced here: 241 us
  Pallas kernels  109 us (45%)
  waiting for transfers between devices  65.5 us (27%)
  starting transfers between devices  27.7 us (11%)
  between operations  14.9 us (6%)
  local copies, waits for them, and re-layouts  12.2 us (5%)
  blocking collectives  9.68 us (4%)
    pallas_call x1, Pallas kernels, pick_text(): pl.pallas_call(functools.partial(pick_kernel, count), in_specs=[scalars,...  81.3 us
    ppermute x9, waiting for transfers between devices, swap(): return lax.ppermute(array, 'req', [(i, i ^ distance) for i in range(reqs)])  36.2 us
    ppermute x1, waiting for transfers between devices, per_device(): lax.ppermute(w_out, 'req', [(2 * i + 1 - i % 2, 2 * (i ^ 1) + 1 - i % 2)...  17.4 us
    pallas_call x2, Pallas kernels, self_attention(): pl.pallas_call(functools.partial(self_kernel, block_rows, heads, first_ro...  16.4 us
    ppermute x2, waiting for transfers between devices, per_device(): held += [lax.ppermute(block, 'req', pairs) for block in held]  11.9 us
    ppermute x4, starting transfers between devices, per_device(): passed = [lax.ppermute(block, 'req', across) for block in held]  10 us
    unnamed x1, blocking collectives  9.68 us
    ppermute x2, starting transfers between devices, per_device(): held += [lax.ppermute(block, 'req', pairs) for block in held]  9.44 us
  transfers between devices with their start and end apart: 17, of which 6 were waited for; matrix products, arithmetic and copies ran while one was open for 3% of the time, Pallas kernels for 42%

profile of v1, /device:TPU:0, one launch (start us, length us, event | category | flops | bytes accessed | tf_op | source)
XLA Modules:
  0.0 240.6 jit_solution(16556728473561683970)
XLA Ops:
  7.2 1.3 collective-permute-start.1
  8.5 4.9 %collective-permute-start.2 = (bf16[1280,640]{1,0:T(8,128)(2,1)}, bf16[1280,640]{1,0:T(8,128)(2,1)}, u32[]{:S(2)}, u32[]{:S(2)}) collective-permute-start(bf16[1280,640]{1,0:T(8,128)(2,1)} %refs_0_.1), channel_id=1, source_target_pairs={{0,16},{12,28},{16,0},{28,12},{1,17},{13,29},{17,1},{29,13},{2,18}... | collective-permute-start | bytes 4915208 | tf_op jit(solution)/shard_map/ppermute | solution.py:261
  13.4 17.4 %collective-permute-done.1.refs_1_ = bf16[1280,640]{1,0:T(8,128)(2,1)} collective-permute-done((bf16[1280,640]{1,0:T(8,128)(2,1)}, bf16[1280,640]{1,0:T(8,128)(2,1)}, u32[]{:S(2)}, u32[]{:S(2)}) %collective-permute-start.1) | collective-permute-done | bytes 1638432 | tf_op jit(solution)/shard_map/ppermute | solution.py:252
  30.8 4.6 %collective-permute-start.3 = (bf16[1280,640]{1,0:T(8,128)(2,1)}, bf16[1280,640]{1,0:T(8,128)(2,1)}, u32[]{:S(2)}, u32[]{:S(2)}) collective-permute-start(bf16[1280,640]{1,0:T(8,128)(2,1)} %collective-permute-done.1.refs_1_), channel_id=1, source_target_pairs={{0,16},{12,28},{16,0},{28,12},{1,17},{13,29},{17,1},{29,13},{2,18}... | collective-permute-start | bytes 4915208 | tf_op jit(solution)/shard_map/ppermute | solution.py:261
  35.4 2.6 %collective-permute-start.4 = (bf16[1280,640]{1,0:T(8,128)(2,1)}, bf16[1280,640]{1,0:T(8,128)(2,1)}, u32[]{:S(2)}, u32[]{:S(2)}) collective-permute-start(bf16[1280,640]{1,0:T(8,128)(2,1)} %refs_0_.1), channel_id=1, source_target_pairs={{0,4},{12,8},{16,20},{28,24},{1,5},{13,9},{17,21},{29,25},{2,6},{1... | collective-permute-start | bytes 4915208 | tf_op jit(solution)/shard_map/ppermute | solution.py:264
  38.0 2.5 %collective-permute-start.5 = (bf16[1280,640]{1,0:T(8,128)(2,1)}, bf16[1280,640]{1,0:T(8,128)(2,1)}, u32[]{:S(2)}, u32[]{:S(2)}) collective-permute-start(bf16[1280,640]{1,0:T(8,128)(2,1)} %collective-permute-done.1.refs_1_), channel_id=1, source_target_pairs={{0,4},{12,8},{16,20},{28,24},{1,5},{13,9},{17,21},{29,25},{2,6},{1... | collective-permute-start | bytes 4915208 | tf_op jit(solution)/shard_map/ppermute | solution.py:264
  40.4 2.5 %collective-permute-start.6 = (bf16[1280,640]{1,0:T(8,128)(2,1)}, bf16[1280,640]{1,0:T(8,128)(2,1)}, u32[]{:S(2)}, u32[]{:S(2)}) collective-permute-start(bf16[1280,640]{1,0:T(8,128)(2,1)} %collective-permute-done.2.refs_2_), channel_id=1, source_target_pairs={{0,4},{12,8},{16,20},{28,24},{1,5},{13,9},{17,21},{29,25},{2,6},{1... | collective-permute-start | bytes 4915208 | tf_op jit(solution)/shard_map/ppermute | solution.py:264
  42.9 11.9 %collective-permute-done.3.refs_3_ = bf16[1280,640]{1,0:T(8,128)(2,1)} collective-permute-done((bf16[1280,640]{1,0:T(8,128)(2,1)}, bf16[1280,640]{1,0:T(8,128)(2,1)}, u32[]{:S(2)}, u32[]{:S(2)}) %collective-permute-start.3) | collective-permute-done | bytes 1638432 | tf_op jit(solution)/shard_map/ppermute | solution.py:261
  54.8 2.5 %collective-permute-start.7 = (bf16[1280,640]{1,0:T(8,128)(2,1)}, bf16[1280,640]{1,0:T(8,128)(2,1)}, u32[]{:S(2)}, u32[]{:S(2)}) collective-permute-start(bf16[1280,640]{1,0:T(8,128)(2,1)} %collective-permute-done.3.refs_3_), channel_id=1, source_target_pairs={{0,4},{12,8},{16,20},{28,24},{1,5},{13,9},{17,21},{29,25},{2,6},{1... | collective-permute-start | bytes 4915208 | tf_op jit(solution)/shard_map/ppermute | solution.py:264
  57.3 1.2 dynamic_slice.4.length_ref
  61.8 8.0 %self_attention.2 = bf16[256,640]{1,0:T(8,128)(2,1)S(1)} custom-call(s32[1]{0:T(128)} %dynamic_slice.4.length_ref, bf16[256,1280]{1,0:T(8,128)(2,1)S(1)} %copy-done, bf16[256,1280]{1,0:T(8,128)(2,1)S(1)} %copy-done.1, bf16[256,1280]{1,0:T(8,128)(2,1)S(1)} %copy-done.2, bf16[4096,1280]{1,0:T(8,128)(2,1)} %bitcast.15, bf16[4096,1280]{1,0:T(8,128)(2,1)} %bitcast.17), custom_call_target="tpu_custom_call" | custom-call | flops 2852126720 | bytes 11141120 | tf_op jit(solution)/shard_map/self_attention/pallas_call | solution.py:90
  69.8 8.3 %self_attention.3 = bf16[256,640]{1,0:T(8,128)(2,1)S(1)} custom-call(s32[1]{0:T(128)} %dynamic_slice.4.length_ref, bf16[256,1280]{1,0:T(8,128)(2,1)S(1)} %copy-done, bf16[256,1280]{1,0:T(8,128)(2,1)S(1)} %copy-done.1, bf16[256,1280]{1,0:T(8,128)(2,1)S(1)} %copy-done.2, bf16[4096,1280]{1,0:T(8,128)(2,1)} %bitcast.16, bf16[4096,1280]{1,0:T(8,128)(2,1)} %bitcast.18), custom_call_target="tpu_custom_call" | custom-call | flops 2852126720 | bytes 11141120 | tf_op jit(solution)/shard_map/self_attention/pallas_call | solution.py:90
  78.4 14.4 %collective-permute-done.near_ref = bf16[256,1280]{1,0:T(8,128)(2,1)S(1)} collective-permute-done((bf16[256,1280]{1,0:T(8,128)(2,1)S(1)}, bf16[256,1280]{1,0:T(8,128)(2,1)S(1)}, u32[]{:S(2)}, u32[]{:S(2)}) %collective-permute-start) | collective-permute-done | bytes 655392 | tf_op jit(solution)/shard_map/ppermute | solution.py:248
  92.8 7.3 %project.1 = bf16[4,512,640]{2,1,0:T(8,128)(2,1)} custom-call(s32[2]{0:T(128)S(1)} %pad_add_fusion.place_ref, bf16[256,1280]{1,0:T(8,128)(2,1)S(1)} %pad_maximum_fusion.own_ref, bf16[256,1280]{1,0:T(8,128)(2,1)S(1)} %collective-permute-done.near_ref, bf16[1280,640]{1,0:T(8,128)(2,1)S(1)} %copy-done.3, bf16[1280,640]{1,0:T(8,128)(2,1)} %collective-permute-done.1.refs_1_, ...), custom_call_target="tpu_custom_call" | custom-call | tf_op jit(solution)/shard_map/project/pallas_call | solution.py:209
  102.2 9.7 %all-reduce.prompt_ref = s32[8]{0:T(128)} all-reduce(s32[8]{0:T(128)S(1)} %dynamic-update-slice), channel_id=1, replica_groups=mesh['req'=8,'tp'=4] {'req'}, use_global_device_ids=true, to_apply=%add | all-reduce | flops 8 | bytes 64
  111.9 81.3 %pick_text.1 = (bf16[2,64,1280]{2,1,0:T(8,128)(2,1)}, bf16[2,64,1280]{2,1,0:T(8,128)(2,1)}, bf16[2,64,1280]{2,1,0:T(8,128)(2,1)}, bf16[2,64,1280]{2,1,0:T(8,128)...) custom-call(s32[1]{0:T(128)} %bitcast.8.place_ref, ...), custom_call_target="tpu_custom_call" | custom-call | tf_op jit(solution)/shard_map/pick_text/pallas_call | solution.py:166
  194.6 2.1 collective-permute-start.13
  197.6 6.6 %collective-permute-done.10.refs_2_ = bf16[2,64,1280]{2,1,0:T(8,128)(2,1)S(1)} collective-permute-done((bf16[2,64,1280]{2,1,0:T(8,128)(2,1)}, bf16[2,64,1280]{2,1,0:T(8,128)(2,1)S(1)}, u32[]{:S(2)}, u32[]{:S(2)}) %collective-permute-start.10) | collective-permute-done | bytes 327712 | tf_op jit(solution)/shard_map/ppermute | solution.py:248
  204.1 5.4 %collective-permute-done.11.refs_3_ = bf16[2,64,1280]{2,1,0:T(8,128)(2,1)S(1)} collective-permute-done((bf16[2,64,1280]{2,1,0:T(8,128)(2,1)}, bf16[2,64,1280]{2,1,0:T(8,128)(2,1)S(1)}, u32[]{:S(2)}, u32[]{:S(2)}) %collective-permute-start.11) | collective-permute-done | bytes 327712 | tf_op jit(solution)/shard_map/ppermute | solution.py:248
  209.5 1.8 collective-permute-start.9
  211.3 2.0 slice_bitcast_fusion
  214.0 2.2 copy.14
  216.1 9.9 %collective-permute-done.13.refs_5_ = bf16[2,64,1280]{2,1,0:T(8,128)(2,1)S(1)} collective-permute-done((bf16[2,64,1280]{2,1,0:T(8,128)(2,1)}, bf16[2,64,1280]{2,1,0:T(8,128)(2,1)S(1)}, u32[]{:S(2)}, u32[]{:S(2)}) %collective-permute-start.13) | collective-permute-done | bytes 327712 | tf_op jit(solution)/shard_map/ppermute | solution.py:248
  226.0 4.2 %cross_attention.1 = bf16[256,1280]{1,0:T(8,128)(2,1)} custom-call(bf16[256,1280]{1,0:T(8,128)(2,1)S(1)} %copy-done.4, bf16[2,64,1280]{2,1,0:T(8,128)(2,1)S(1)} %copy-done.5, bf16[2,64,1280]{2,1,0:T(8,128)(2,1)S(1)} %collective-permute-done.9.refs_1_, bf16[2,64,1280]{2,1,0:T(8,128)(2,1)S(1)} %collective-permute-done.10.refs_2_, ...), custom_call_target="tpu_custom_call" | custom-call | tf_op jit(solution)/shard_map/cross_attention/pallas_call | solution.py:138
  (47 shorter events, 11.4 us)
Async XLA Ops:
  7.2 204.1 %reduce-scatter.2.cloned.1.call-start = ((), (), s32[]{:S(2)}) async-start(), calls=%async_computation.1 | async-start | bytes 3276800 | tf_op jit(solution)/shard_map/reduce_scatter | solution.py:281
  7.2 23.6 %collective-permute-start.1 = (bf16[1280,640]{1,0:T(8,128)(2,1)}, bf16[1280,640]{1,0:T(8,128)(2,1)}, u32[]{:S(2)}, u32[]{:S(2)}) collective-permute-start(bf16[1280,640]{1,0:T(8,128)(2,1)} %refs_0_.1), channel_id=1, source_target_pairs={{4,12},{8,0},{20,28},{24,16},{5,13},{9,1},{21,29},{25,17},{6,14},{... | collective-permute-start | bytes 4915208 | tf_op jit(solution)/shard_map/ppermute | solution.py:252
  8.5 31.9 %collective-permute-start.2 = (bf16[1280,640]{1,0:T(8,128)(2,1)}, bf16[1280,640]{1,0:T(8,128)(2,1)}, u32[]{:S(2)}, u32[]{:S(2)}) collective-permute-start(bf16[1280,640]{1,0:T(8,128)(2,1)} %refs_0_.1), channel_id=1, source_target_pairs={{0,16},{12,28},{16,0},{28,12},{1,17},{13,29},{17,1},{29,13},{2,18}... | collective-permute-start | bytes 4915208 | tf_op jit(solution)/shard_map/ppermute | solution.py:261
  30.8 24.0 %collective-permute-start.3 = (bf16[1280,640]{1,0:T(8,128)(2,1)}, bf16[1280,640]{1,0:T(8,128)(2,1)}, u32[]{:S(2)}, u32[]{:S(2)}) collective-permute-start(bf16[1280,640]{1,0:T(8,128)(2,1)} %collective-permute-done.1.refs_1_), channel_id=1, source_target_pairs={{0,16},{12,28},{16,0},{28,12},{1,17},{13,29},{17,1},{29,13},{2,18}... | collective-permute-start | bytes 4915208 | tf_op jit(solution)/shard_map/ppermute | solution.py:261
  35.4 57.4 %collective-permute-start.4 = (bf16[1280,640]{1,0:T(8,128)(2,1)}, bf16[1280,640]{1,0:T(8,128)(2,1)}, u32[]{:S(2)}, u32[]{:S(2)}) collective-permute-start(bf16[1280,640]{1,0:T(8,128)(2,1)} %refs_0_.1), channel_id=1, source_target_pairs={{0,4},{12,8},{16,20},{28,24},{1,5},{13,9},{17,21},{29,25},{2,6},{1... | collective-permute-start | bytes 4915208 | tf_op jit(solution)/shard_map/ppermute | solution.py:264
  38.0 54.8 %collective-permute-start.5 = (bf16[1280,640]{1,0:T(8,128)(2,1)}, bf16[1280,640]{1,0:T(8,128)(2,1)}, u32[]{:S(2)}, u32[]{:S(2)}) collective-permute-start(bf16[1280,640]{1,0:T(8,128)(2,1)} %collective-permute-done.1.refs_1_), channel_id=1, source_target_pairs={{0,4},{12,8},{16,20},{28,24},{1,5},{13,9},{17,21},{29,25},{2,6},{1... | collective-permute-start | bytes 4915208 | tf_op jit(solution)/shard_map/ppermute | solution.py:264
  40.4 52.4 %collective-permute-start.6 = (bf16[1280,640]{1,0:T(8,128)(2,1)}, bf16[1280,640]{1,0:T(8,128)(2,1)}, u32[]{:S(2)}, u32[]{:S(2)}) collective-permute-start(bf16[1280,640]{1,0:T(8,128)(2,1)} %collective-permute-done.2.refs_2_), channel_id=1, source_target_pairs={{0,4},{12,8},{16,20},{28,24},{1,5},{13,9},{17,21},{29,25},{2,6},{1... | collective-permute-start | bytes 4915208 | tf_op jit(solution)/shard_map/ppermute | solution.py:264
  54.8 38.0 %collective-permute-start.7 = (bf16[1280,640]{1,0:T(8,128)(2,1)}, bf16[1280,640]{1,0:T(8,128)(2,1)}, u32[]{:S(2)}, u32[]{:S(2)}) collective-permute-start(bf16[1280,640]{1,0:T(8,128)(2,1)} %collective-permute-done.3.refs_3_), channel_id=1, source_target_pairs={{0,4},{12,8},{16,20},{28,24},{1,5},{13,9},{17,21},{29,25},{2,6},{1... | collective-permute-start | bytes 4915208 | tf_op jit(solution)/shard_map/ppermute | solution.py:264
  58.5 1.1 copy-start
  59.6 1.1 copy-start.1
  69.8 23.0 %copy-start.3 = (bf16[1280,640]{1,0:T(8,128)(2,1)S(1)}, bf16[1280,640]{1,0:T(8,128)(2,1)}, u32[]{:S(2)}) copy-start(bf16[1280,640]{1,0:T(8,128)(2,1)} %refs_0_.1) | copy-start | bytes 4915204
  78.2 14.6 %collective-permute-start = (bf16[256,1280]{1,0:T(8,128)(2,1)S(1)}, bf16[256,1280]{1,0:T(8,128)(2,1)S(1)}, u32[]{:S(2)}, u32[]{:S(2)}) collective-permute-start(bf16[256,1280]{1,0:T(8,128)(2,1)S(1)} %pad_maximum_fusion.own_ref), channel_id=1, source_target_pairs={{0,8},{4,12},{8,0},{12,4},{16,24},{20,28},{24,16},{28,20},{1,9},{5... | collective-permute-start | bytes 1966088 | tf_op jit(solution)/shard_map/ppermute | solution.py:248
  193.2 32.8 %copy-start.4 = (bf16[256,1280]{1,0:T(8,128)(2,1)S(1)}, bf16[256,1280]{1,0:T(8,128)(2,1)}, u32[]{:S(2)}) copy-start(bf16[256,1280]{1,0:T(8,128)(2,1)} %q_ref.5) | copy-start | bytes 1966084
  193.2 32.8 %copy-start.5 = (bf16[2,64,1280]{2,1,0:T(8,128)(2,1)S(1)}, bf16[2,64,1280]{2,1,0:T(8,128)(2,1)}, u32[]{:S(2)}) copy-start(bf16[2,64,1280]{2,1,0:T(8,128)(2,1)} %get-tuple-element.10.refs_0_) | copy-start | bytes 983044
  193.2 10.9 %collective-permute-start.10 = (bf16[2,64,1280]{2,1,0:T(8,128)(2,1)}, bf16[2,64,1280]{2,1,0:T(8,128)(2,1)S(1)}, u32[]{:S(2)}, u32[]{:S(2)}) collective-permute-start(bf16[2,64,1280]{2,1,0:T(8,128)(2,1)} %get-tuple-element.12), channel_id=1, source_target_pairs={{0,8},{4,12},{8,0},{12,4},{16,24},{20,28},{24,16},{28,20},{1,9},{5... | collective-permute-start | bytes 983048 | tf_op jit(solution)/shard_map/ppermute | solution.py:248
  194.1 15.4 %collective-permute-start.11 = (bf16[2,64,1280]{2,1,0:T(8,128)(2,1)}, bf16[2,64,1280]{2,1,0:T(8,128)(2,1)S(1)}, u32[]{:S(2)}, u32[]{:S(2)}) collective-permute-start(bf16[2,64,1280]{2,1,0:T(8,128)(2,1)} %get-tuple-element.13), channel_id=1, source_target_pairs={{0,12},{4,8},{8,4},{12,0},{16,28},{20,24},{24,20},{28,16},{1,13},{... | collective-permute-start | bytes 983048 | tf_op jit(solution)/shard_map/ppermute | solution.py:248
  194.1 19.1 %collective-permute-start.12 = (bf16[2,64,1280]{2,1,0:T(8,128)(2,1)}, bf16[2,64,1280]{2,1,0:T(8,128)(2,1)S(1)}, u32[]{:S(2)}, u32[]{:S(2)}) collective-permute-start(bf16[2,64,1280]{2,1,0:T(8,128)(2,1)} %get-tuple-element.14), channel_id=1, source_target_pairs={{0,16},{4,20},{8,24},{12,28},{16,0},{20,4},{24,8},{28,12},{1,17},{... | collective-permute-start | bytes 983048 | tf_op jit(solution)/shard_map/ppermute | solution.py:248
  194.6 31.4 %collective-permute-start.13 = (bf16[2,64,1280]{2,1,0:T(8,128)(2,1)}, bf16[2,64,1280]{2,1,0:T(8,128)(2,1)S(1)}, u32[]{:S(2)}, u32[]{:S(2)}) collective-permute-start(bf16[2,64,1280]{2,1,0:T(8,128)(2,1)} %get-tuple-element.15), channel_id=1, source_target_pairs={{0,20},{4,16},{8,28},{12,24},{16,4},{20,0},{24,12},{28,8},{1,21},{... | collective-permute-start | bytes 983048 | tf_op jit(solution)/shard_map/ppermute | solution.py:248
  196.8 29.2 %collective-permute-start.14 = (bf16[2,64,1280]{2,1,0:T(8,128)(2,1)}, bf16[2,64,1280]{2,1,0:T(8,128)(2,1)S(1)}, u32[]{:S(2)}, u32[]{:S(2)}) collective-permute-start(bf16[2,64,1280]{2,1,0:T(8,128)(2,1)} %get-tuple-element.16), channel_id=1, source_target_pairs={{0,24},{4,28},{8,16},{12,20},{16,8},{20,12},{24,0},{28,4},{1,25},{... | collective-permute-start | bytes 983048 | tf_op jit(solution)/shard_map/ppermute | solution.py:248
  204.1 21.9 %collective-permute-start.15 = (bf16[2,64,1280]{2,1,0:T(8,128)(2,1)}, bf16[2,64,1280]{2,1,0:T(8,128)(2,1)S(1)}, u32[]{:S(2)}, u32[]{:S(2)}) collective-permute-start(bf16[2,64,1280]{2,1,0:T(8,128)(2,1)} %get-tuple-element.17), channel_id=1, source_target_pairs={{0,28},{4,24},{8,20},{12,16},{16,12},{20,8},{24,4},{28,0},{1,29},{... | collective-permute-start | bytes 983048 | tf_op jit(solution)/shard_map/ppermute | solution.py:248
  209.5 16.5 %collective-permute-start.9 = (bf16[2,64,1280]{2,1,0:T(8,128)(2,1)}, bf16[2,64,1280]{2,1,0:T(8,128)(2,1)S(1)}, u32[]{:S(2)}, u32[]{:S(2)}) collective-permute-start(bf16[2,64,1280]{2,1,0:T(8,128)(2,1)} %get-tuple-element.11), channel_id=1, source_target_pairs={{0,4},{4,0},{8,12},{12,8},{16,20},{20,16},{24,28},{28,24},{1,5},{5... | collective-permute-start | bytes 983048 | tf_op jit(solution)/shard_map/ppermute | solution.py:248
  213.3 17.0 %collective-permute-start.8 = (bf16[1,256,640]{2,1,0:T(8,128)(2,1)}, bf16[1,256,640]{2,1,0:T(8,128)(2,1)}, u32[]{:S(2)}, u32[]{:S(2)}) collective-permute-start(bf16[1,256,640]{2,1,0:T(8,128)(2,1)} %get-tuple-element.21), channel_id=1, source_target_pairs={{0,8},{4,12},{8,0},{12,4},{16,24},{20,28},{24,16},{28,20},{1,9},{5... | collective-permute-start | bytes 983048 | tf_op jit(solution)/shard_map/ppermute | solution.py:248
  226.0 4.2 %copy-start.7 = (bf16[1,1,256,640]{3,2,1,0:T(8,128)(2,1)S(1)}, bf16[1,1,256,640]{3,2,1,0:T(8,128)(2,1)}, u32[]{:S(2)}) copy-start(bf16[1,1,256,640]{3,2,1,0:T(8,128)(2,1)} %get-tuple-element.20) | copy-start | bytes 983044
  231.4 1.1 copy-start.6
  (2 other events, 1.8 us)
Sparse Core Ops, SparseCore 0:
  100.3 54.5 reduce-scatter.1

commit v2 on v1

--- a/solution.py
+++ b/solution.py
@@ -10,6 +10,7 @@
 HD = 128
 CACHE_BLOCK = 1024
 HEAD_GROUPS = 2
+TAG_ROWS = 16
 NEG_FILL = -1e30
 LOG2E = 1.4426950408889634
 VMEM_LIMIT = 48 * 2**20
@@ -117,67 +118,111 @@
     )(length.reshape(1), queries, new_keys, new_values, keys, values)
 
 
-def cross_kernel(heads, q_ref, *refs):
-    pieces, o_ref = refs[:-1], refs[-1]
+def cross_kernel(heads, pieces_count, prompts_ref, side_ref, q_ref, near_ref, *refs):
+    pieces, (own_ref, other_ref) = refs[:pieces_count], refs[pieces_count:]
+    rows = q_ref.shape[0]
+    span = pieces[0].shape[2]
+    width = heads * HD
+    first = pl.multiple_of(side_ref[0] * width, HD)
+    for part in range(2):
+        prompt = prompts_ref[part]
+        for head in range(heads):
+            cols = slice(head * HD, (head + 1) * HD)
+            if part == 0:
+                queries = q_ref[:, pl.ds(pl.multiple_of(first + head * HD, HD), HD)]
+            else:
+                queries = near_ref[:rows, cols]
+            keys = jnp.concatenate([piece[0, prompt, :, cols] for piece in pieces], axis=0)
+            values = jnp.concatenate([piece[1, prompt, :, cols] for piece in pieces], axis=0)
+            state = (
+                jnp.full((rows, HD), NEG_FILL, jnp.float32),
+                jnp.zeros((rows, HD), jnp.float32),
+                jnp.zeros((rows, HD), jnp.float32),
+            )
+            _, mass, total = attend(queries, keys, values, state, None)
+            target = other_ref if part else own_ref
+            target[:, cols] = (total / mass).astype(target.dtype)
+
+
+def cross_attention(prompts, side, queries, near, pieces):
+    rows, width = queries.shape
+    half = width // 2
+    scalars = pl.BlockSpec(memory_space=pltpu.SMEM)
+    vmem = pl.BlockSpec(memory_space=pltpu.VMEM)
+    return pl.pallas_call(
+        functools.partial(cross_kernel, half // HD, len(pieces)),
+        in_specs=[scalars, scalars] + [vmem] * (2 + len(pieces)),
+        out_specs=[vmem, vmem],
+        out_shape=[jax.ShapeDtypeStruct((rows, half), jnp.bfloat16)] * 2,
+        compiler_params=pltpu.CompilerParams(vmem_limit_bytes=VMEM_LIMIT),
+        name="cross_attention",
+    )(prompts, side.reshape(1), queries, near, *pieces)
+
+
+def pack_kernel(side_ref, prompt_ref, k_ref, v_ref, q_ref, keep_ref, give_ref, ask_ref):
+    half = keep_ref.shape[3]
+    kept = pl.ds(pl.multiple_of(side_ref[0] * half, HD), half)
+    given = pl.ds(pl.multiple_of((1 - side_ref[0]) * half, HD), half)
+    for part, source in enumerate((k_ref, v_ref)):
+        keep_ref[part] = source[:, :, kept]
+        give_ref[part] = source[:, :, given]
+    rows = q_ref.shape[0]
+    ask_ref[:rows, :] = q_ref[:, given]
+    tag = jnp.full((TAG_ROWS, half), prompt_ref[0], jnp.int32)
+    ask_ref[rows:, :] = tag.astype(jnp.float32).astype(ask_ref.dtype)
+
+
+def pack(side, prompt_of, text_k, text_v, queries):
+    prompts, text_rows, width = text_k.shape
+    rows, half = queries.shape[0], width // 2
+    text = jax.ShapeDtypeStruct((2, prompts, text_rows, half), text_k.dtype)
+    scalars = pl.BlockSpec(memory_space=pltpu.SMEM)
+    vmem = pl.BlockSpec(memory_space=pltpu.VMEM)
+    return pl.pallas_call(
+        pack_kernel,
+        in_specs=[scalars, scalars, vmem, vmem, vmem],
+        out_specs=[vmem] * 3,
+        out_shape=[text, text, jax.ShapeDtypeStruct((rows + TAG_ROWS, half), queries.dtype)],
+        compiler_params=pltpu.CompilerParams(vmem_limit_bytes=VMEM_LIMIT),
+        name="pack",
+    )(side.reshape(1), prompt_of, text_k, text_v, queries)
+
+
+def whole_cross_kernel(heads, q_ref, k_ref, v_ref, o_ref):
     rows = q_ref.shape[0]
     for head in range(heads):
         cols = slice(head * HD, (head + 1) * HD)
-        keys = jnp.concatenate([piece[0, :, cols] for piece in pieces], axis=0)
-        values = jnp.concatenate([piece[1, :, cols] for piece in pieces], axis=0)
         state = (
             jnp.full((rows, HD), NEG_FILL, jnp.float32),
             jnp.zeros((rows, HD), jnp.float32),
             jnp.zeros((rows, HD), jnp.float32),
         )
-        _, mass, total = attend(q_ref[:, cols], keys, values, state, None)
+        _, mass, total = attend(q_ref[:, cols], k_ref[:, cols], v_ref[:, cols], state, None)
         o_ref[:, cols] = (total / mass).astype(o_ref.dtype)
 
 
-def cross_attention(queries, pieces):
-    rows, width = queries.shape
-    return pl.pallas_call(
-        functools.partial(cross_kernel, width // HD),
-        out_shape=jax.ShapeDtypeStruct((rows, width), jnp.bfloat16),
-        compiler_params=pltpu.CompilerParams(vmem_limit_bytes=VMEM_LIMIT),
-        name="cross_attention",
-    )(queries, *pieces)
-
-
-def pick_kernel(count, place_ref, prompt_ref, k_ref, v_ref, *refs):
-    outs, sems = refs[:count], refs[count]
-    copies = []
-    for step in range(count):
-        prompt = prompt_ref[place_ref[0] ^ step]
-        copies.append(pltpu.make_async_copy(k_ref.at[prompt], outs[step].at[0], sems.at[2 * step]))
-        copies.append(
-            pltpu.make_async_copy(v_ref.at[prompt], outs[step].at[1], sems.at[2 * step + 1])
+def whole_cross(queries, prompt_of, text_k, text_v):
+    keys, values = (
+        lax.dynamic_index_in_dim(
+            lax.all_gather(text, "req", axis=1, tiled=True), prompt_of[0], 0, keepdims=False
         )
-    for copy in copies:
-        copy.start()
-    for copy in copies:
-        copy.wait()
-
-
-def pick_text(place, prompts, text_k, text_v):
-    count = prompts.shape[0]
-    _, rows, width = text_k.shape
-    scalars = pl.BlockSpec(memory_space=pltpu.SMEM)
-    hbm = pl.BlockSpec(memory_space=pl.ANY)
-    return pl.pallas_call(
-        functools.partial(pick_kernel, count),
-        in_specs=[scalars, scalars, hbm, hbm],
-        out_specs=[hbm] * count,
-        out_shape=[jax.ShapeDtypeStruct((2, rows, width), text_k.dtype)] * count,
-        scratch_shapes=[pltpu.SemaphoreType.DMA((2 * count,))],
-        name="pick_text",
-    )(place.reshape(1), prompts, text_k, text_v)
-
-
-def project_kernel(count, place_ref, own_ref, near_ref, *refs):
+        for text in (text_k, text_v)
+    )
+    return pl.pallas_call(
+        functools.partial(whole_cross_kernel, queries.shape[1] // HD),
+        out_shape=jax.ShapeDtypeStruct(queries.shape, jnp.bfloat16),
+        compiler_params=pltpu.CompilerParams(vmem_limit_bytes=VMEM_LIMIT),
+        name="whole_cross",
+    )(queries, keys, values)
+
+
+def project_kernel(count, groups, place_ref, *refs):
+    own, near = refs[:groups], refs[groups : 2 * groups]
+    refs = refs[2 * groups :]
     held, passed = refs[:count], refs[count : 2 * count]
     o_ref, weights, sems = refs[2 * count :]
     chip, holder = place_ref[0], place_ref[1]
-    rows = own_ref.shape[0]
+    rows = own[0].shape[0]
 
     def each(choice, act):
         for step in range(count):
@@ -194,21 +239,22 @@
     for step in range(count):
         pltpu.make_async_copy(held[step], weights.at[step], sems.at[step]).wait()
         at = chip ^ step
-        for part, x_ref in enumerate((own_ref, near_ref)):
+        for part, x_refs in enumerate((own, near)):
+            x = jnp.concatenate([x_ref[...] for x_ref in x_refs], axis=1)
             o_ref[at, part * rows : (part + 1) * rows, :] = jnp.dot(
-                x_ref[...], weights[step], preferred_element_type=jnp.float32
+                x, weights[step], preferred_element_type=jnp.float32
             ).astype(o_ref.dtype)
 
 
 def project(chip, holder, own, near, held, passed):
-    count = len(held)
-    rows, depth = own.shape
-    columns = held[0].shape[1]
+    count, groups = len(held), len(own)
+    rows = own[0].shape[0]
+    depth, columns = held[0].shape
     hbm = pl.BlockSpec(memory_space=pl.ANY)
     vmem = pl.BlockSpec(memory_space=pltpu.VMEM)
     return pl.pallas_call(
-        functools.partial(project_kernel, count),
-        in_specs=[pl.BlockSpec(memory_space=pltpu.SMEM), vmem, vmem] + [hbm] * (2 * count),
+        functools.partial(project_kernel, count, groups),
+        in_specs=[pl.BlockSpec(memory_space=pltpu.SMEM)] + [vmem] * (2 * groups) + [hbm] * (2 * count),
         out_specs=vmem,
         out_shape=jax.ShapeDtypeStruct((count, 2 * rows, columns), jnp.bfloat16),
         scratch_shapes=[
@@ -217,7 +263,11 @@
         ],
         compiler_params=pltpu.CompilerParams(vmem_limit_bytes=VMEM_LIMIT),
         name="project",
-    )(jnp.stack([chip, holder]).astype(jnp.int32), own, near, *held, *passed)
+    )(jnp.stack([chip, holder]).astype(jnp.int32), *own, *near, *held, *passed)
+
+
+def after(value, *others):
+    return lax.optimization_barrier((value, *others))[0]
 
 
 def per_device(
@@ -247,46 +297,70 @@
     def swap(array, distance):
         return lax.ppermute(array, "req", [(i, i ^ distance) for i in range(reqs)])
 
-    held = [w_out]
-    held.append(
-        lax.ppermute(
-            w_out,
-            "req",
-            [(2 * i + 1 - i % 2, 2 * (i ^ 1) + 1 - i % 2) for i in range(chips)],
-        )
-    )
-    bit = 2
-    while bit < chips:
-        pairs = [(2 * i + i % 2, 2 * (i ^ bit) + i % 2) for i in range(chips)]
-        held += [lax.ppermute(block, "req", pairs) for block in held]
-        bit *= 2
-    across = [(2 * i + i % 2, 2 * i + 1 - i % 2) for i in range(chips)]
-    passed = [lax.ppermute(block, "req", across) for block in held]
-
-    prompts = lax.all_gather(prompt_of, "req", axis=0, tiled=True)
-    pieces = pick_text(place, prompts, text_k, text_v)
-    pieces = [pieces[0]] + [swap(pieces[i], i) for i in range(1, reqs)]
+    first_of = [2 * i + i % 2 for i in range(chips)]
+    second_of = [2 * i + 1 - i % 2 for i in range(chips)]
+    beside = lax.ppermute(
+        w_out,
+        "req",
+        [(first_of[i], first_of[i ^ 2]) for i in range(chips)]
+        + [(second_of[i], second_of[i ^ 1]) for i in range(chips)],
+    )
+    own_passed = lax.ppermute(w_out, "req", list(zip(first_of, second_of)))
 
     groups = HEAD_GROUPS if (width // HD) % HEAD_GROUPS == 0 else 1
     group_width = width // groups
-    parts = [
-        self_attention(
-            q_new, k_new, v_new, cache_k[0], cache_v[0], length, 0, rows, group, group_width
+    own, near = [], []
+    for group in range(groups):
+        queries = q_new if group == 0 else after(q_new, beside)
+        own.append(
+            self_attention(
+                queries, k_new, v_new, cache_k[0], cache_v[0], length, 0, rows, group, group_width
+            )
         )
-        for group in range(groups)
-    ]
-    own = jnp.concatenate(parts, axis=1)
-    near = swap(own, 2)
+        near.append(swap(own[-1], 2))
+        if group == 0:
+            beside = after(beside, own[0])
+            across = lax.ppermute(
+                beside, "req", [(second_of[i], second_of[i ^ 2]) for i in range(chips)]
+            )
+            beside_passed = swap(beside, 1)
+    across_passed = lax.ppermute(across, "req", list(zip(second_of, first_of)))
+    held = [w_out, beside_passed, beside, across_passed]
+    passed = [own_passed, beside, beside_passed, across]
+    bit = 4
+    while bit < chips:
+        held += [swap(block, 2 * bit) for block in held]
+        passed += [swap(block, 2 * bit) for block in passed]
+        bit *= 2
     terms = project(chip, holder, own, near, held, passed)
     summed = lax.psum_scatter(terms, "tp", scatter_dimension=0, tiled=True)
+
+    def in_order(kept, received, axis):
+        return jnp.where(
+            side == 0,
+            jnp.concatenate([kept, received], axis=axis),
+            jnp.concatenate([received, kept], axis=axis),
+        )
+
+    if (width // HD) % 2 == 0:
+        keep, give, ask = pack(side, prompt_of, text_k, text_v, after(q_cross, own[-1]))
+        from_x = swap(give, 2)
+        asked = swap(ask, 2)
+        pieces = [keep, from_x]
+        bit = 2
+        while bit < chips:
+            pieces += [swap(piece, 2 * bit) for piece in pieces]
+            bit *= 2
+        pieces += [swap(piece, 1) for piece in pieces]
+        prompts = jnp.concatenate([prompt_of, asked[rows, :1].astype(jnp.int32)])
+        mine, others = cross_attention(prompts, side, q_cross, asked, pieces)
+        cross_heads = in_order(mine, swap(others, 2), 1)
+    else:
+        cross_heads = whole_cross(q_cross, prompt_of, text_k, text_v)
+
     kept, given = summed[:, :rows], summed[:, rows:]
-    received = swap(given, 2)
-    ordered = jnp.where(
-        side == 0, jnp.stack([kept, received], axis=1), jnp.stack([received, kept], axis=1)
-    )
-    ordered = ordered.transpose(2, 0, 1, 3).reshape(rows, -1)
+    ordered = in_order(kept, swap(given, 2), 2).transpose(1, 0, 2).reshape(rows, width)
     hidden_out = (hidden.astype(jnp.float32) + ordered.astype(jnp.float32)).astype(jnp.bfloat16)
-    cross_heads = cross_attention(q_cross, pieces)
     return (hidden_out, cross_heads)
 
 

time: 242 us -> 163 us (0.67)
  Pallas kernels: 109 us -> 30.5 us
  blocking collectives: 9.68 us -> 0 us
  waiting for transfers between devices: 65.5 us -> 71.9 us
  starting transfers between devices: 27.7 us -> 33.7 us
  local copies, waits for them, and re-layouts: 12.2 us -> 8.51 us
    pallas_call x3, Pallas kernels: 92.8 us -> 13 us  [the longest x1 8.21 us: project(): pl.pallas_call(functools.partial(project_kernel, count, groups), in_specs...]
    ppermute x9 -> x13, waiting for transfers between devices: 36.2 us -> 64.1 us  [swap(): return lax.ppermute(array, 'req', [(i, i ^ distance) for i in range(reqs)])]
    ppermute x7 -> x4, waiting for transfers between devices: 29.3 us -> 6.07 us  [the longest x1 6.06 us: per_device(): lax.ppermute(w_out, 'req', [(first_of[i], first_of[i ^ 2]) for i in range...]
    ppermute x9 -> x13, starting transfers between devices: 6.92 us -> 22.8 us  [swap(): return lax.ppermute(array, 'req', [(i, i ^ distance) for i in range(reqs)])]
    ppermute x7 -> x4, starting transfers between devices: 20.7 us -> 10.9 us  [the longest x1 4.58 us: per_device(): own_passed = lax.ppermute(w_out, 'req', list(zip(first_of, second_of)))]
    unnamed x1 -> x0, blocking collectives: 9.68 us -> none
    unnamed x23 -> x20, local copies, waits for them, and re-layouts: 8.55 us -> 5.6 us
  transfers between devices with their start and end apart: 17 -> 18, of which waited for: 6 -> 8; matrix products, arithmetic and copies ran while one was open for 3% -> 2% of each run, Pallas kernels for 42% -> 14%
where the time goes in v2:
time: 163 us; the launch traced here: 162 us
  waiting for transfers between devices  71.9 us (44%)
  starting transfers between devices  33.7 us (21%)
  Pallas kernels  30.5 us (19%)
  between operations  15.6 us (10%)
  local copies, waits for them, and re-layouts  8.51 us (5%)
  other arithmetic  2.21 us (1%)
    ppermute x13, waiting for transfers between devices, swap(): return lax.ppermute(array, 'req', [(i, i ^ distance) for i in range(reqs)])  64.1 us
    ppermute x13, starting transfers between devices, swap(): return lax.ppermute(array, 'req', [(i, i ^ distance) for i in range(reqs)])  22.8 us
    pallas_call x2, Pallas kernels, self_attention(): pl.pallas_call(functools.partial(self_kernel, block_rows, heads, first_ro...  17.5 us
    pallas_call x1, Pallas kernels, project(): pl.pallas_call(functools.partial(project_kernel, count, groups), in_specs...  8.21 us
    ppermute x1, waiting for transfers between devices, per_device(): lax.ppermute(w_out, 'req', [(first_of[i], first_of[i ^ 2]) for i in range...  6.06 us
    unnamed x20, local copies, waits for them, and re-layouts  5.6 us
    pallas_call x1, Pallas kernels, cross_attention(): pl.pallas_call(functools.partial(cross_kernel, half // HD, len(pieces)),...  4.62 us
    ppermute x1, starting transfers between devices, per_device(): own_passed = lax.ppermute(w_out, 'req', list(zip(first_of, second_of)))  4.58 us
  transfers between devices with their start and end apart: 18, of which 8 were waited for; matrix products, arithmetic and copies ran while one was open for 2% of the time, Pallas kernels for 14%

profile of v2, /device:TPU:0, one launch (start us, length us, event | category | flops | bytes accessed | tf_op | source)
XLA Modules:
  0.0 162.5 jit_solution(16642833110003622132)
XLA Ops:
  7.2 3.0 %collective-permute-start = (bf16[1280,640]{1,0:T(8,128)(2,1)}, bf16[1280,640]{1,0:T(8,128)(2,1)}, u32[]{:S(2)}, u32[]{:S(2)}) collective-permute-start(bf16[1280,640]{1,0:T(8,128)(2,1)} %refs_4_.1), channel_id=1, source_target_pairs={{0,16},{12,28},{16,0},{28,12},{4,8},{8,4},{20,24},{24,20},{1,17},{... | collective-permute-start | bytes 4915208 | tf_op jit(solution)/shard_map/ppermute | solution.py:302
  10.2 1.3 dynamic_slice.4.length_ref
  11.5 1.1 copy-done
  12.6 1.1 copy-done.1
  13.7 1.1 copy-done.2
  14.8 8.8 %self_attention.2.refs_0_ = bf16[256,640]{1,0:T(8,128)(2,1)} custom-call(s32[1]{0:T(128)} %dynamic_slice.4.length_ref, bf16[256,1280]{1,0:T(8,128)(2,1)S(1)} %copy-done, bf16[256,1280]{1,0:T(8,128)(2,1)S(1)} %copy-done.1, bf16[256,1280]{1,0:T(8,128)(2,1)S(1)} %copy-done.2, bf16[4096,1280]{1,0:T(8,128)(2,1)} %bitcast.10, bf16[4096,1280]{1,0:T(8,128)(2,1)} %bitcast.12), custom_call_target="tpu_custom_call" | custom-call | flops 2852126720 | bytes 11141120 | tf_op jit(solution)/shard_map/self_attention/pallas_call | solution.py:91
  23.6 6.1 %collective-permute-done.refs_6_.refs_9_ = bf16[1280,640]{1,0:T(8,128)(2,1)} collective-permute-done((bf16[1280,640]{1,0:T(8,128)(2,1)}, bf16[1280,640]{1,0:T(8,128)(2,1)}, u32[]{:S(2)}, u32[]{:S(2)}) %collective-permute-start) | collective-permute-done | bytes 1638432 | tf_op jit(solution)/shard_map/ppermute | solution.py:302
  29.7 1.8 %collective-permute-start.4 = (bf16[1280,640]{1,0:T(8,128)(2,1)}, bf16[1280,640]{1,0:T(8,128)(2,1)}, u32[]{:S(2)}, u32[]{:S(2)}) collective-permute-start(bf16[1280,640]{1,0:T(8,128)(2,1)} %collective-permute-done.refs_6_.refs_9_), channel_id=1, source_target_pairs={{4,20},{8,24},{20,4},{24,8},{5,21},{9,25},{21,5},{25,9},{6,22},{10... | collective-permute-start | bytes 4915208 | tf_op jit(solution)/shard_map/ppermute | solution.py:323
  31.5 4.6 %collective-permute-start.6 = (bf16[1280,640]{1,0:T(8,128)(2,1)S(1)}, bf16[1280,640]{1,0:T(8,128)(2,1)}, u32[]{:S(2)}, u32[]{:S(2)}) collective-permute-start(bf16[1280,640]{1,0:T(8,128)(2,1)S(1)} %copy-done.4), channel_id=1, source_target_pairs={{0,4},{12,8},{16,20},{28,24},{1,5},{13,9},{17,21},{29,25},{2,6},{1... | collective-permute-start | bytes 4915208 | tf_op jit(solution)/shard_map/ppermute | solution.py:308
  36.1 1.5 collective-permute-start.5
  37.6 19.3 %collective-permute-start.1 = (bf16[256,640]{1,0:T(8,128)(2,1)}, bf16[256,640]{1,0:T(8,128)(2,1)}, u32[]{:S(2)}, u32[]{:S(2)}) collective-permute-start(bf16[256,640]{1,0:T(8,128)(2,1)} %self_attention.2.refs_0_), channel_id=1, source_target_pairs={{0,8},{4,12},{8,0},{12,4},{16,24},{20,28},{24,16},{28,20},{1,9},{5... | collective-permute-start | bytes 983048 | tf_op jit(solution)/shard_map/ppermute | solution.py:298
  56.9 8.7 %self_attention.3.refs_1_ = bf16[256,640]{1,0:T(8,128)(2,1)} custom-call(s32[1]{0:T(128)} %dynamic_slice.4.length_ref, bf16[256,1280]{1,0:T(8,128)(2,1)S(1)} %copy-done, bf16[256,1280]{1,0:T(8,128)(2,1)S(1)} %copy-done.1, bf16[256,1280]{1,0:T(8,128)(2,1)S(1)} %copy-done.2, bf16[4096,1280]{1,0:T(8,128)(2,1)} %bitcast.11, bf16[4096,1280]{1,0:T(8,128)(2,1)} %bitcast.13), custom_call_target="tpu_custom_call" | custom-call | flops 2852126720 | bytes 11141120 | tf_op jit(solution)/shard_map/self_attention/pallas_call | solution.py:91
  65.7 10.4 %collective-permute-done.2.refs_3_ = bf16[256,640]{1,0:T(8,128)(2,1)} collective-permute-done((bf16[256,640]{1,0:T(8,128)(2,1)}, bf16[256,640]{1,0:T(8,128)(2,1)}, u32[]{:S(2)}, u32[]{:S(2)}) %collective-permute-start.2) | collective-permute-done | bytes 327712 | tf_op jit(solution)/shard_map/ppermute | solution.py:298
  76.1 8.2 %project.1 = bf16[4,512,640]{2,1,0:T(8,128)(2,1)} custom-call(s32[2]{0:T(128)S(1)} %pad_add_fusion.place_ref, bf16[256,640]{1,0:T(8,128)(2,1)} %self_attention.2.refs_0_, bf16[256,640]{1,0:T(8,128)(2,1)} %self_attention.3.refs_1_, bf16[256,640]{1,0:T(8,128)(2,1)} %collective-permute-done.1.refs_2_, bf16[256,640]{1,0:T(8,128)(2,1)} %collective-permute-done.2.refs_3_, ...), custom_call_target="tpu_custom_call" | custom-call | tf_op jit(solution)/shard_map/project/pallas_call | solution.py:255
  86.4 16.9 %collective-permute-done.9.refs_1_ = bf16[2,4,64,640]{3,2,1,0:T(8,128)(2,1)S(1)} collective-permute-done((bf16[2,4,64,640]{3,2,1,0:T(8,128)(2,1)S(1)}, bf16[2,4,64,640]{3,2,1,0:T(8,128)(2,1)S(1)}, u32[]{:S(2)}, u32[]{:S(2)}) %collective-permute-start.9) | collective-permute-done | bytes 655392 | tf_op jit(solution)/shard_map/ppermute | solution.py:298
  104.2 15.7 %collective-permute-done.11.refs_3_ = bf16[2,4,64,640]{3,2,1,0:T(8,128)(2,1)S(1)} collective-permute-done((bf16[2,4,64,640]{3,2,1,0:T(8,128)(2,1)S(1)}, bf16[2,4,64,640]{3,2,1,0:T(8,128)(2,1)S(1)}, u32[]{:S(2)}, u32[]{:S(2)}) %collective-permute-start.11) | collective-permute-done | bytes 655392 | tf_op jit(solution)/shard_map/ppermute | solution.py:298
  120.0 10.4 %collective-permute-done.8.near_ref = bf16[272,640]{1,0:T(8,128)(2,1)S(1)} collective-permute-done((bf16[272,640]{1,0:T(8,128)(2,1)S(1)}, bf16[272,640]{1,0:T(8,128)(2,1)S(1)}, u32[]{:S(2)}, u32[]{:S(2)}) %collective-permute-start.8) | collective-permute-done | bytes 348192 | tf_op jit(solution)/shard_map/ppermute | solution.py:298
  133.4 4.6 %cross_attention.1 = (bf16[256,640]{1,0:T(8,128)(2,1)S(1)}, bf16[256,640]{1,0:T(8,128)(2,1)S(1)}) custom-call(s32[2]{0:T(128)S(1)} %pad_add_fusion.1.prompts_ref, s32[1]{0:T(128)} %bitcast.6.side_ref, bf16[256,1280]{1,0:T(8,128)(2,1)S(1)} %copy-done.3, bf16[272,640]{1,0:T(8,128)(2,1)S(1)} %collective-permute-done.8.near_ref, ...), custom_call_target="tpu_custom_call" | custom-call | tf_op jit(solution)/shard_map/cross_attention/pallas_call | solution.py:152
  138.4 1.8 %reduce-scatter.2.cloned.1.call-done = bf16[1,512,640]{2,1,0:T(8,128)(2,1)} async-done(((bf16[4,512,640]{2,1,0:T(8,128)(2,1)}), bf16[1,512,640]{2,1,0:T(8,128)(2,1)}) %reduce-scatter.2.cloned.1.call-update) | async-done | bytes 655376 | tf_op jit(solution)/shard_map/reduce_scatter | solution.py:336
  140.1 1.1 slice_bitcast_fusion
  141.3 1.5 collective-permute-start.7
  142.8 5.9 %collective-permute-done.16 = bf16[256,640]{1,0:T(8,128)(2,1)S(1)} collective-permute-done((bf16[256,640]{1,0:T(8,128)(2,1)S(1)}, bf16[256,640]{1,0:T(8,128)(2,1)S(1)}, u32[]{:S(2)}, u32[]{:S(2)}) %collective-permute-start.16) | collective-permute-done | bytes 327712 | tf_op jit(solution)/shard_map/ppermute | solution.py:298
  149.6 4.9 %collective-permute-done.7 = bf16[1,256,640]{2,1,0:T(8,128)(2,1)S(1)} collective-permute-done((bf16[1,256,640]{2,1,0:T(8,128)(2,1)S(1)}, bf16[1,256,640]{2,1,0:T(8,128)(2,1)S(1)}, u32[]{:S(2)}, u32[]{:S(2)}) %collective-permute-start.7) | collective-permute-done | bytes 327712 | tf_op jit(solution)/shard_map/ppermute | solution.py:298
  154.5 1.1 add_convert_fusion
  (45 shorter events, 6.2 us)
Async XLA Ops:
  7.2 133.0 %reduce-scatter.2.cloned.1.call-start = ((), (), s32[]{:S(2)}) async-start(), calls=%async_computation.1 | async-start | bytes 3276800 | tf_op jit(solution)/shard_map/reduce_scatter | solution.py:336
  7.2 22.4 %collective-permute-start = (bf16[1280,640]{1,0:T(8,128)(2,1)}, bf16[1280,640]{1,0:T(8,128)(2,1)}, u32[]{:S(2)}, u32[]{:S(2)}) collective-permute-start(bf16[1280,640]{1,0:T(8,128)(2,1)} %refs_4_.1), channel_id=1, source_target_pairs={{0,16},{12,28},{16,0},{28,12},{4,8},{8,4},{20,24},{24,20},{1,17},{... | collective-permute-start | bytes 4915208 | tf_op jit(solution)/shard_map/ppermute | solution.py:302
  11.5 1.1 copy-start
  14.8 16.7 %copy-start.4 = (bf16[1280,640]{1,0:T(8,128)(2,1)S(1)}, bf16[1280,640]{1,0:T(8,128)(2,1)}, u32[]{:S(2)}) copy-start(bf16[1280,640]{1,0:T(8,128)(2,1)} %refs_4_.1) | copy-start | bytes 4915204
  29.7 6.4 %collective-permute-start.4 = (bf16[1280,640]{1,0:T(8,128)(2,1)}, bf16[1280,640]{1,0:T(8,128)(2,1)}, u32[]{:S(2)}, u32[]{:S(2)}) collective-permute-start(bf16[1280,640]{1,0:T(8,128)(2,1)} %collective-permute-done.refs_6_.refs_9_), channel_id=1, source_target_pairs={{4,20},{8,24},{20,4},{24,8},{5,21},{9,25},{21,5},{25,9},{6,22},{10... | collective-permute-start | bytes 4915208 | tf_op jit(solution)/shard_map/ppermute | solution.py:323
  31.5 34.2 %collective-permute-start.6 = (bf16[1280,640]{1,0:T(8,128)(2,1)S(1)}, bf16[1280,640]{1,0:T(8,128)(2,1)}, u32[]{:S(2)}, u32[]{:S(2)}) collective-permute-start(bf16[1280,640]{1,0:T(8,128)(2,1)S(1)} %copy-done.4), channel_id=1, source_target_pairs={{0,4},{12,8},{16,20},{28,24},{1,5},{13,9},{17,21},{29,25},{2,6},{1... | collective-permute-start | bytes 4915208 | tf_op jit(solution)/shard_map/ppermute | solution.py:308
  36.1 40.0 %collective-permute-start.3 = (bf16[1280,640]{1,0:T(8,128)(2,1)}, bf16[1280,640]{1,0:T(8,128)(2,1)S(1)}, u32[]{:S(2)}, u32[]{:S(2)}) collective-permute-start(bf16[1280,640]{1,0:T(8,128)(2,1)} %collective-permute-done.refs_6_.refs_9_), channel_id=1, source_target_pairs={{0,4},{4,0},{8,12},{12,8},{16,20},{20,16},{24,28},{28,24},{1,5},{5... | collective-permute-start | bytes 4915208 | tf_op jit(solution)/shard_map/ppermute | solution.py:298
  36.1 40.0 %collective-permute-start.5 = (bf16[1280,640]{1,0:T(8,128)(2,1)}, bf16[1280,640]{1,0:T(8,128)(2,1)}, u32[]{:S(2)}, u32[]{:S(2)}) collective-permute-start(bf16[1280,640]{1,0:T(8,128)(2,1)} %collective-permute-done.4.refs_11_), channel_id=1, source_target_pairs={{4,0},{8,12},{20,16},{24,28},{5,1},{9,13},{21,17},{25,29},{6,2},{1... | collective-permute-start | bytes 4915208 | tf_op jit(solution)/shard_map/ppermute | solution.py:327
  37.6 28.1 %collective-permute-start.1 = (bf16[256,640]{1,0:T(8,128)(2,1)}, bf16[256,640]{1,0:T(8,128)(2,1)}, u32[]{:S(2)}, u32[]{:S(2)}) collective-permute-start(bf16[256,640]{1,0:T(8,128)(2,1)} %self_attention.2.refs_0_), channel_id=1, source_target_pairs={{0,8},{4,12},{8,0},{12,4},{16,24},{20,28},{24,16},{28,20},{1,9},{5... | collective-permute-start | bytes 983048 | tf_op jit(solution)/shard_map/ppermute | solution.py:298
  65.6 10.5 %collective-permute-start.2 = (bf16[256,640]{1,0:T(8,128)(2,1)}, bf16[256,640]{1,0:T(8,128)(2,1)}, u32[]{:S(2)}, u32[]{:S(2)}) collective-permute-start(bf16[256,640]{1,0:T(8,128)(2,1)} %self_attention.3.refs_1_), channel_id=1, source_target_pairs={{0,8},{4,12},{8,0},{12,4},{16,24},{20,28},{24,16},{28,20},{1,9},{5... | collective-permute-start | bytes 983048 | tf_op jit(solution)/shard_map/ppermute | solution.py:298
  84.3 1.1 copy-start.3
  84.3 1.3 copy-start.5
  84.3 1.5 copy-start.6
  85.9 17.3 %collective-permute-start.9 = (bf16[2,4,64,640]{3,2,1,0:T(8,128)(2,1)S(1)}, bf16[2,4,64,640]{3,2,1,0:T(8,128)(2,1)S(1)}, u32[]{:S(2)}, u32[]{:S(2)}) collective-permute-start(bf16[2,4,64,640]{3,2,1,0:T(8,128)(2,1)S(1)} %get-tuple-element.15), channel_id=1, source_target_pairs={{0,8},{4,12},{8,0},{12,4},{16,24},{20,28},{24,16},{28,20},{1,9},{5... | collective-permute-start | bytes 1966088 | tf_op jit(solution)/shard_map/ppermute | solution.py:298
  86.4 17.4 %collective-permute-start.10 = (bf16[2,4,64,640]{3,2,1,0:T(8,128)(2,1)S(1)}, bf16[2,4,64,640]{3,2,1,0:T(8,128)(2,1)S(1)}, u32[]{:S(2)}, u32[]{:S(2)}) collective-permute-start(bf16[2,4,64,640]{3,2,1,0:T(8,128)(2,1)S(1)} %get-tuple-element.14.refs_0_), channel_id=1, source_target_pairs={{0,16},{4,20},{8,24},{12,28},{16,0},{20,4},{24,8},{28,12},{1,17},{... | collective-permute-start | bytes 1966088 | tf_op jit(solution)/shard_map/ppermute | solution.py:298
  103.3 16.6 %collective-permute-start.11 = (bf16[2,4,64,640]{3,2,1,0:T(8,128)(2,1)S(1)}, bf16[2,4,64,640]{3,2,1,0:T(8,128)(2,1)S(1)}, u32[]{:S(2)}, u32[]{:S(2)}) collective-permute-start(bf16[2,4,64,640]{3,2,1,0:T(8,128)(2,1)S(1)} %collective-permute-done.9.refs_1_), channel_id=1, source_target_pairs={{0,16},{4,20},{8,24},{12,28},{16,0},{20,4},{24,8},{28,12},{1,17},{... | collective-permute-start | bytes 1966088 | tf_op jit(solution)/shard_map/ppermute | solution.py:298
  103.3 28.4 %collective-permute-start.12 = (bf16[2,4,64,640]{3,2,1,0:T(8,128)(2,1)S(1)}, bf16[2,4,64,640]{3,2,1,0:T(8,128)(2,1)S(1)}, u32[]{:S(2)}, u32[]{:S(2)}) collective-permute-start(bf16[2,4,64,640]{3,2,1,0:T(8,128)(2,1)S(1)} %get-tuple-element.14.refs_0_), channel_id=1, source_target_pairs={{0,4},{4,0},{8,12},{12,8},{16,20},{20,16},{24,28},{28,24},{1,5},{5... | collective-permute-start | bytes 1966088 | tf_op jit(solution)/shard_map/ppermute | solution.py:298
  103.3 28.4 %collective-permute-start.13 = (bf16[2,4,64,640]{3,2,1,0:T(8,128)(2,1)S(1)}, bf16[2,4,64,640]{3,2,1,0:T(8,128)(2,1)S(1)}, u32[]{:S(2)}, u32[]{:S(2)}) collective-permute-start(bf16[2,4,64,640]{3,2,1,0:T(8,128)(2,1)S(1)} %collective-permute-done.9.refs_1_), channel_id=1, source_target_pairs={{0,4},{4,0},{8,12},{12,8},{16,20},{20,16},{24,28},{28,24},{1,5},{5... | collective-permute-start | bytes 1966088 | tf_op jit(solution)/shard_map/ppermute | solution.py:298
  103.8 27.9 %collective-permute-start.14 = (bf16[2,4,64,640]{3,2,1,0:T(8,128)(2,1)S(1)}, bf16[2,4,64,640]{3,2,1,0:T(8,128)(2,1)S(1)}, u32[]{:S(2)}, u32[]{:S(2)}) collective-permute-start(bf16[2,4,64,640]{3,2,1,0:T(8,128)(2,1)S(1)} %collective-permute-done.10.refs_2_), channel_id=1, source_target_pairs={{0,4},{4,0},{8,12},{12,8},{16,20},{20,16},{24,28},{28,24},{1,5},{5... | collective-permute-start | bytes 1966088 | tf_op jit(solution)/shard_map/ppermute | solution.py:298
  119.9 11.8 %collective-permute-start.15 = (bf16[2,4,64,640]{3,2,1,0:T(8,128)(2,1)S(1)}, bf16[2,4,64,640]{3,2,1,0:T(8,128)(2,1)S(1)}, u32[]{:S(2)}, u32[]{:S(2)}) collective-permute-start(bf16[2,4,64,640]{3,2,1,0:T(8,128)(2,1)S(1)} %collective-permute-done.11.refs_3_), channel_id=1, source_target_pairs={{0,4},{4,0},{8,12},{12,8},{16,20},{20,16},{24,28},{28,24},{1,5},{5... | collective-permute-start | bytes 1966088 | tf_op jit(solution)/shard_map/ppermute | solution.py:298
  119.9 10.6 %collective-permute-start.8 = (bf16[272,640]{1,0:T(8,128)(2,1)S(1)}, bf16[272,640]{1,0:T(8,128)(2,1)S(1)}, u32[]{:S(2)}, u32[]{:S(2)}) collective-permute-start(bf16[272,640]{1,0:T(8,128)(2,1)S(1)} %get-tuple-element.13), channel_id=1, source_target_pairs={{0,8},{4,12},{8,0},{12,4},{16,24},{20,28},{24,16},{28,20},{1,9},{5... | collective-permute-start | bytes 1044488 | tf_op jit(solution)/shard_map/ppermute | solution.py:298
  138.0 16.6 %copy-start.9 = (bf16[256,1280]{1,0:T(8,128)(2,1)S(1)}, bf16[256,1280]{1,0:T(8,128)(2,1)}, u32[]{:S(2)}) copy-start(bf16[256,1280]{1,0:T(8,128)(2,1)} %param.12) | copy-start | bytes 1966084
  138.0 10.7 %collective-permute-start.16 = (bf16[256,640]{1,0:T(8,128)(2,1)S(1)}, bf16[256,640]{1,0:T(8,128)(2,1)S(1)}, u32[]{:S(2)}, u32[]{:S(2)}) collective-permute-start(bf16[256,640]{1,0:T(8,128)(2,1)S(1)} %get-tuple-element.17), channel_id=1, source_target_pairs={{0,8},{4,12},{8,0},{12,4},{16,24},{20,28},{24,16},{28,20},{1,9},{5... | collective-permute-start | bytes 983048 | tf_op jit(solution)/shard_map/ppermute | solution.py:298
  141.3 13.3 %collective-permute-start.7 = (bf16[1,256,640]{2,1,0:T(8,128)(2,1)S(1)}, bf16[1,256,640]{2,1,0:T(8,128)(2,1)S(1)}, u32[]{:S(2)}, u32[]{:S(2)}) collective-permute-start(bf16[1,256,640]{2,1,0:T(8,128)(2,1)S(1)} %get-tuple-element.19), channel_id=1, source_target_pairs={{0,8},{4,12},{8,0},{12,4},{16,24},{20,28},{24,16},{28,20},{1,9},{5... | collective-permute-start | bytes 983048 | tf_op jit(solution)/shard_map/ppermute | solution.py:298
  (4 other events, 3.8 us)
Sparse Core Ops, SparseCore 0:
  84.5 55.6 reduce-scatter.1

commit v3 on v2

--- a/solution.py
+++ b/solution.py
@@ -13,33 +13,55 @@
 TAG_ROWS = 16
 NEG_FILL = -1e30
 LOG2E = 1.4426950408889634
-VMEM_LIMIT = 48 * 2**20
-
-
-def attend(queries, keys, values, state, visible):
-    top_old, mass, total = state
+VMEM_LIMIT = 60 * 2**20
+
+
+def repeat_lanes(array, times):
+    return jnp.concatenate([array] * times, axis=1) if times > 1 else array
+
+
+def score(queries, keys):
+    return lax.dot_general(
+        queries, keys, (((1,), (1,)), ((), ())), preferred_element_type=jnp.float32
+    )
+
+
+def absorb(scores, values, state, visible):
+    top_old, total = state
     scale = HD ** (-0.5) * LOG2E
-    scores = lax.dot_general(
-        queries, keys, (((1,), (1,)), ((), ())), preferred_element_type=jnp.float32
-    )
     if visible is not None:
         scores = jnp.where(visible, scores, NEG_FILL)
     top = jnp.maximum(top_old, jnp.max(scores, axis=1, keepdims=True))
     shrink = jnp.exp2((top_old - top) * scale)
-    weights = jnp.exp2(scores * scale - top[:, :1] * scale)
-    mass = mass * shrink + jnp.sum(weights, axis=1, keepdims=True)
-    total = total * shrink + lax.dot_general(
-        weights.astype(jnp.bfloat16),
-        values,
-        (((1,), (0,)), ((), ())),
-        preferred_element_type=jnp.float32,
-    )
-    return top, mass, total
+    shift = repeat_lanes(top * scale, scores.shape[1] // HD)
+    weights = jnp.exp2(scores * scale - shift).astype(jnp.bfloat16)
+    extended = jnp.concatenate([values, jnp.ones_like(values)], axis=1)
+    total = total * repeat_lanes(shrink, 2) + jnp.dot(
+        weights, extended, preferred_element_type=jnp.float32
+    )
+    return top, total
+
+
+def empty_state(rows):
+    return jnp.full((rows, HD), NEG_FILL, jnp.float32), jnp.zeros((rows, 2 * HD), jnp.float32)
+
+
+def finished(total):
+    return (total[:, :HD] / total[:, HD:]).astype(jnp.bfloat16)
+
+
+def visit_heads(count, scores_of, use):
+    ahead = scores_of(0)
+    for head in range(count):
+        scores = ahead
+        if head + 1 < count:
+            ahead = scores_of(head + 1)
+        use(head, scores)
 
 
 def self_kernel(
     block_rows, heads, first_query, length_ref, q_ref, kn_ref, vn_ref, kc_ref, vc_ref, o_ref,
-    top_ref, mass_ref, total_ref,
+    top_ref, total_ref,
 ):
     step, steps = pl.program_id(0), pl.num_programs(0)
     left = length_ref[0] - step * block_rows
@@ -47,35 +69,39 @@
 
     @pl.when(step == 0)
     def _():
-        top_ref[...] = jnp.full_like(top_ref, NEG_FILL)
-        mass_ref[...] = jnp.zeros_like(mass_ref)
-        total_ref[...] = jnp.zeros_like(total_ref)
-
-    def visit(head, k_ref, v_ref, visible):
-        cols = slice(head * HD, (head + 1) * HD)
-        state = (top_ref[head], mass_ref[head], total_ref[head])
-        state = attend(q_ref[:, cols], k_ref[:, cols], v_ref[:, cols], state, visible)
-        top_ref[head], mass_ref[head], total_ref[head] = state
-        return state
+        for head in range(heads):
+            top_ref[head], total_ref[head] = empty_state(rows)
+
+    def visit(k_ref, v_ref, visible, last):
+        def use(head, scores):
+            cols = slice(head * HD, (head + 1) * HD)
+            state = (top_ref[head], total_ref[head])
+            top, total = absorb(scores, v_ref[:, cols], state, visible)
+            if last:
+                o_ref[:, cols] = finished(total)
+            else:
+                top_ref[head], total_ref[head] = top, total
+
+        def scores_of(head):
+            cols = slice(head * HD, (head + 1) * HD)
+            return score(q_ref[:, cols], k_ref[:, cols])
+
+        visit_heads(heads, scores_of, use)
 
     @pl.when(jnp.logical_and(step < steps - 1, left >= block_rows))
     def _():
-        for head in range(heads):
-            visit(head, kc_ref, vc_ref, None)
+        visit(kc_ref, vc_ref, None, False)
 
     @pl.when(jnp.logical_and(step < steps - 1, jnp.logical_and(left > 0, left < block_rows)))
     def _():
         visible = lax.broadcasted_iota(jnp.int32, (rows, block_rows), 1) < left
-        for head in range(heads):
-            visit(head, kc_ref, vc_ref, visible)
+        visit(kc_ref, vc_ref, visible, False)
 
     @pl.when(step == steps - 1)
     def _():
         key_ids = lax.broadcasted_iota(jnp.int32, (rows, new_rows), 1)
         query_ids = lax.broadcasted_iota(jnp.int32, (rows, new_rows), 0) + first_query
-        for head in range(heads):
-            _, mass, total = visit(head, kn_ref, vn_ref, key_ids <= query_ids)
-            o_ref[:, head * HD : (head + 1) * HD] = (total / mass).astype(o_ref.dtype)
+        visit(kn_ref, vn_ref, key_ids <= query_ids, True)
 
 
 def self_attention(queries, new_keys, new_values, keys, values, length, first_row, rows, group, width):
@@ -103,8 +129,7 @@
             out_specs=pl.BlockSpec((rows, width), lambda i, n: (0, 0)),
             scratch_shapes=[
                 pltpu.VMEM((heads, rows, HD), jnp.float32),
-                pltpu.VMEM((heads, rows, HD), jnp.float32),
-                pltpu.VMEM((heads, rows, HD), jnp.float32),
+                pltpu.VMEM((heads, rows, 2 * HD), jnp.float32),
             ],
         ),
         out_shape=jax.ShapeDtypeStruct((rows, width), jnp.bfloat16),
@@ -121,27 +146,28 @@
 def cross_kernel(heads, pieces_count, prompts_ref, side_ref, q_ref, near_ref, *refs):
     pieces, (own_ref, other_ref) = refs[:pieces_count], refs[pieces_count:]
     rows = q_ref.shape[0]
-    span = pieces[0].shape[2]
     width = heads * HD
     first = pl.multiple_of(side_ref[0] * width, HD)
     for part in range(2):
         prompt = prompts_ref[part]
-        for head in range(heads):
+        target = other_ref if part else own_ref
+
+        def gathered(kind, head, prompt=prompt):
             cols = slice(head * HD, (head + 1) * HD)
+            return jnp.concatenate([piece[kind, prompt, :, cols] for piece in pieces], axis=0)
+
+        def scores_of(head, part=part, gathered=gathered):
             if part == 0:
                 queries = q_ref[:, pl.ds(pl.multiple_of(first + head * HD, HD), HD)]
             else:
-                queries = near_ref[:rows, cols]
-            keys = jnp.concatenate([piece[0, prompt, :, cols] for piece in pieces], axis=0)
-            values = jnp.concatenate([piece[1, prompt, :, cols] for piece in pieces], axis=0)
-            state = (
-                jnp.full((rows, HD), NEG_FILL, jnp.float32),
-                jnp.zeros((rows, HD), jnp.float32),
-                jnp.zeros((rows, HD), jnp.float32),
-            )
-            _, mass, total = attend(queries, keys, values, state, None)
-            target = other_ref if part else own_ref
-            target[:, cols] = (total / mass).astype(target.dtype)
+                queries = near_ref[:rows, head * HD : (head + 1) * HD]
+            return score(queries, gathered(0, head))
+
+        def use(head, scores, target=target, gathered=gathered):
+            _, total = absorb(scores, gathered(1, head), empty_state(rows), None)
+            target[:, head * HD : (head + 1) * HD] = finished(total)
+
+        visit_heads(heads, scores_of, use)
 
 
 def cross_attention(prompts, side, queries, near, pieces):
@@ -189,16 +215,16 @@
 
 
 def whole_cross_kernel(heads, q_ref, k_ref, v_ref, o_ref):
-    rows = q_ref.shape[0]
-    for head in range(heads):
+    def scores_of(head):
         cols = slice(head * HD, (head + 1) * HD)
-        state = (
-            jnp.full((rows, HD), NEG_FILL, jnp.float32),
-            jnp.zeros((rows, HD), jnp.float32),
-            jnp.zeros((rows, HD), jnp.float32),
-        )
-        _, mass, total = attend(q_ref[:, cols], k_ref[:, cols], v_ref[:, cols], state, None)
-        o_ref[:, cols] = (total / mass).astype(o_ref.dtype)
+        return score(q_ref[:, cols], k_ref[:, cols])
+
+    def use(head, scores):
+        cols = slice(head * HD, (head + 1) * HD)
+        _, total = absorb(scores, v_ref[:, cols], empty_state(q_ref.shape[0]), None)
+        o_ref[:, cols] = finished(total)
+
+    visit_heads(heads, scores_of, use)
 
 
 def whole_cross(queries, prompt_of, text_k, text_v):
@@ -222,7 +248,6 @@
     held, passed = refs[:count], refs[count : 2 * count]
     o_ref, weights, sems = refs[2 * count :]
     chip, holder = place_ref[0], place_ref[1]
-    rows = own[0].shape[0]
 
     def each(choice, act):
         for step in range(count):
@@ -236,14 +261,14 @@
     def _():
         each(passed, lambda copy: copy.start())
 
+    x = jnp.concatenate(
+        [jnp.concatenate([x_ref[...] for x_ref in x_refs], axis=1) for x_refs in (own, near)], axis=0
+    )
     for step in range(count):
         pltpu.make_async_copy(held[step], weights.at[step], sems.at[step]).wait()
-        at = chip ^ step
-        for part, x_refs in enumerate((own, near)):
-            x = jnp.concatenate([x_ref[...] for x_ref in x_refs], axis=1)
-            o_ref[at, part * rows : (part + 1) * rows, :] = jnp.dot(
-                x, weights[step], preferred_element_type=jnp.float32
-            ).astype(o_ref.dtype)
+        o_ref[chip ^ step] = jnp.dot(
+            x, weights[step], preferred_element_type=jnp.float32
+        ).astype(o_ref.dtype)
 
 
 def project(chip, holder, own, near, held, passed):
@@ -324,7 +349,7 @@
                 beside, "req", [(second_of[i], second_of[i ^ 2]) for i in range(chips)]
             )
             beside_passed = swap(beside, 1)
-    across_passed = lax.ppermute(across, "req", list(zip(second_of, first_of)))
+    across_passed = lax.ppermute(after(across, own[-1]), "req", list(zip(second_of, first_of)))
     held = [w_out, beside_passed, beside, across_passed]
     passed = [own_passed, beside, beside_passed, across]
     bit = 4

time: 163 us -> 161 us (0.988)
  local copies, waits for them, and re-layouts: 8.51 us -> 5.48 us
  starting transfers between devices: 33.7 us -> 31 us
    ppermute x1, waiting for transfers between devices: 6.06 us -> 11.4 us  [per_device(): lax.ppermute(w_out, 'req', [(first_of[i], first_of[i ^ 2]) for i in range...]
    pallas_call x2, Pallas kernels: 17.5 us -> 13.1 us  [self_attention(): pl.pallas_call(functools.partial(self_kernel, block_rows, heads, first_ro...]
    unnamed x20 -> x22, local copies, waits for them, and re-layouts: 5.6 us -> 2.4 us
    pallas_call x1, Pallas kernels: 0.13 us -> 2.78 us  [pack(): pl.pallas_call(pack_kernel, in_specs=[scalars, scalars, vmem, vmem, vmem]...]
    ppermute x13, starting transfers between devices: 22.8 us -> 20.1 us  [swap(): return lax.ppermute(array, 'req', [(i, i ^ distance) for i in range(reqs)])]
    ppermute x13, waiting for transfers between devices: 64.1 us -> 61.8 us  [swap(): return lax.ppermute(array, 'req', [(i, i ^ distance) for i in range(reqs)])]
    pallas_call x1, Pallas kernels: 8.21 us -> 10.3 us  [project(): pl.pallas_call(functools.partial(project_kernel, count, groups), in_specs...]
    reduce_scatter x1, waiting for transfers between devices: 1.77 us -> 0.01 us  [per_device(): summed = lax.psum_scatter(terms, 'tp', scatter_dimension=0, tiled=True)]
  transfers between devices with their start and end apart: 18 -> 18, of which waited for: 8 -> 8; matrix products, arithmetic and copies ran while one was open for 2% -> 3% of each run, Pallas kernels for 14% -> 14%
where the time goes in v3:
time: 161 us
  waiting for transfers between devices  73.2 us (45%)
  Pallas kernels  32 us (20%)
  starting transfers between devices  31 us (19%)
  between operations  15.5 us (10%)
  local copies, waits for them, and re-layouts  5.48 us (3%)
  other arithmetic  3.32 us (2%)
    ppermute x13, waiting for transfers between devices, swap(): return lax.ppermute(array, 'req', [(i, i ^ distance) for i in range(reqs)])  61.8 us
    ppermute x13, starting transfers between devices, swap(): return lax.ppermute(array, 'req', [(i, i ^ distance) for i in range(reqs)])  20.1 us
    pallas_call x2, Pallas kernels, self_attention(): pl.pallas_call(functools.partial(self_kernel, block_rows, heads, first_ro...  13.1 us
    ppermute x1, waiting for transfers between devices, per_device(): lax.ppermute(w_out, 'req', [(first_of[i], first_of[i ^ 2]) for i in range...  11.4 us
    pallas_call x1, Pallas kernels, project(): pl.pallas_call(functools.partial(project_kernel, count, groups), in_specs...  10.3 us
    pallas_call x1, Pallas kernels, cross_attention(): pl.pallas_call(functools.partial(cross_kernel, half // HD, len(pieces)),...  5.83 us
    ppermute x1, starting transfers between devices, per_device(): own_passed = lax.ppermute(w_out, 'req', list(zip(first_of, second_of)))  4.48 us
  transfers between devices with their start and end apart: 18, of which 8 were waited for; matrix products, arithmetic and copies ran while one was open for 3% of the time, Pallas kernels for 14%

profile of v3, /device:TPU:0, one launch (start us, length us, event | category | flops | bytes accessed | tf_op | source)
XLA Modules:
  0.0 160.5 jit_solution(16848477343129894814)
XLA Ops:
  7.2 3.0 %collective-permute-start = (bf16[1280,640]{1,0:T(8,128)(2,1)}, bf16[1280,640]{1,0:T(8,128)(2,1)S(1)}, u32[]{:S(2)}, u32[]{:S(2)}) collective-permute-start(bf16[1280,640]{1,0:T(8,128)(2,1)} %refs_4_.1), channel_id=1, source_target_pairs={{0,16},{12,28},{16,0},{28,12},{4,8},{8,4},{20,24},{24,20},{1,17},{... | collective-permute-start | bytes 4915208 | tf_op jit(solution)/shard_map/ppermute | solution.py:327
  10.2 1.3 dynamic_slice.4.length_ref
  11.6 6.6 %self_attention.2.refs_0_ = bf16[256,640]{1,0:T(8,128)(2,1)} custom-call(s32[1]{0:T(128)} %dynamic_slice.4.length_ref, bf16[256,1280]{1,0:T(8,128)(2,1)} %q_ref.3, bf16[256,1280]{1,0:T(8,128)(2,1)} %kn_ref.3, bf16[256,1280]{1,0:T(8,128)(2,1)} %vn_ref.3, bf16[4096,1280]{1,0:T(8,128)(2,1)} %bitcast.10, bf16[4096,1280]{1,0:T(8,128)(2,1)} %bitcast.12), custom_call_target="tpu_custom_call" | custom-call | flops 2852126720 | bytes 11141120 | tf_op jit(solution)/shard_map/self_attention/pallas_call | solution.py:117
  18.1 11.4 %collective-permute-done.refs_6_.refs_9_ = bf16[1280,640]{1,0:T(8,128)(2,1)S(1)} collective-permute-done((bf16[1280,640]{1,0:T(8,128)(2,1)}, bf16[1280,640]{1,0:T(8,128)(2,1)S(1)}, u32[]{:S(2)}, u32[]{:S(2)}) %collective-permute-start) | collective-permute-done | bytes 1638432 | tf_op jit(solution)/shard_map/ppermute | solution.py:327
  29.6 1.8 %collective-permute-start.4 = (bf16[1280,640]{1,0:T(8,128)(2,1)S(1)}, bf16[1280,640]{1,0:T(8,128)(2,1)}, u32[]{:S(2)}, u32[]{:S(2)}) collective-permute-start(bf16[1280,640]{1,0:T(8,128)(2,1)S(1)} %collective-permute-done.refs_6_.refs_9_), channel_id=1, source_target_pairs={{4,20},{8,24},{20,4},{24,8},{5,21},{9,25},{21,5},{25,9},{6,22},{10... | collective-permute-start | bytes 4915208 | tf_op jit(solution)/shard_map/ppermute | solution.py:348
  31.4 4.5 %collective-permute-start.6 = (bf16[1280,640]{1,0:T(8,128)(2,1)}, bf16[1280,640]{1,0:T(8,128)(2,1)}, u32[]{:S(2)}, u32[]{:S(2)}) collective-permute-start(bf16[1280,640]{1,0:T(8,128)(2,1)} %refs_4_.1), channel_id=1, source_target_pairs={{0,4},{12,8},{16,20},{28,24},{1,5},{13,9},{17,21},{29,25},{2,6},{1... | collective-permute-start | bytes 4915208 | tf_op jit(solution)/shard_map/ppermute | solution.py:333
  35.9 6.5 %self_attention.3.refs_1_ = bf16[256,640]{1,0:T(8,128)(2,1)} custom-call(s32[1]{0:T(128)} %dynamic_slice.4.length_ref, bf16[256,1280]{1,0:T(8,128)(2,1)} %q_ref.3, bf16[256,1280]{1,0:T(8,128)(2,1)} %kn_ref.3, bf16[256,1280]{1,0:T(8,128)(2,1)} %vn_ref.3, bf16[4096,1280]{1,0:T(8,128)(2,1)} %bitcast.11, bf16[4096,1280]{1,0:T(8,128)(2,1)} %bitcast.13), custom_call_target="tpu_custom_call" | custom-call | flops 2852126720 | bytes 11141120 | tf_op jit(solution)/shard_map/self_attention/pallas_call | solution.py:117
  42.4 1.5 collective-permute-start.5
  43.9 12.7 %collective-permute-start.1 = (bf16[256,640]{1,0:T(8,128)(2,1)}, bf16[256,640]{1,0:T(8,128)(2,1)}, u32[]{:S(2)}, u32[]{:S(2)}) collective-permute-start(bf16[256,640]{1,0:T(8,128)(2,1)} %self_attention.2.refs_0_), channel_id=1, source_target_pairs={{0,8},{4,12},{8,0},{12,4},{16,24},{20,28},{24,16},{28,20},{1,9},{5... | collective-permute-start | bytes 983048 | tf_op jit(solution)/shard_map/ppermute | solution.py:323
  57.3 8.3 %collective-permute-done.1.refs_2_ = bf16[256,640]{1,0:T(8,128)(2,1)} collective-permute-done((bf16[256,640]{1,0:T(8,128)(2,1)}, bf16[256,640]{1,0:T(8,128)(2,1)}, u32[]{:S(2)}, u32[]{:S(2)}) %collective-permute-start.1) | collective-permute-done | bytes 327712 | tf_op jit(solution)/shard_map/ppermute | solution.py:323
  65.6 5.5 %collective-permute-done.2.refs_3_ = bf16[256,640]{1,0:T(8,128)(2,1)} collective-permute-done((bf16[256,640]{1,0:T(8,128)(2,1)}, bf16[256,640]{1,0:T(8,128)(2,1)}, u32[]{:S(2)}, u32[]{:S(2)}) %collective-permute-start.2) | collective-permute-done | bytes 327712 | tf_op jit(solution)/shard_map/ppermute | solution.py:323
  71.1 1.2 copy-done.1
  72.3 10.3 %project.1 = bf16[4,512,640]{2,1,0:T(8,128)(2,1)} custom-call(s32[2]{0:T(128)} %pad_add_fusion.place_ref, bf16[256,640]{1,0:T(8,128)(2,1)} %self_attention.2.refs_0_, bf16[256,640]{1,0:T(8,128)(2,1)} %self_attention.3.refs_1_, bf16[256,640]{1,0:T(8,128)(2,1)} %collective-permute-done.1.refs_2_, bf16[256,640]{1,0:T(8,128)(2,1)} %collective-permute-done.2.refs_3_, ...), custom_call_target="tpu_custom_call" | custom-call | tf_op jit(solution)/shard_map/project/pallas_call | solution.py:280
  83.2 2.8 %pack.1 = (bf16[2,4,64,640]{3,2,1,0:T(8,128)(2,1)}, bf16[2,4,64,640]{3,2,1,0:T(8,128)(2,1)}, bf16[272,640]{1,0:T(8,128)(2,1)}) custom-call(s32[1]{0:T(128)} %bitcast.6.side_ref, s32[1]{0:T(128)S(6)} %copy.14.prompt_ref, bf16[4,64,1280]{2,1,0:T(8,128)(2,1)} %k_ref.1, bf16[4,64,1280]{2,1,0:T(8,128)(2,1)} %v_ref.1, bf16[256,1280]{1,0:T(8,128)(2,1)} %q_ref.5), custom_call_target="tpu_custom_call" | custom-call | tf_op jit(solution)/shard_map/pack/pallas_call | solution.py:207
  86.3 1.5 collective-permute-start.10
  87.8 13.7 %collective-permute-done.9.refs_1_ = bf16[2,4,64,640]{3,2,1,0:T(8,128)(2,1)S(1)} collective-permute-done((bf16[2,4,64,640]{3,2,1,0:T(8,128)(2,1)}, bf16[2,4,64,640]{3,2,1,0:T(8,128)(2,1)S(1)}, u32[]{:S(2)}, u32[]{:S(2)}) %collective-permute-start.9) | collective-permute-done | bytes 655392 | tf_op jit(solution)/shard_map/ppermute | solution.py:323
  101.5 1.5 collective-permute-start.11
  103.6 12.3 %collective-permute-done.11.refs_3_ = bf16[2,4,64,640]{3,2,1,0:T(8,128)(2,1)S(1)} collective-permute-done((bf16[2,4,64,640]{3,2,1,0:T(8,128)(2,1)S(1)}, bf16[2,4,64,640]{3,2,1,0:T(8,128)(2,1)S(1)}, u32[]{:S(2)}, u32[]{:S(2)}) %collective-permute-start.11) | collective-permute-done | bytes 655392 | tf_op jit(solution)/shard_map/ppermute | solution.py:323
  116.0 1.3 collective-permute-start.8
  117.3 9.4 %collective-permute-done.8.near_ref = bf16[272,640]{1,0:T(8,128)(2,1)S(1)} collective-permute-done((bf16[272,640]{1,0:T(8,128)(2,1)}, bf16[272,640]{1,0:T(8,128)(2,1)S(1)}, u32[]{:S(2)}, u32[]{:S(2)}) %collective-permute-start.8) | collective-permute-done | bytes 348192 | tf_op jit(solution)/shard_map/ppermute | solution.py:323
  130.0 5.8 %cross_attention.1 = (bf16[256,640]{1,0:T(8,128)(2,1)}, bf16[256,640]{1,0:T(8,128)(2,1)}) custom-call(s32[2]{0:T(128)} %pad_add_fusion.1.prompts_ref, s32[1]{0:T(128)} %bitcast.6.side_ref, bf16[256,1280]{1,0:T(8,128)(2,1)} %q_ref.5, bf16[272,640]{1,0:T(8,128)(2,1)} %copy-done.9, bf16[2,4,64,640]{3,2,1,0:T(8,128)(2,1)} %get-tuple-element.16.refs_0_, ...), custom_call_target="tpu_custom_call" | custom-call | tf_op jit(solution)/shard_map/cross_attention/pallas_call | solution.py:178
  135.8 1.4 collective-permute-start.16
  139.1 7.6 %collective-permute-done.16 = bf16[256,640]{1,0:T(8,128)(2,1)S(1)} collective-permute-done((bf16[256,640]{1,0:T(8,128)(2,1)}, bf16[256,640]{1,0:T(8,128)(2,1)S(1)}, u32[]{:S(2)}, u32[]{:S(2)}) %collective-permute-start.16) | collective-permute-done | bytes 327712 | tf_op jit(solution)/shard_map/ppermute | solution.py:323
  147.7 4.9 %collective-permute-done.7 = bf16[1,256,640]{2,1,0:T(8,128)(2,1)S(1)} collective-permute-done((bf16[1,256,640]{2,1,0:T(8,128)(2,1)S(1)}, bf16[1,256,640]{2,1,0:T(8,128)(2,1)S(1)}, u32[]{:S(2)}, u32[]{:S(2)}) %collective-permute-start.7) | collective-permute-done | bytes 327712 | tf_op jit(solution)/shard_map/ppermute | solution.py:323
  (47 shorter events, 8.1 us)
Async XLA Ops:
  7.2 130.1 %reduce-scatter.2.cloned.1.call-start = ((), (), s32[]{:S(2)}) async-start(), calls=%async_computation.1 | async-start | bytes 3276800 | tf_op jit(solution)/shard_map/reduce_scatter | solution.py:361
  7.2 22.3 %collective-permute-start = (bf16[1280,640]{1,0:T(8,128)(2,1)}, bf16[1280,640]{1,0:T(8,128)(2,1)S(1)}, u32[]{:S(2)}, u32[]{:S(2)}) collective-permute-start(bf16[1280,640]{1,0:T(8,128)(2,1)} %refs_4_.1), channel_id=1, source_target_pairs={{0,16},{12,28},{16,0},{28,12},{4,8},{8,4},{20,24},{24,20},{1,17},{... | collective-permute-start | bytes 4915208 | tf_op jit(solution)/shard_map/ppermute | solution.py:327
  29.6 12.9 %copy-start = (bf16[1280,640]{1,0:T(8,128)(2,1)}, bf16[1280,640]{1,0:T(8,128)(2,1)S(1)}, u32[]{:S(2)}) copy-start(bf16[1280,640]{1,0:T(8,128)(2,1)S(1)} %collective-permute-done.refs_6_.refs_9_) | copy-start | bytes 4915204
  29.6 12.9 %collective-permute-start.4 = (bf16[1280,640]{1,0:T(8,128)(2,1)S(1)}, bf16[1280,640]{1,0:T(8,128)(2,1)}, u32[]{:S(2)}, u32[]{:S(2)}) collective-permute-start(bf16[1280,640]{1,0:T(8,128)(2,1)S(1)} %collective-permute-done.refs_6_.refs_9_), channel_id=1, source_target_pairs={{4,20},{8,24},{20,4},{24,8},{5,21},{9,25},{21,5},{25,9},{6,22},{10... | collective-permute-start | bytes 4915208 | tf_op jit(solution)/shard_map/ppermute | solution.py:348
  31.4 34.2 %collective-permute-start.6 = (bf16[1280,640]{1,0:T(8,128)(2,1)}, bf16[1280,640]{1,0:T(8,128)(2,1)}, u32[]{:S(2)}, u32[]{:S(2)}) collective-permute-start(bf16[1280,640]{1,0:T(8,128)(2,1)} %refs_4_.1), channel_id=1, source_target_pairs={{0,4},{12,8},{16,20},{28,24},{1,5},{13,9},{17,21},{29,25},{2,6},{1... | collective-permute-start | bytes 4915208 | tf_op jit(solution)/shard_map/ppermute | solution.py:333
  35.9 35.2 %collective-permute-start.3 = (bf16[1280,640]{1,0:T(8,128)(2,1)S(1)}, bf16[1280,640]{1,0:T(8,128)(2,1)S(1)}, u32[]{:S(2)}, u32[]{:S(2)}) collective-permute-start(bf16[1280,640]{1,0:T(8,128)(2,1)S(1)} %collective-permute-done.refs_6_.refs_9_), channel_id=1, source_target_pairs={{0,4},{4,0},{8,12},{12,8},{16,20},{20,16},{24,28},{28,24},{1,5},{5... | collective-permute-start | bytes 4915208 | tf_op jit(solution)/shard_map/ppermute | solution.py:323
  42.4 28.7 %collective-permute-start.5 = (bf16[1280,640]{1,0:T(8,128)(2,1)}, bf16[1280,640]{1,0:T(8,128)(2,1)}, u32[]{:S(2)}, u32[]{:S(2)}) collective-permute-start(bf16[1280,640]{1,0:T(8,128)(2,1)} %collective-permute-done.4.refs_11_), channel_id=1, source_target_pairs={{4,0},{8,12},{20,16},{24,28},{5,1},{9,13},{21,17},{25,29},{6,2},{1... | collective-permute-start | bytes 4915208 | tf_op jit(solution)/shard_map/ppermute | solution.py:352
  43.9 21.6 %collective-permute-start.1 = (bf16[256,640]{1,0:T(8,128)(2,1)}, bf16[256,640]{1,0:T(8,128)(2,1)}, u32[]{:S(2)}, u32[]{:S(2)}) collective-permute-start(bf16[256,640]{1,0:T(8,128)(2,1)} %self_attention.2.refs_0_), channel_id=1, source_target_pairs={{0,8},{4,12},{8,0},{12,4},{16,24},{20,28},{24,16},{28,20},{1,9},{5... | collective-permute-start | bytes 983048 | tf_op jit(solution)/shard_map/ppermute | solution.py:323
  56.6 14.5 %collective-permute-start.2 = (bf16[256,640]{1,0:T(8,128)(2,1)}, bf16[256,640]{1,0:T(8,128)(2,1)}, u32[]{:S(2)}, u32[]{:S(2)}) collective-permute-start(bf16[256,640]{1,0:T(8,128)(2,1)} %self_attention.3.refs_1_), channel_id=1, source_target_pairs={{0,8},{4,12},{8,0},{12,4},{16,24},{20,28},{24,16},{28,20},{1,9},{5... | collective-permute-start | bytes 983048 | tf_op jit(solution)/shard_map/ppermute | solution.py:323
  86.0 15.5 %collective-permute-start.9 = (bf16[2,4,64,640]{3,2,1,0:T(8,128)(2,1)}, bf16[2,4,64,640]{3,2,1,0:T(8,128)(2,1)S(1)}, u32[]{:S(2)}, u32[]{:S(2)}) collective-permute-start(bf16[2,4,64,640]{3,2,1,0:T(8,128)(2,1)} %get-tuple-element.17), channel_id=1, source_target_pairs={{0,8},{4,12},{8,0},{12,4},{16,24},{20,28},{24,16},{28,20},{1,9},{5... | collective-permute-start | bytes 1966088 | tf_op jit(solution)/shard_map/ppermute | solution.py:323
  86.3 17.2 %collective-permute-start.10 = (bf16[2,4,64,640]{3,2,1,0:T(8,128)(2,1)}, bf16[2,4,64,640]{3,2,1,0:T(8,128)(2,1)S(1)}, u32[]{:S(2)}, u32[]{:S(2)}) collective-permute-start(bf16[2,4,64,640]{3,2,1,0:T(8,128)(2,1)} %get-tuple-element.16.refs_0_), channel_id=1, source_target_pairs={{0,16},{4,20},{8,24},{12,28},{16,0},{20,4},{24,8},{28,12},{1,17},{... | collective-permute-start | bytes 1966088 | tf_op jit(solution)/shard_map/ppermute | solution.py:323
  101.5 27.3 %copy-start.2 = (bf16[2,4,64,640]{3,2,1,0:T(8,128)(2,1)}, bf16[2,4,64,640]{3,2,1,0:T(8,128)(2,1)S(1)}, u32[]{:S(2)}) copy-start(bf16[2,4,64,640]{3,2,1,0:T(8,128)(2,1)S(1)} %collective-permute-done.9.refs_1_) | copy-start | bytes 1966084
  101.5 14.5 %collective-permute-start.11 = (bf16[2,4,64,640]{3,2,1,0:T(8,128)(2,1)S(1)}, bf16[2,4,64,640]{3,2,1,0:T(8,128)(2,1)S(1)}, u32[]{:S(2)}, u32[]{:S(2)}) collective-permute-start(bf16[2,4,64,640]{3,2,1,0:T(8,128)(2,1)S(1)} %collective-permute-done.9.refs_1_), channel_id=1, source_target_pairs={{0,16},{4,20},{8,24},{12,28},{16,0},{20,4},{24,8},{28,12},{1,17},{... | collective-permute-start | bytes 1966088 | tf_op jit(solution)/shard_map/ppermute | solution.py:323
  103.0 25.7 %collective-permute-start.12 = (bf16[2,4,64,640]{3,2,1,0:T(8,128)(2,1)}, bf16[2,4,64,640]{3,2,1,0:T(8,128)(2,1)S(1)}, u32[]{:S(2)}, u32[]{:S(2)}) collective-permute-start(bf16[2,4,64,640]{3,2,1,0:T(8,128)(2,1)} %get-tuple-element.16.refs_0_), channel_id=1, source_target_pairs={{0,4},{4,0},{8,12},{12,8},{16,20},{20,16},{24,28},{28,24},{1,5},{5... | collective-permute-start | bytes 1966088 | tf_op jit(solution)/shard_map/ppermute | solution.py:323
  103.0 25.7 %collective-permute-start.13 = (bf16[2,4,64,640]{3,2,1,0:T(8,128)(2,1)S(1)}, bf16[2,4,64,640]{3,2,1,0:T(8,128)(2,1)S(1)}, u32[]{:S(2)}, u32[]{:S(2)}) collective-permute-start(bf16[2,4,64,640]{3,2,1,0:T(8,128)(2,1)S(1)} %collective-permute-done.9.refs_1_), channel_id=1, source_target_pairs={{0,4},{4,0},{8,12},{12,8},{16,20},{20,16},{24,28},{28,24},{1,5},{5... | collective-permute-start | bytes 1966088 | tf_op jit(solution)/shard_map/ppermute | solution.py:323
  103.5 25.3 %copy-start.3 = (bf16[2,4,64,640]{3,2,1,0:T(8,128)(2,1)}, bf16[2,4,64,640]{3,2,1,0:T(8,128)(2,1)S(1)}, u32[]{:S(2)}) copy-start(bf16[2,4,64,640]{3,2,1,0:T(8,128)(2,1)S(1)} %collective-permute-done.10.refs_2_) | copy-start | bytes 1966084
  103.5 25.2 %collective-permute-start.14 = (bf16[2,4,64,640]{3,2,1,0:T(8,128)(2,1)S(1)}, bf16[2,4,64,640]{3,2,1,0:T(8,128)(2,1)S(1)}, u32[]{:S(2)}, u32[]{:S(2)}) collective-permute-start(bf16[2,4,64,640]{3,2,1,0:T(8,128)(2,1)S(1)} %collective-permute-done.10.refs_2_), channel_id=1, source_target_pairs={{0,4},{4,0},{8,12},{12,8},{16,20},{20,16},{24,28},{28,24},{1,5},{5... | collective-permute-start | bytes 1966088 | tf_op jit(solution)/shard_map/ppermute | solution.py:323
  115.9 12.8 %copy-start.4 = (bf16[2,4,64,640]{3,2,1,0:T(8,128)(2,1)}, bf16[2,4,64,640]{3,2,1,0:T(8,128)(2,1)S(1)}, u32[]{:S(2)}) copy-start(bf16[2,4,64,640]{3,2,1,0:T(8,128)(2,1)S(1)} %collective-permute-done.11.refs_3_) | copy-start | bytes 1966084
  115.9 12.8 %collective-permute-start.15 = (bf16[2,4,64,640]{3,2,1,0:T(8,128)(2,1)S(1)}, bf16[2,4,64,640]{3,2,1,0:T(8,128)(2,1)}, u32[]{:S(2)}, u32[]{:S(2)}) collective-permute-start(bf16[2,4,64,640]{3,2,1,0:T(8,128)(2,1)S(1)} %collective-permute-done.11.refs_3_), channel_id=1, source_target_pairs={{0,4},{4,0},{8,12},{12,8},{16,20},{20,16},{24,28},{28,24},{1,5},{5... | collective-permute-start | bytes 1966088 | tf_op jit(solution)/shard_map/ppermute | solution.py:323
  116.0 10.8 %collective-permute-start.8 = (bf16[272,640]{1,0:T(8,128)(2,1)}, bf16[272,640]{1,0:T(8,128)(2,1)S(1)}, u32[]{:S(2)}, u32[]{:S(2)}) collective-permute-start(bf16[272,640]{1,0:T(8,128)(2,1)} %get-tuple-element.15), channel_id=1, source_target_pairs={{0,8},{4,12},{8,0},{12,4},{16,24},{20,28},{24,16},{28,20},{1,9},{5... | collective-permute-start | bytes 1044488 | tf_op jit(solution)/shard_map/ppermute | solution.py:323
  135.8 10.9 %copy-start.10 = (bf16[256,640]{1,0:T(8,128)(2,1)S(1)}, bf16[256,640]{1,0:T(8,128)(2,1)}, u32[]{:S(2)}) copy-start(bf16[256,640]{1,0:T(8,128)(2,1)} %get-tuple-element.18) | copy-start | bytes 983044
  135.8 16.8 %copy-start.8 = (bf16[256,1280]{1,0:T(8,128)(2,1)S(1)}, bf16[256,1280]{1,0:T(8,128)(2,1)}, u32[]{:S(2)}) copy-start(bf16[256,1280]{1,0:T(8,128)(2,1)} %param.12) | copy-start | bytes 1966084
  135.8 10.9 %collective-permute-start.16 = (bf16[256,640]{1,0:T(8,128)(2,1)}, bf16[256,640]{1,0:T(8,128)(2,1)S(1)}, u32[]{:S(2)}, u32[]{:S(2)}) collective-permute-start(bf16[256,640]{1,0:T(8,128)(2,1)} %get-tuple-element.19), channel_id=1, source_target_pairs={{0,8},{4,12},{8,0},{12,4},{16,24},{20,28},{24,16},{28,20},{1,9},{5... | collective-permute-start | bytes 983048 | tf_op jit(solution)/shard_map/ppermute | solution.py:323
  138.4 14.2 %collective-permute-start.7 = (bf16[1,256,640]{2,1,0:T(8,128)(2,1)S(1)}, bf16[1,256,640]{2,1,0:T(8,128)(2,1)S(1)}, u32[]{:S(2)}, u32[]{:S(2)}) collective-permute-start(bf16[1,256,640]{2,1,0:T(8,128)(2,1)S(1)} %get-tuple-element.21), channel_id=1, source_target_pairs={{0,8},{4,12},{8,0},{12,4},{16,24},{20,28},{24,16},{28,20},{1,9},{5... | collective-permute-start | bytes 983048 | tf_op jit(solution)/shard_map/ppermute | solution.py:323
  (5 other events, 6.3 us)
Sparse Core Ops, SparseCore 0:
  82.7 52.4 reduce-scatter.1

commit v4 on v3

v4 whole, which is shorter than its diff:
```python
import functools

import jax
import jax.numpy as jnp
from jax import lax
from jax.experimental import pallas as pl
from jax.experimental.pallas import tpu as pltpu
from jax.sharding import PartitionSpec as P

HD = 128
CACHE_BLOCK = 1024
TAG_ROWS = 16
NEG_FILL = -1e30
LOG2E = 1.4426950408889634
VMEM_LIMIT = 60 * 2**20
PEAK = 1.1535e15


def cost_of(seconds):
    return pl.CostEstimate(flops=int(seconds * PEAK), bytes_accessed=0, transcendentals=0)


def repeat_lanes(array, times):
    return jnp.concatenate([array] * times, axis=1) if times > 1 else array


def score(queries, keys):
    return lax.dot_general(
        queries, keys, (((1,), (1,)), ((), ())), preferred_element_type=jnp.float32
    )


def absorb(scores, values, state, visible):
    top_old, total = state
    scale = HD ** (-0.5) * LOG2E
    if visible is not None:
        scores = jnp.where(visible, scores, NEG_FILL)
    top = jnp.maximum(top_old, jnp.max(scores, axis=1, keepdims=True))
    shrink = jnp.exp2((top_old - top) * scale)
    shift = repeat_lanes(top * scale, scores.shape[1] // HD)
    weights = jnp.exp2(scores * scale - shift).astype(jnp.bfloat16)
    extended = jnp.concatenate([values, jnp.ones_like(values)], axis=1)
    total = total * repeat_lanes(shrink, 2) + jnp.dot(
        weights, extended, preferred_element_type=jnp.float32
    )
    return top, total


def empty_state(rows):
    return jnp.full((rows, HD), NEG_FILL, jnp.float32), jnp.zeros((rows, 2 * HD), jnp.float32)


def finished(total):
    return (total[:, :HD] / total[:, HD:]).astype(jnp.bfloat16)


def visit_heads(count, scores_of, use):
    ahead = scores_of(0)
    for head in range(count):
        scores = ahead
        if head + 1 < count:
            ahead = scores_of(head + 1)
        use(head, scores)


def self_kernel(
    block_rows, heads, length_ref, q_ref, kn_ref, vn_ref, kc_ref, vc_ref, o_ref, top_ref, total_ref
):
    step, steps = pl.program_id(0), pl.num_programs(0)
    left = length_ref[0] - step * block_rows
    rows, new_rows = q_ref.shape[0], kn_ref.shape[0]

    @pl.when(step == 0)
    def _():
        for head in range(heads):
            top_ref[head], total_ref[head] = empty_state(rows)

    def visit(k_ref, v_ref, visible, last):
        def use(head, scores):
            cols = slice(head * HD, (head + 1) * HD)
            state = (top_ref[head], total_ref[head])
            top, total = absorb(scores, v_ref[:, cols], state, visible)
            if last:
                o_ref[:, cols] = finished(total)
            else:
                top_ref[head], total_ref[head] = top, total

        def scores_of(head):
            cols = slice(head * HD, (head + 1) * HD)
            return score(q_ref[:, cols], k_ref[:, cols])

        visit_heads(heads, scores_of, use)

    @pl.when(jnp.logical_and(step < steps - 1, left >= block_rows))
    def _():
        visit(kc_ref, vc_ref, None, False)

    @pl.when(jnp.logical_and(step < steps - 1, jnp.logical_and(left > 0, left < block_rows)))
    def _():
        visible = lax.broadcasted_iota(jnp.int32, (rows, block_rows), 1) < left
        visit(kc_ref, vc_ref, visible, False)

    @pl.when(step == steps - 1)
    def _():
        key_ids = lax.broadcasted_iota(jnp.int32, (rows, new_rows), 1)
        query_ids = lax.broadcasted_iota(jnp.int32, (rows, new_rows), 0)
        visit(kn_ref, vn_ref, key_ids <= query_ids, True)


def self_attention(queries, new_keys, new_values, keys, values, length):
    rows, width = queries.shape
    new_rows, capacity = new_keys.shape[0], keys.shape[0]
    block_rows = min(CACHE_BLOCK, capacity)
    heads = width // HD
    whole = pl.BlockSpec((rows, width), lambda i, n: (0, 0))
    new = pl.BlockSpec((new_rows, width), lambda i, n: (0, 0))
    cached = pl.BlockSpec(
        (block_rows, width), lambda i, n: (jnp.minimum(i, (n[0] - 1) // block_rows), 0)
    )
    return pl.pallas_call(
        functools.partial(self_kernel, block_rows, heads),
        grid_spec=pltpu.PrefetchScalarGridSpec(
            num_scalar_prefetch=1,
            grid=(capacity // block_rows + 1,),
            in_specs=[whole, new, new, cached, cached],
            out_specs=whole,
            scratch_shapes=[
                pltpu.VMEM((heads, rows, HD), jnp.float32),
                pltpu.VMEM((heads, rows, 2 * HD), jnp.float32),
            ],
        ),
        out_shape=jax.ShapeDtypeStruct((rows, width), jnp.bfloat16),
        compiler_params=pltpu.CompilerParams(vmem_limit_bytes=VMEM_LIMIT),
        cost_estimate=cost_of(20e-6),
        name="self_attention",
    )(length.reshape(1), queries, new_keys, new_values, keys, values)


def cross_kernel(heads, pieces_count, spans, prompts_ref, side_ref, q_ref, near_ref, *refs):
    pieces, (own_ref, other_ref) = refs[:pieces_count], refs[pieces_count:]
    rows = q_ref.shape[0]
    width = heads * HD
    first = pl.multiple_of(side_ref[0] * width, HD)
    asked = 2 * spans[0] * spans[1]
    for part in range(2):
        prompt = prompts_ref[part]
        target = other_ref if part else own_ref

        def gathered(kind, head, prompt=prompt):
            cols = slice(head * HD, (head + 1) * HD)
            count, text_rows = spans
            at = pl.ds(pl.multiple_of((kind * count + prompt) * text_rows, text_rows), text_rows)
            return jnp.concatenate([piece[at, cols] for piece in pieces], axis=0)

        def scores_of(head, part=part, gathered=gathered):
            if part == 0:
                queries = q_ref[:, pl.ds(pl.multiple_of(first + head * HD, HD), HD)]
            else:
                queries = near_ref[asked : asked + rows, head * HD : (head + 1) * HD]
            return score(queries, gathered(0, head))

        def use(head, scores, target=target, gathered=gathered):
            _, total = absorb(scores, gathered(1, head), empty_state(rows), None)
            target[:, head * HD : (head + 1) * HD] = finished(total)

        visit_heads(heads, scores_of, use)


def cross_attention(prompts, side, queries, near, pieces, spans):
    rows, width = queries.shape
    half = width // 2
    scalars = pl.BlockSpec(memory_space=pltpu.SMEM)
    vmem = pl.BlockSpec(memory_space=pltpu.VMEM)
    return pl.pallas_call(
        functools.partial(cross_kernel, half // HD, len(pieces), spans),
        in_specs=[scalars, scalars] + [vmem] * (2 + len(pieces)),
        out_specs=[vmem, vmem],
        out_shape=[jax.ShapeDtypeStruct((rows, half), jnp.bfloat16)] * 2,
        compiler_params=pltpu.CompilerParams(vmem_limit_bytes=VMEM_LIMIT),
        cost_estimate=cost_of(0),
        name="cross_attention",
    )(prompts, side.reshape(1), queries, near, *pieces)


def prompts_kernel(prompt_ref, tag_ref, *refs):
    refs[-1][0] = prompt_ref[0]
    refs[-1][1] = jnp.max(tag_ref[...].astype(jnp.float32)).astype(jnp.int32)


def read_prompts(prompt_of, asked, gates):
    rows, half = asked.shape
    scalars = pl.BlockSpec(memory_space=pltpu.SMEM)
    return pl.pallas_call(
        prompts_kernel,
        grid=(1,),
        in_specs=[scalars, pl.BlockSpec((TAG_ROWS, half), lambda i: (rows // TAG_ROWS - 1, 0))]
        + [pl.BlockSpec(memory_space=pl.ANY)] * len(gates),
        out_specs=scalars,
        out_shape=jax.ShapeDtypeStruct((2,), jnp.int32),
        cost_estimate=cost_of(100e-6),
        name="read_prompts",
    )(prompt_of, asked, *gates)


def pack_kernel(side_ref, prompt_ref, k_ref, v_ref, q_ref, keep_ref, give_ref, ask_ref):
    half = keep_ref.shape[1]
    prompts, text_rows, _ = k_ref.shape
    kept = pl.ds(pl.multiple_of(side_ref[0] * half, HD), half)
    given = pl.ds(pl.multiple_of((1 - side_ref[0]) * half, HD), half)
    for part, source in enumerate((k_ref, v_ref)):
        for prompt in range(prompts):
            first = (part * prompts + prompt) * text_rows
            at = slice(first, first + text_rows)
            keep_ref[at, :] = source[prompt, :, kept]
            give_ref[at, :] = source[prompt, :, given]
            ask_ref[at, :] = source[prompt, :, given]
    first, rows = give_ref.shape[0], q_ref.shape[0]
    ask_ref[first : first + rows, :] = q_ref[:, given]
    tag = jnp.full((TAG_ROWS, half), prompt_ref[0], jnp.int32)
    ask_ref[first + rows :, :] = tag.astype(jnp.float32).astype(ask_ref.dtype)


def pack(side, prompt_of, text_k, text_v, queries):
    prompts, text_rows, width = text_k.shape
    rows, half = queries.shape[0], width // 2
    text = jax.ShapeDtypeStruct((2 * prompts * text_rows, half), text_k.dtype)
    ask = jax.ShapeDtypeStruct((text.shape[0] + rows + TAG_ROWS, half), queries.dtype)
    scalars = pl.BlockSpec(memory_space=pltpu.SMEM)
    vmem = pl.BlockSpec(memory_space=pltpu.VMEM)
    return pl.pallas_call(
        pack_kernel,
        in_specs=[scalars, scalars, vmem, vmem, vmem],
        out_specs=[vmem] * 3,
        out_shape=[text, text, ask],
        compiler_params=pltpu.CompilerParams(vmem_limit_bytes=VMEM_LIMIT),
        cost_estimate=cost_of(3e-6),
        name="pack",
    )(side.reshape(1), prompt_of, text_k, text_v, queries)


def whole_cross_kernel(heads, q_ref, k_ref, v_ref, o_ref):
    def scores_of(head):
        cols = slice(head * HD, (head + 1) * HD)
        return score(q_ref[:, cols], k_ref[:, cols])

    def use(head, scores):
        cols = slice(head * HD, (head + 1) * HD)
        _, total = absorb(scores, v_ref[:, cols], empty_state(q_ref.shape[0]), None)
        o_ref[:, cols] = finished(total)

    visit_heads(heads, scores_of, use)


def whole_cross(queries, prompt_of, text_k, text_v):
    keys, values = (
        lax.dynamic_index_in_dim(
            lax.all_gather(text, "req", axis=1, tiled=True), prompt_of[0], 0, keepdims=False
        )
        for text in (text_k, text_v)
    )
    return pl.pallas_call(
        functools.partial(whole_cross_kernel, queries.shape[1] // HD),
        out_shape=jax.ShapeDtypeStruct(queries.shape, jnp.bfloat16),
        compiler_params=pltpu.CompilerParams(vmem_limit_bytes=VMEM_LIMIT),
        name="whole_cross",
    )(queries, keys, values)


def project_kernel(count, span, places, place_ref, own_ref, near_ref, *refs):
    held, passed = refs[:count], refs[count : 2 * count]
    outs = refs[2 * count : 2 * count + places]
    x_ref, weights, terms, x_sems, sems, out_sems = refs[2 * count + places :]
    chip, holder, at_tp = place_ref[0], place_ref[1], place_ref[2]
    rows, columns = own_ref.shape[0], held[0].shape[1]
    blocks = outs[0].shape[1]

    def rows_in(part):
        source = (near_ref, own_ref)[part]
        return pltpu.make_async_copy(
            source, x_ref.at[part * rows : (part + 1) * rows], x_sems.at[part]
        )

    def weights_in(choice, at):
        first = (at % span) * columns
        place = weights.at[at // span, :, first : first + columns]
        return pltpu.make_async_copy(choice[at], place, sems.at[at])

    def terms_out(at, distance, block):
        return pltpu.make_async_copy(terms.at[at], outs[distance].at[:, block], out_sems.at[at])

    for part in range(2):
        rows_in(part).start()

    @pl.when(holder == 1)
    def _():
        for at in range(count):
            weights_in(held, at).start()

    @pl.when(holder == 0)
    def _():
        for at in range(count):
            weights_in(passed, at).start()

    for part in range(2):
        rows_in(part).wait()
    for first in range(0, count, span):
        for at in range(first, first + span):
            weights_in(held, at).wait()
        product = jnp.dot(
            x_ref[...], weights[first // span], preferred_element_type=jnp.float32
        ).astype(terms.dtype)
        for at in range(first, first + span):
            cols = slice((at - first) * columns, (at - first + 1) * columns)
            source = chip ^ at
            block = lax.rem(source, blocks)
            away = lax.div(source, blocks) ^ at_tp
            for part in range(2):
                terms[at, part] = product[part * rows : (part + 1) * rows, cols]
            for distance in range(places):

                @pl.when(away == distance)
                def _(at=at, distance=distance, block=block):
                    terms_out(at, distance, block).start()

    for at in range(count):
        terms_out(at, 0, 0).wait()


def project(tps, place, own, near, held, passed):
    rows = own.shape[0]
    depth, columns = held[0].shape
    count = len(held)
    span = 2 if columns % HD == 0 else 1
    hbm = pl.BlockSpec(memory_space=pl.ANY)
    out = jax.ShapeDtypeStruct((2, count // tps, rows, columns), jnp.bfloat16)
    return pl.pallas_call(
        functools.partial(project_kernel, count, span, tps),
        in_specs=[pl.BlockSpec(memory_space=pltpu.SMEM)] + [hbm] * (2 + 2 * count),
        out_specs=[hbm] * tps,
        out_shape=[out] * tps,
        scratch_shapes=[
            pltpu.VMEM((2 * rows, depth), jnp.bfloat16),
            pltpu.VMEM((count // span, depth, span * columns), jnp.bfloat16),
            pltpu.VMEM((count, 2, rows, columns), jnp.bfloat16),
            pltpu.SemaphoreType.DMA((2,)),
            pltpu.SemaphoreType.DMA((count,)),
            pltpu.SemaphoreType.DMA((count,)),
        ],
        compiler_params=pltpu.CompilerParams(vmem_limit_bytes=VMEM_LIMIT),
        cost_estimate=cost_of(10e-6),
        name="project",
    )(place, own, near, *held, *passed)


def add_kernel(count, *refs):
    outs, (scratch, sems) = refs[count:-2], refs[-2:]
    copies = [
        pltpu.make_async_copy(refs[at], scratch.at[at], sems.at[at]) for at in range(count)
    ]
    for copy in copies:
        copy.start()
    for copy in copies:
        copy.wait()
    total = scratch[0].astype(jnp.float32)
    for at in range(1, count):
        total += scratch[at].astype(jnp.float32)
    total = total.astype(scratch.dtype)
    if len(outs) == 1:
        outs[0][...] = total
    else:
        for at, out in enumerate(outs):
            out[...] = total[at]


def add(*terms, parted=True):
    hbm = pl.BlockSpec(memory_space=pl.ANY)
    vmem = pl.BlockSpec(memory_space=pltpu.VMEM)
    shape, dtype = terms[0].shape, terms[0].dtype
    return pl.pallas_call(
        functools.partial(add_kernel, len(terms)),
        in_specs=[hbm] * len(terms),
        out_specs=[vmem] * shape[0] if parted else vmem,
        out_shape=(
            [jax.ShapeDtypeStruct(shape[1:], dtype)] * shape[0]
            if parted
            else jax.ShapeDtypeStruct(shape, dtype)
        ),
        scratch_shapes=[
            pltpu.VMEM((len(terms),) + shape, dtype),
            pltpu.SemaphoreType.DMA((len(terms),)),
        ],
        compiler_params=pltpu.CompilerParams(vmem_limit_bytes=VMEM_LIMIT),
        cost_estimate=cost_of(2e-6),
        name="add",
    )(*terms)


def to_tp(value, pairs):
    return lax.ppermute(value, "tp", pairs)


def apart(tps, distance):
    return [(i, i ^ distance) for i in range(tps)]


def after(value, *others):
    return lax.optimization_barrier((value, *others))[0]


def per_device(
    reqs,
    tps,
    hidden,
    q_new,
    k_new,
    v_new,
    cache_k,
    cache_v,
    cache_len,
    w_out,
    q_cross,
    text_k,
    text_v,
    prompt_of,
):
    rows, width = q_new.shape
    chips = reqs // 2
    place = lax.axis_index("req")
    chip, core = place // 2, place % 2
    side = chip % 2
    text_side = (chip // 2) % 2
    holder = core == side
    length = lax.dynamic_index_in_dim(cache_len, place, 0, keepdims=False)

    def swap(array, distance):
        return lax.ppermute(array, "req", [(i, i ^ distance) for i in range(reqs)])

    first_of = [2 * i + i % 2 for i in range(chips)]
    second_of = [2 * i + 1 - i % 2 for i in range(chips)]
    beside = lax.ppermute(
        w_out,
        "req",
        [(first_of[i], first_of[i ^ 2]) for i in range(chips)]
        + [(second_of[i], second_of[i ^ 1]) for i in range(chips)],
    )
    own_passed = lax.ppermute(w_out, "req", list(zip(first_of, second_of)))

    own = self_attention(q_new, k_new, v_new, cache_k[0], cache_v[0], length)
    near = swap(own, 2)
    beside = after(beside, own)
    across = lax.ppermute(
        beside, "req", [(second_of[i], second_of[i ^ 2]) for i in range(chips)]
    )
    beside_passed = swap(beside, 1)
    split_heads = (width // HD) % 2 == 0
    if split_heads:
        keep, give, ask = pack(text_side, prompt_of, text_k, text_v, after(q_cross, own))
        across = after(across, keep)
        give, keep, ask = after((give, keep, ask), near)
        asked = swap(ask, 4)
        if chips == 4:
            pieces = [keep, asked, swap(keep, 2), swap(give, 6)]
        else:
            pieces = [keep, asked[: give.shape[0]]]
            for bit in range(chips.bit_length() - 1):
                if bit != 1:
                    pieces += [swap(piece, 2 << bit) for piece in pieces]
        spans = text_k.shape[:2]
        prompts = read_prompts(prompt_of, asked, pieces[2:])

    across_passed = lax.ppermute(after(across, near), "req", list(zip(second_of, first_of)))
    held = [w_out, beside_passed, beside, across_passed]
    passed = [own_passed, beside, beside_passed, across]
    bit = 4
    while bit < chips:
        held += [swap(block, 2 * bit) for block in held]
        passed += [swap(block, 2 * bit) for block in passed]
        bit *= 2
    at = lax.axis_index("tp")
    order = jnp.stack([chip, holder, at]).astype(jnp.int32)

    terms = project(tps, order, own, near, held, passed)

    if split_heads and tps == 4 and chips == 4:
        far = to_tp(terms[3], [(0, 1), (3, 2)])
        inner = to_tp(terms[3], [(1, 2), (2, 1)])
        joined = add(terms[2], after(far, inner, prompts), parted=False)
        crossing = to_tp(joined, apart(4, 2))
        outer, pieces = after((terms[1], pieces), joined)
        outer = to_tp(outer, apart(4, 1))
        pieces += [swap(piece, 1) for piece in pieces]
        mine, others = cross_attention(prompts, text_side, q_cross, asked, pieces, spans)
        outer, crossing = after((outer, crossing), mine)
        given, kept = add(terms[0], inner, outer, crossing)
    else:
        given, kept = add(terms[0], *[to_tp(terms[d], apart(tps, d)) for d in range(1, tps)])
        if split_heads:
            pieces += [swap(piece, 1) for piece in pieces]
            mine, others = cross_attention(prompts, text_side, q_cross, asked, pieces, spans)

    def in_order(side, kept, received, axis):
        return jnp.where(
            side == 0,
            jnp.concatenate([kept, received], axis=axis),
            jnp.concatenate([received, kept], axis=axis),
        )

    if split_heads:
        cross_heads = in_order(text_side, mine, swap(others, 4), 1)
    else:
        cross_heads = whole_cross(q_cross, prompt_of, text_k, text_v)

    ordered = in_order(side, kept, swap(given, 2), 2).transpose(1, 0, 2).reshape(rows, width)
    hidden_out = (hidden.astype(jnp.float32) + ordered.astype(jnp.float32)).astype(jnp.bfloat16)
    return (hidden_out, cross_heads)


def solution(mesh):
    placed = (
        P("req", "tp"),
        P("req", "tp"),
        P("req", "tp"),
        P("req", "tp"),
        P("req", None, "tp"),
        P("req", None, "tp"),
        P(),
        P("tp", "req"),
        P("req", "tp"),
        P(None, "req", "tp"),
        P(None, "req", "tp"),
        P("req"),
    )
    return jax.shard_map(
        functools.partial(per_device, mesh.shape["req"], mesh.shape["tp"]),
        mesh=mesh,
        in_specs=placed,
        out_specs=(P("req", "tp"), P("req", "tp")),
        check_vma=False,
    )
```

time: 161 us -> 140 us (0.87)
  waiting for transfers between devices: 73.2 us -> 55.6 us
  between operations: 15.5 us -> 1.47 us
  starting transfers between devices: 31 us -> 36.1 us
  Pallas kernels: 32 us -> 35.4 us
    ppermute x13 -> x11, waiting for transfers between devices: 61.8 us -> 27 us  [swap(): return lax.ppermute(array, 'req', [(i, i ^ distance) for i in range(reqs)])]
    ppermute x1 -> x5, waiting for transfers between devices: 0.01 us -> 20.6 us  [the longest x4 20.6 us: to_tp(): return lax.ppermute(value, 'tp', pairs)]
    ppermute x1 -> x5, starting transfers between devices: 1.47 us -> 13.4 us  [the longest x4 11.9 us: to_tp(): return lax.ppermute(value, 'tp', pairs)]
    ppermute x13 -> x11, starting transfers between devices: 20.1 us -> 15.3 us  [swap(): return lax.ppermute(array, 'req', [(i, i ^ distance) for i in range(reqs)])]
    ppermute x1, waiting for transfers between devices: 11.4 us -> 8.02 us  [per_device(): lax.ppermute(w_out, 'req', [(first_of[i], first_of[i ^ 2]) for i in range...]
    pallas_call x4 -> x6, Pallas kernels: 29.2 us -> 32.2 us  [the longest x1 10.2 us: self_attention(): pl.pallas_call(functools.partial(self_kernel, block_rows, heads), grid_sp...]
    unnamed x22 -> x34, local copies, waits for them, and re-layouts: 2.4 us -> 5.08 us
    ppermute x1, starting transfers between devices: 4.48 us -> 2.47 us  [per_device(): own_passed = lax.ppermute(w_out, 'req', list(zip(first_of, second_of)))]
  transfers between devices with their start and end apart: 18 -> 19, of which waited for: 8 -> 8; matrix products, arithmetic and copies ran while one was open for 3% -> 3% of each run, Pallas kernels for 14% -> 22%
where the time goes in v4:
time: 140 us; the launch traced here: 139 us
  waiting for transfers between devices  55.6 us (40%)
  starting transfers between devices  36.1 us (26%)
  Pallas kernels  35.4 us (25%)
  local copies, waits for them, and re-layouts  6.32 us (5%)
  other arithmetic  3.78 us (3%)
  between operations  1.47 us (1%)
    ppermute x11, waiting for transfers between devices, swap(): return lax.ppermute(array, 'req', [(i, i ^ distance) for i in range(reqs)])  27 us
    ppermute x4, waiting for transfers between devices, to_tp(): return lax.ppermute(value, 'tp', pairs)  20.6 us
    ppermute x11, starting transfers between devices, swap(): return lax.ppermute(array, 'req', [(i, i ^ distance) for i in range(reqs)])  15.3 us
    ppermute x4, starting transfers between devices, to_tp(): return lax.ppermute(value, 'tp', pairs)  11.9 us
    pallas_call x1, Pallas kernels, self_attention(): pl.pallas_call(functools.partial(self_kernel, block_rows, heads), grid_sp...  10.2 us
    pallas_call x1, Pallas kernels, project(): pl.pallas_call(functools.partial(project_kernel, count, span, tps), in_sp...  9.29 us
    ppermute x1, waiting for transfers between devices, per_device(): lax.ppermute(w_out, 'req', [(first_of[i], first_of[i ^ 2]) for i in range...  8.02 us
    pallas_call x1, Pallas kernels, cross_attention(): pl.pallas_call(functools.partial(cross_kernel, half // HD, len(pieces), s...  6.12 us
  transfers between devices with their start and end apart: 19, of which 8 were waited for; matrix products, arithmetic and copies ran while one was open for 3% of the time, Pallas kernels for 22%

profile of v4, /device:TPU:0, one launch (start us, length us, event | category | flops | bytes accessed | tf_op | source)
XLA Modules:
  0.0 138.6 jit_solution(1918259559837530708)
XLA Ops:
  0.6 3.0 %collective-permute-start.1 = (bf16[1280,640]{1,0:T(8,128)(2,1)}, bf16[1280,640]{1,0:T(8,128)(2,1)}, u32[]{:S(2)}, u32[]{:S(2)}) collective-permute-start(bf16[1280,640]{1,0:T(8,128)(2,1)} %refs_0_.1), channel_id=1, source_target_pairs={{0,16},{12,28},{16,0},{28,12},{4,8},{8,4},{20,24},{24,20},{1,17},{... | collective-permute-start | bytes 4915208 | tf_op jit(solution)/shard_map/ppermute | solution.py:440
  4.9 10.2 %self_attention.1.own_ref = bf16[256,1280]{1,0:T(8,128)(2,1)} custom-call(s32[1]{0:T(128)} %dynamic_slice.4.length_ref, bf16[256,1280]{1,0:T(8,128)(2,1)} %q_ref.2, bf16[256,1280]{1,0:T(8,128)(2,1)} %kn_ref.1, bf16[256,1280]{1,0:T(8,128)(2,1)} %vn_ref.1, bf16[4096,1280]{1,0:T(8,128)(2,1)} %bitcast.10, bf16[4096,1280]{1,0:T(8,128)(2,1)} %bitcast.11), custom_call_target="tpu_custom_call" | custom-call | flops 23069999104 | tf_op jit(solution)/shard_map/self_attention/pallas_call | solution.py:120
  15.1 8.0 %collective-permute-done.1.refs_2_.refs_5_ = bf16[1280,640]{1,0:T(8,128)(2,1)} collective-permute-done((bf16[1280,640]{1,0:T(8,128)(2,1)}, bf16[1280,640]{1,0:T(8,128)(2,1)}, u32[]{:S(2)}, u32[]{:S(2)}) %collective-permute-start.1) | collective-permute-done | bytes 1638432 | tf_op jit(solution)/shard_map/ppermute | solution.py:440
  23.1 1.8 %collective-permute-start.3 = (bf16[1280,640]{1,0:T(8,128)(2,1)}, bf16[1280,640]{1,0:T(8,128)(2,1)}, u32[]{:S(2)}, u32[]{:S(2)}) collective-permute-start(bf16[1280,640]{1,0:T(8,128)(2,1)} %collective-permute-done.1.refs_2_.refs_5_), channel_id=1, source_target_pairs={{4,20},{8,24},{20,4},{24,8},{5,21},{9,25},{21,5},{25,9},{6,22},{10... | collective-permute-start | bytes 4915208 | tf_op jit(solution)/shard_map/ppermute | solution.py:451
  24.9 3.1 %collective-permute-start = (bf16[256,1280]{1,0:T(8,128)(2,1)}, bf16[256,1280]{1,0:T(8,128)(2,1)S(1)}, u32[]{:S(2)}, u32[]{:S(2)}) collective-permute-start(bf16[256,1280]{1,0:T(8,128)(2,1)} %self_attention.1.own_ref), channel_id=1, source_target_pairs={{0,8},{4,12},{8,0},{12,4},{16,24},{20,28},{24,16},{28,20},{1,9},{5... | collective-permute-start | bytes 1966088 | tf_op jit(solution)/shard_map/ppermute | solution.py:436
  28.0 2.5 %collective-permute-start.5 = (bf16[1280,640]{1,0:T(8,128)(2,1)}, bf16[1280,640]{1,0:T(8,128)(2,1)}, u32[]{:S(2)}, u32[]{:S(2)}) collective-permute-start(bf16[1280,640]{1,0:T(8,128)(2,1)} %refs_0_.1), channel_id=1, source_target_pairs={{0,4},{12,8},{16,20},{28,24},{1,5},{13,9},{17,21},{29,25},{2,6},{1... | collective-permute-start | bytes 4915208 | tf_op jit(solution)/shard_map/ppermute | solution.py:446
  31.1 3.1 %pack.1 = (bf16[512,640]{1,0:T(8,128)(2,1)}, bf16[512,640]{1,0:T(8,128)(2,1)}, bf16[784,640]{1,0:T(8,128)(2,1)}) custom-call(s32[1]{0:T(128)} %bitcast.5.side_ref, s32[1]{0:T(128)S(6)} %copy.14.prompt_ref, bf16[4,64,1280]{2,1,0:T(8,128)(2,1)} %k_ref.1, bf16[4,64,1280]{2,1,0:T(8,128)(2,1)} %v_ref.1, bf16[256,1280]{1,0:T(8,128)(2,1)} %q_ref.4), custom_call_target="tpu_custom_call" | custom-call | flops 3460499968 | tf_op jit(solution)/shard_map/pack/pallas_call | solution.py:230
  34.3 9.0 %collective-permute-done.near_ref = bf16[256,1280]{1,0:T(8,128)(2,1)S(1)} collective-permute-done((bf16[256,1280]{1,0:T(8,128)(2,1)}, bf16[256,1280]{1,0:T(8,128)(2,1)S(1)}, u32[]{:S(2)}, u32[]{:S(2)}) %collective-permute-start) | collective-permute-done | bytes 655392 | tf_op jit(solution)/shard_map/ppermute | solution.py:436
  43.2 1.5 %collective-permute-start.4 = (bf16[1280,640]{1,0:T(8,128)(2,1)}, bf16[1280,640]{1,0:T(8,128)(2,1)}, u32[]{:S(2)}, u32[]{:S(2)}) collective-permute-start(bf16[1280,640]{1,0:T(8,128)(2,1)} %collective-permute-done.3.refs_7_), channel_id=1, source_target_pairs={{4,0},{8,12},{20,16},{24,28},{5,1},{9,13},{21,17},{25,29},{6,2},{1... | collective-permute-start | bytes 4915208 | tf_op jit(solution)/shard_map/ppermute | solution.py:471
  45.9 8.1 %collective-permute-start.8 = (bf16[512,640]{1,0:T(8,128)(2,1)}, bf16[512,640]{1,0:T(8,128)(2,1)S(1)}, u32[]{:S(2)}, u32[]{:S(2)}) collective-permute-start(bf16[512,640]{1,0:T(8,128)(2,1)} %get-tuple-element.44.refs_0_), channel_id=1, source_target_pairs={{0,8},{4,12},{8,0},{12,4},{16,24},{20,28},{24,16},{28,20},{1,9},{5... | collective-permute-start | bytes 1966088 | tf_op jit(solution)/shard_map/ppermute | solution.py:436
  54.3 9.3 %project.1 = (bf16[2,1,256,640]{3,2,1,0:T(8,128)(2,1)}, bf16[2,1,256,640]{3,2,1,0:T(8,128)(2,1)}, bf16[2,1,256,640]{3,2,1,0:T(8,128)(2,1)}, bf16[2,1,256,640]{3,2,1,0:T(8,128)(2,1)}) custom-call(s32[3]{0:T(128)} %pad_add_fusion.place_ref, bf16[256,1280]{1,0:T(8,128)(2,1)} %self_attention.1.own_ref, bf16[256,1280]{1,0:T(8,128)(2,1)} %copy-done.13, ...), custom_call_target="tpu_custom_call" | custom-call | flops 11534999552 | tf_op jit(solution)/shard_map/project/pallas_call | solution.py:336
  64.3 7.1 %collective-permute-start.10 = (bf16[2,1,256,640]{3,2,1,0:T(8,128)(2,1)}, bf16[2,1,256,640]{3,2,1,0:T(8,128)(2,1)}, u32[]{:S(2)}, u32[]{:S(2)}) collective-permute-start(bf16[2,1,256,640]{3,2,1,0:T(8,128)(2,1)} %get-tuple-element.34), channel_id=1, source_target_pairs={{0,1},{3,2},{4,5},{7,6},{8,9},{11,10},{12,13},{15,14},{16,17},{19,... | collective-permute-start | bytes 1966088 | tf_op jit(solution)/shard_map/ppermute | solution.py:399
  71.3 9.3 %collective-permute-done.9.refs_1_.refs_3_ = bf16[512,640]{1,0:T(8,128)(2,1)S(1)} collective-permute-done((bf16[512,640]{1,0:T(8,128)(2,1)}, bf16[512,640]{1,0:T(8,128)(2,1)S(1)}, u32[]{:S(2)}, u32[]{:S(2)}) %collective-permute-start.9) | collective-permute-done | bytes 655392 | tf_op jit(solution)/shard_map/ppermute | solution.py:436
  80.7 1.7 %collective-permute-done.7.tag_ref.near_ref.refs_1_ = bf16[784,640]{1,0:T(8,128)(2,1)S(1)} collective-permute-done((bf16[784,640]{1,0:T(8,128)(2,1)}, bf16[784,640]{1,0:T(8,128)(2,1)S(1)}, u32[]{:S(2)}, u32[]{:S(2)}) %collective-permute-start.7) | collective-permute-done | bytes 1003552 | tf_op jit(solution)/shard_map/ppermute | solution.py:436
  85.6 2.4 %add.31 = bf16[2,1,256,640]{3,2,1,0:T(8,128)(2,1)} custom-call(bf16[2,1,256,640]{3,2,1,0:T(8,128)(2,1)} %get-tuple-element.41.refs_0_, bf16[2,1,256,640]{3,2,1,0:T(8,128)(2,1)} %collective-permute-done.10.refs_1_), custom_call_target="tpu_custom_call" | custom-call | flops 2307000064 | tf_op jit(solution)/shard_map/add/pallas_call | solution.py:379
  88.1 2.1 %collective-permute-start.13 = (bf16[512,640]{1,0:T(8,128)(2,1)S(1)}, bf16[512,640]{1,0:T(8,128)(2,1)S(1)}, u32[]{:S(2)}, u32[]{:S(2)}) collective-permute-start(bf16[512,640]{1,0:T(8,128)(2,1)S(1)} %copy-done.4), channel_id=1, source_target_pairs={{0,4},{4,0},{8,12},{12,8},{16,20},{20,16},{24,28},{28,24},{1,5},{5... | collective-permute-start | bytes 1966088 | tf_op jit(solution)/shard_map/ppermute | solution.py:436
  90.8 1.6 %collective-permute-start.11 = (bf16[2,1,256,640]{3,2,1,0:T(8,128)(2,1)}, bf16[2,1,256,640]{3,2,1,0:T(8,128)(2,1)}, u32[]{:S(2)}, u32[]{:S(2)}) collective-permute-start(bf16[2,1,256,640]{3,2,1,0:T(8,128)(2,1)} %get-tuple-element.43), channel_id=1, source_target_pairs={{0,1},{1,0},{2,3},{3,2},{4,5},{5,4},{6,7},{7,6},{8,9},{9,8},{10,11... | collective-permute-start | bytes 1966088 | tf_op jit(solution)/shard_map/ppermute | solution.py:399
  92.4 2.6 %collective-permute-start.12 = (bf16[2,1,256,640]{3,2,1,0:T(8,128)(2,1)}, bf16[2,1,256,640]{3,2,1,0:T(8,128)(2,1)S(1)}, u32[]{:S(2)}, u32[]{:S(2)}) collective-permute-start(bf16[2,1,256,640]{3,2,1,0:T(8,128)(2,1)} %add.31), channel_id=1, source_target_pairs={{0,2},{1,3},{2,0},{3,1},{4,6},{5,7},{6,4},{7,5},{8,10},{9,11},{10,... | collective-permute-start | bytes 1966088 | tf_op jit(solution)/shard_map/ppermute | solution.py:399
  97.7 6.1 %cross_attention.1 = (bf16[256,640]{1,0:T(8,128)(2,1)}, bf16[256,640]{1,0:T(8,128)(2,1)}) custom-call(s32[2]{0:T(128)} %read_prompts.1.prompts_ref, s32[1]{0:T(128)} %bitcast.5.side_ref, bf16[256,1280]{1,0:T(8,128)(2,1)} %q_ref.4, bf16[784,640]{1,0:T(8,128)(2,1)} %copy-done, bf16[512,640]{1,0:T(8,128)(2,1)} %get-tuple-element.44.refs_0_, ...), custom_call_target="tpu_custom_call" | custom-call | tf_op jit(solution)/shard_map/cross_attention/pallas_call | solution.py:174
  103.8 18.3 %collective-permute-done.11.refs_2_ = bf16[2,1,256,640]{3,2,1,0:T(8,128)(2,1)} collective-permute-done((bf16[2,1,256,640]{3,2,1,0:T(8,128)(2,1)}, bf16[2,1,256,640]{3,2,1,0:T(8,128)(2,1)}, u32[]{:S(2)}, u32[]{:S(2)}) %collective-permute-start.11) | collective-permute-done | bytes 655392 | tf_op jit(solution)/shard_map/ppermute | solution.py:399
  122.1 2.3 %collective-permute-done.12.refs_3_ = bf16[2,1,256,640]{3,2,1,0:T(8,128)(2,1)S(1)} collective-permute-done((bf16[2,1,256,640]{3,2,1,0:T(8,128)(2,1)}, bf16[2,1,256,640]{3,2,1,0:T(8,128)(2,1)S(1)}, u32[]{:S(2)}, u32[]{:S(2)}) %collective-permute-start.12) | collective-permute-done | bytes 655392 | tf_op jit(solution)/shard_map/ppermute | solution.py:399
  125.2 2.9 %add.32 = (bf16[1,256,640]{2,1,0:T(8,128)(2,1)}, bf16[1,256,640]{2,1,0:T(8,128)(2,1)}) custom-call(bf16[2,1,256,640]{3,2,1,0:T(8,128)(2,1)} %get-tuple-element.33.refs_0_, bf16[2,1,256,640]{3,2,1,0:T(8,128)(2,1)} %copy-done.14, bf16[2,1,256,640]{3,2,1,0:T(8,128)(2,1)} %collective-permute-done.11.refs_2_, bf16[2,1,256,640]{3,2,1,0:T(8,128)(2,1)} %copy-done.15), custom_call_target="tpu_custom_call" | custom-call | flops 2307000064 | tf_op jit(solution)/shard_map/add/pallas_call | solution.py:379
  128.8 6.7 %collective-permute-done.17 = bf16[1,256,640]{2,1,0:T(8,128)(2,1)S(1)} collective-permute-done((bf16[1,256,640]{2,1,0:T(8,128)(2,1)}, bf16[1,256,640]{2,1,0:T(8,128)(2,1)S(1)}, u32[]{:S(2)}, u32[]{:S(2)}) %collective-permute-start.17) | collective-permute-done | bytes 327712 | tf_op jit(solution)/shard_map/ppermute | solution.py:436
  135.5 2.1 %add_convert_fusion = bf16[256,1280]{1,0:T(8,128)(2,1)} fusion(bf16[256,1280]{1,0:T(8,128)(2,1)S(1)} %copy-done.3, bf16[256,640]{1,0:T(8,128)(2,1)S(1)} %bitcast.9, bf16[256,640]{1,0:T(8,128)(2,1)} %bitcast.8, pred[]{:T(512)S(6)} %eq.13), kind=kLoop, calls=%fused_computation | loop fusion | flops 4259840 | bytes 1966081 | tf_op jit(solution)/shard_map/convert_element_type | solution.py:514
  (59 shorter events, 12.3 us)
Async XLA Ops:
  0.6 22.4 %collective-permute-start.1 = (bf16[1280,640]{1,0:T(8,128)(2,1)}, bf16[1280,640]{1,0:T(8,128)(2,1)}, u32[]{:S(2)}, u32[]{:S(2)}) collective-permute-start(bf16[1280,640]{1,0:T(8,128)(2,1)} %refs_0_.1), channel_id=1, source_target_pairs={{0,16},{12,28},{16,0},{28,12},{4,8},{8,4},{20,24},{24,20},{1,17},{... | collective-permute-start | bytes 4915208 | tf_op jit(solution)/shard_map/ppermute | solution.py:440
  23.1 11.2 %collective-permute-start.3 = (bf16[1280,640]{1,0:T(8,128)(2,1)}, bf16[1280,640]{1,0:T(8,128)(2,1)}, u32[]{:S(2)}, u32[]{:S(2)}) collective-permute-start(bf16[1280,640]{1,0:T(8,128)(2,1)} %collective-permute-done.1.refs_2_.refs_5_), channel_id=1, source_target_pairs={{4,20},{8,24},{20,4},{24,8},{5,21},{9,25},{21,5},{25,9},{6,22},{10... | collective-permute-start | bytes 4915208 | tf_op jit(solution)/shard_map/ppermute | solution.py:451
  24.9 18.3 %collective-permute-start = (bf16[256,1280]{1,0:T(8,128)(2,1)}, bf16[256,1280]{1,0:T(8,128)(2,1)S(1)}, u32[]{:S(2)}, u32[]{:S(2)}) collective-permute-start(bf16[256,1280]{1,0:T(8,128)(2,1)} %self_attention.1.own_ref), channel_id=1, source_target_pairs={{0,8},{4,12},{8,0},{12,4},{16,24},{20,28},{24,16},{28,20},{1,9},{5... | collective-permute-start | bytes 1966088 | tf_op jit(solution)/shard_map/ppermute | solution.py:436
  28.0 26.0 %collective-permute-start.5 = (bf16[1280,640]{1,0:T(8,128)(2,1)}, bf16[1280,640]{1,0:T(8,128)(2,1)}, u32[]{:S(2)}, u32[]{:S(2)}) collective-permute-start(bf16[1280,640]{1,0:T(8,128)(2,1)} %refs_0_.1), channel_id=1, source_target_pairs={{0,4},{12,8},{16,20},{28,24},{1,5},{13,9},{17,21},{29,25},{2,6},{1... | collective-permute-start | bytes 4915208 | tf_op jit(solution)/shard_map/ppermute | solution.py:446
  34.3 20.0 %collective-permute-start.2 = (bf16[1280,640]{1,0:T(8,128)(2,1)}, bf16[1280,640]{1,0:T(8,128)(2,1)}, u32[]{:S(2)}, u32[]{:S(2)}) collective-permute-start(bf16[1280,640]{1,0:T(8,128)(2,1)} %collective-permute-done.1.refs_2_.refs_5_), channel_id=1, source_target_pairs={{0,4},{4,0},{8,12},{12,8},{16,20},{20,16},{24,28},{28,24},{1,5},{5... | collective-permute-start | bytes 4915208 | tf_op jit(solution)/shard_map/ppermute | solution.py:436
  43.2 11.0 %copy-start.13 = (bf16[256,1280]{1,0:T(8,128)(2,1)}, bf16[256,1280]{1,0:T(8,128)(2,1)S(1)}, u32[]{:S(2)}) copy-start(bf16[256,1280]{1,0:T(8,128)(2,1)S(1)} %collective-permute-done.near_ref) | copy-start | bytes 1966084
  43.2 11.0 %collective-permute-start.4 = (bf16[1280,640]{1,0:T(8,128)(2,1)}, bf16[1280,640]{1,0:T(8,128)(2,1)}, u32[]{:S(2)}, u32[]{:S(2)}) collective-permute-start(bf16[1280,640]{1,0:T(8,128)(2,1)} %collective-permute-done.3.refs_7_), channel_id=1, source_target_pairs={{4,0},{8,12},{20,16},{24,28},{5,1},{9,13},{21,17},{25,29},{6,2},{1... | collective-permute-start | bytes 4915208 | tf_op jit(solution)/shard_map/ppermute | solution.py:471
  45.3 37.1 %collective-permute-start.7 = (bf16[784,640]{1,0:T(8,128)(2,1)}, bf16[784,640]{1,0:T(8,128)(2,1)S(1)}, u32[]{:S(2)}, u32[]{:S(2)}) collective-permute-start(bf16[784,640]{1,0:T(8,128)(2,1)} %get-tuple-element.39), channel_id=1, source_target_pairs={{0,16},{4,20},{8,24},{12,28},{16,0},{20,4},{24,8},{28,12},{1,17},{... | collective-permute-start | bytes 3010568 | tf_op jit(solution)/shard_map/ppermute | solution.py:436
  45.9 25.5 %collective-permute-start.8 = (bf16[512,640]{1,0:T(8,128)(2,1)}, bf16[512,640]{1,0:T(8,128)(2,1)S(1)}, u32[]{:S(2)}, u32[]{:S(2)}) collective-permute-start(bf16[512,640]{1,0:T(8,128)(2,1)} %get-tuple-element.44.refs_0_), channel_id=1, source_target_pairs={{0,8},{4,12},{8,0},{12,4},{16,24},{20,28},{24,16},{28,20},{1,9},{5... | collective-permute-start | bytes 1966088 | tf_op jit(solution)/shard_map/ppermute | solution.py:436
  54.0 26.7 %collective-permute-start.9 = (bf16[512,640]{1,0:T(8,128)(2,1)}, bf16[512,640]{1,0:T(8,128)(2,1)S(1)}, u32[]{:S(2)}, u32[]{:S(2)}) collective-permute-start(bf16[512,640]{1,0:T(8,128)(2,1)} %get-tuple-element.40), channel_id=1, source_target_pairs={{0,24},{4,28},{8,16},{12,20},{16,8},{20,12},{24,0},{28,4},{1,25},{... | collective-permute-start | bytes 1966088 | tf_op jit(solution)/shard_map/ppermute | solution.py:436
  63.6 21.2 %collective-permute-start.6 = (bf16[2,1,256,640]{3,2,1,0:T(8,128)(2,1)}, bf16[2,1,256,640]{3,2,1,0:T(8,128)(2,1)S(1)}, u32[]{:S(2)}, u32[]{:S(2)}) collective-permute-start(bf16[2,1,256,640]{3,2,1,0:T(8,128)(2,1)} %get-tuple-element.34), channel_id=1, source_target_pairs={{1,2},{2,1},{5,6},{6,5},{9,10},{10,9},{13,14},{14,13},{17,18},{18,... | collective-permute-start | bytes 1966088 | tf_op jit(solution)/shard_map/ppermute | solution.py:399
  64.3 20.5 %collective-permute-start.10 = (bf16[2,1,256,640]{3,2,1,0:T(8,128)(2,1)}, bf16[2,1,256,640]{3,2,1,0:T(8,128)(2,1)}, u32[]{:S(2)}, u32[]{:S(2)}) collective-permute-start(bf16[2,1,256,640]{3,2,1,0:T(8,128)(2,1)} %get-tuple-element.34), channel_id=1, source_target_pairs={{0,1},{3,2},{4,5},{7,6},{8,9},{11,10},{12,13},{15,14},{16,17},{19,... | collective-permute-start | bytes 1966088 | tf_op jit(solution)/shard_map/ppermute | solution.py:399
  71.3 11.1 %copy-start.5 = (bf16[512,640]{1,0:T(8,128)(2,1)}, bf16[512,640]{1,0:T(8,128)(2,1)S(1)}, u32[]{:S(2)}) copy-start(bf16[512,640]{1,0:T(8,128)(2,1)S(1)} %collective-permute-done.8.refs_0_.refs_2_) | copy-start | bytes 1966084
  85.6 5.1 %copy-start.8 = (bf16[512,640]{1,0:T(8,128)(2,1)S(1)}, bf16[512,640]{1,0:T(8,128)(2,1)}, u32[]{:S(2)}) copy-start(bf16[512,640]{1,0:T(8,128)(2,1)} %copy-done.7) | copy-start | bytes 1966084
  88.1 4.3 %collective-permute-start.13 = (bf16[512,640]{1,0:T(8,128)(2,1)S(1)}, bf16[512,640]{1,0:T(8,128)(2,1)S(1)}, u32[]{:S(2)}, u32[]{:S(2)}) collective-permute-start(bf16[512,640]{1,0:T(8,128)(2,1)S(1)} %copy-done.4), channel_id=1, source_target_pairs={{0,4},{4,0},{8,12},{12,8},{16,20},{20,16},{24,28},{28,24},{1,5},{5... | collective-permute-start | bytes 1966088 | tf_op jit(solution)/shard_map/ppermute | solution.py:436
  90.2 6.5 %collective-permute-start.14 = (bf16[784,640]{1,0:T(8,128)(2,1)S(1)}, bf16[784,640]{1,0:T(8,128)(2,1)S(1)}, u32[]{:S(2)}, u32[]{:S(2)}) collective-permute-start(bf16[784,640]{1,0:T(8,128)(2,1)S(1)} %copy-done.1), channel_id=1, source_target_pairs={{0,4},{4,0},{8,12},{12,8},{16,20},{20,16},{24,28},{28,24},{1,5},{5... | collective-permute-start | bytes 3010568 | tf_op jit(solution)/shard_map/ppermute | solution.py:436
  90.3 4.7 %collective-permute-start.15 = (bf16[512,640]{1,0:T(8,128)(2,1)S(1)}, bf16[512,640]{1,0:T(8,128)(2,1)S(1)}, u32[]{:S(2)}, u32[]{:S(2)}) collective-permute-start(bf16[512,640]{1,0:T(8,128)(2,1)S(1)} %copy-done.6), channel_id=1, source_target_pairs={{0,4},{4,0},{8,12},{12,8},{16,20},{20,16},{24,28},{28,24},{1,5},{5... | collective-permute-start | bytes 1966088 | tf_op jit(solution)/shard_map/ppermute | solution.py:436
  90.7 4.5 %collective-permute-start.16 = (bf16[512,640]{1,0:T(8,128)(2,1)S(1)}, bf16[512,640]{1,0:T(8,128)(2,1)S(1)}, u32[]{:S(2)}, u32[]{:S(2)}) collective-permute-start(bf16[512,640]{1,0:T(8,128)(2,1)S(1)} %copy-done.8), channel_id=1, source_target_pairs={{0,4},{4,0},{8,12},{12,8},{16,20},{20,16},{24,28},{28,24},{1,5},{5... | collective-permute-start | bytes 1966088 | tf_op jit(solution)/shard_map/ppermute | solution.py:436
  90.8 31.3 %collective-permute-start.11 = (bf16[2,1,256,640]{3,2,1,0:T(8,128)(2,1)}, bf16[2,1,256,640]{3,2,1,0:T(8,128)(2,1)}, u32[]{:S(2)}, u32[]{:S(2)}) collective-permute-start(bf16[2,1,256,640]{3,2,1,0:T(8,128)(2,1)} %get-tuple-element.43), channel_id=1, source_target_pairs={{0,1},{1,0},{2,3},{3,2},{4,5},{5,4},{6,7},{7,6},{8,9},{9,8},{10,11... | collective-permute-start | bytes 1966088 | tf_op jit(solution)/shard_map/ppermute | solution.py:399
  92.4 32.0 %collective-permute-start.12 = (bf16[2,1,256,640]{3,2,1,0:T(8,128)(2,1)}, bf16[2,1,256,640]{3,2,1,0:T(8,128)(2,1)S(1)}, u32[]{:S(2)}, u32[]{:S(2)}) collective-permute-start(bf16[2,1,256,640]{3,2,1,0:T(8,128)(2,1)} %add.31), channel_id=1, source_target_pairs={{0,2},{1,3},{2,0},{3,1},{4,6},{5,7},{6,4},{7,5},{8,10},{9,11},{10,... | collective-permute-start | bytes 1966088 | tf_op jit(solution)/shard_map/ppermute | solution.py:399
  125.2 10.2 %copy-start.3 = (bf16[256,1280]{1,0:T(8,128)(2,1)S(1)}, bf16[256,1280]{1,0:T(8,128)(2,1)}, u32[]{:S(2)}) copy-start(bf16[256,1280]{1,0:T(8,128)(2,1)} %param.12) | copy-start | bytes 1966084
  128.1 9.5 %copy-start.12 = (bf16[256,640]{1,0:T(8,128)(2,1)S(1)}, bf16[256,640]{1,0:T(8,128)(2,1)}, u32[]{:S(2)}) copy-start(bf16[256,640]{1,0:T(8,128)(2,1)} %get-tuple-element.48) | copy-start | bytes 983044
  128.1 7.4 %collective-permute-start.17 = (bf16[1,256,640]{2,1,0:T(8,128)(2,1)}, bf16[1,256,640]{2,1,0:T(8,128)(2,1)S(1)}, u32[]{:S(2)}, u32[]{:S(2)}) collective-permute-start(bf16[1,256,640]{2,1,0:T(8,128)(2,1)} %get-tuple-element.52), channel_id=1, source_target_pairs={{0,8},{4,12},{8,0},{12,4},{16,24},{20,28},{24,16},{28,20},{1,9},{5... | collective-permute-start | bytes 983048 | tf_op jit(solution)/shard_map/ppermute | solution.py:436
  128.2 9.4 %collective-permute-start.18 = (bf16[256,640]{1,0:T(8,128)(2,1)S(1)}, bf16[256,640]{1,0:T(8,128)(2,1)S(1)}, u32[]{:S(2)}, u32[]{:S(2)}) collective-permute-start(bf16[256,640]{1,0:T(8,128)(2,1)S(1)} %copy-done.16), channel_id=1, source_target_pairs={{0,16},{4,20},{8,24},{12,28},{16,0},{20,4},{24,8},{28,12},{1,17},{... | collective-permute-start | bytes 983048 | tf_op jit(solution)/shard_map/ppermute | solution.py:436
  (12 other events, 24.6 us)

commit v5 on v4

--- a/solution.py
+++ b/solution.py
@@ -12,7 +12,7 @@
 TAG_ROWS = 16
 NEG_FILL = -1e30
 LOG2E = 1.4426950408889634
-VMEM_LIMIT = 60 * 2**20
+VMEM_LIMIT = 64 * 2**20 - 2**17
 PEAK = 1.1535e15
 
 
@@ -200,6 +200,22 @@
         cost_estimate=cost_of(100e-6),
         name="read_prompts",
     )(prompt_of, asked, *gates)
+
+
+def gate_kernel(value_ref, *refs):
+    refs[-1][0] = value_ref[0]
+
+
+def gate(value, *waited):
+    scalars = pl.BlockSpec(memory_space=pltpu.SMEM)
+    return pl.pallas_call(
+        gate_kernel,
+        in_specs=[scalars] + [pl.BlockSpec(memory_space=pltpu.HBM)] * len(waited),
+        out_specs=scalars,
+        out_shape=jax.ShapeDtypeStruct((1,), jnp.int32),
+        cost_estimate=cost_of(100e-6),
+        name="gate",
+    )(value.reshape(1), *waited)[0]
 
 
 def pack_kernel(side_ref, prompt_ref, k_ref, v_ref, q_ref, keep_ref, give_ref, ask_ref):
@@ -266,13 +282,15 @@
     )(queries, keys, values)
 
 
-def project_kernel(count, span, places, place_ref, own_ref, near_ref, *refs):
+def project_kernel(count, span, places, joint, place_ref, own_ref, near_ref, *refs):
     held, passed = refs[:count], refs[count : 2 * count]
-    outs = refs[2 * count : 2 * count + places]
-    x_ref, weights, terms, x_sems, sems, out_sems = refs[2 * count + places :]
+    outs = refs[2 * count : -6]
+    x_ref, weights, terms, x_sems, sems, out_sems = refs[-6:]
     chip, holder, at_tp = place_ref[0], place_ref[1], place_ref[2]
     rows, columns = own_ref.shape[0], held[0].shape[1]
-    blocks = outs[0].shape[1]
+    blocks = outs[0].shape[0]
+    if joint:
+        outs = (*outs[: places - 1], outs[-1].at[0], *outs[places - 1 : -1], outs[-1].at[1])
 
     def rows_in(part):
         source = (near_ref, own_ref)[part]
@@ -285,8 +303,9 @@
         place = weights.at[at // span, :, first : first + columns]
         return pltpu.make_async_copy(choice[at], place, sems.at[at])
 
-    def terms_out(at, distance, block):
-        return pltpu.make_async_copy(terms.at[at], outs[distance].at[:, block], out_sems.at[at])
+    def terms_out(at, part, distance, block):
+        target = outs[part * places + distance].at[block]
+        return pltpu.make_async_copy(terms.at[at, part], target, out_sems.at[at, part])
 
     for part in range(2):
         rows_in(part).start()
@@ -320,31 +339,37 @@
 
                 @pl.when(away == distance)
                 def _(at=at, distance=distance, block=block):
-                    terms_out(at, distance, block).start()
+                    for part in range(2):
+                        terms_out(at, part, distance, block).start()
 
     for at in range(count):
-        terms_out(at, 0, 0).wait()
-
-
-def project(tps, place, own, near, held, passed):
+        for part in range(2):
+            terms_out(at, part, 0, 0).wait()
+
+
+def project(tps, place, own, near, held, passed, joint):
     rows = own.shape[0]
     depth, columns = held[0].shape
     count = len(held)
     span = 2 if columns % HD == 0 else 1
-    hbm = pl.BlockSpec(memory_space=pl.ANY)
-    out = jax.ShapeDtypeStruct((2, count // tps, rows, columns), jnp.bfloat16)
-    return pl.pallas_call(
-        functools.partial(project_kernel, count, span, tps),
+    hbm = pl.BlockSpec(memory_space=pltpu.HBM)
+    out = jax.ShapeDtypeStruct((count // tps, rows, columns), jnp.bfloat16)
+    return pl.pallas_call(
+        functools.partial(project_kernel, count, span, tps, joint),
         in_specs=[pl.BlockSpec(memory_space=pltpu.SMEM)] + [hbm] * (2 + 2 * count),
-        out_specs=[hbm] * tps,
-        out_shape=[out] * tps,
+        out_specs=[hbm] * (2 * tps - joint),
+        out_shape=(
+            [out] * (2 * tps - 2) + [jax.ShapeDtypeStruct((2, *out.shape), out.dtype)]
+            if joint
+            else [out] * (2 * tps)
+        ),
         scratch_shapes=[
             pltpu.VMEM((2 * rows, depth), jnp.bfloat16),
             pltpu.VMEM((count // span, depth, span * columns), jnp.bfloat16),
             pltpu.VMEM((count, 2, rows, columns), jnp.bfloat16),
             pltpu.SemaphoreType.DMA((2,)),
             pltpu.SemaphoreType.DMA((count,)),
-            pltpu.SemaphoreType.DMA((count,)),
+            pltpu.SemaphoreType.DMA((count, 2)),
         ],
         compiler_params=pltpu.CompilerParams(vmem_limit_bytes=VMEM_LIMIT),
         cost_estimate=cost_of(10e-6),
@@ -352,47 +377,96 @@
     )(place, own, near, *held, *passed)
 
 
-def add_kernel(count, *refs):
-    outs, (scratch, sems) = refs[count:-2], refs[-2:]
+def fetch(sources, scratch, sems):
     copies = [
-        pltpu.make_async_copy(refs[at], scratch.at[at], sems.at[at]) for at in range(count)
+        pltpu.make_async_copy(source, scratch.at[at], sems.at[at])
+        for at, source in enumerate(sources)
     ]
     for copy in copies:
         copy.start()
     for copy in copies:
         copy.wait()
-    total = scratch[0].astype(jnp.float32)
-    for at in range(1, count):
-        total += scratch[at].astype(jnp.float32)
-    total = total.astype(scratch.dtype)
-    if len(outs) == 1:
-        outs[0][...] = total
-    else:
-        for at, out in enumerate(outs):
-            out[...] = total[at]
-
-
-def add(*terms, parted=True):
-    hbm = pl.BlockSpec(memory_space=pl.ANY)
-    vmem = pl.BlockSpec(memory_space=pltpu.VMEM)
+    return [scratch[at].astype(jnp.float32) for at in range(len(copies))]
+
+
+def add_kernel(halves, *refs):
+    out, scratch, sems = refs[-3:]
+    sources = [ref if half is None else ref.at[half] for ref, half in zip(refs, halves)]
+    out[...] = sum(fetch(sources, scratch, sems)).astype(out.dtype)
+
+
+def add(*terms):
+    halves = tuple(term[1] if isinstance(term, tuple) else None for term in terms)
+    terms = [term[0] if isinstance(term, tuple) else term for term in terms]
     shape, dtype = terms[0].shape, terms[0].dtype
     return pl.pallas_call(
-        functools.partial(add_kernel, len(terms)),
-        in_specs=[hbm] * len(terms),
-        out_specs=[vmem] * shape[0] if parted else vmem,
-        out_shape=(
-            [jax.ShapeDtypeStruct(shape[1:], dtype)] * shape[0]
-            if parted
-            else jax.ShapeDtypeStruct(shape, dtype)
-        ),
+        functools.partial(add_kernel, halves),
+        in_specs=[pl.BlockSpec(memory_space=pltpu.HBM)] * len(terms),
+        out_specs=pl.BlockSpec(memory_space=pltpu.VMEM),
+        out_shape=jax.ShapeDtypeStruct(shape, dtype),
         scratch_shapes=[
             pltpu.VMEM((len(terms),) + shape, dtype),
             pltpu.SemaphoreType.DMA((len(terms),)),
         ],
         compiler_params=pltpu.CompilerParams(vmem_limit_bytes=VMEM_LIMIT),
-        cost_estimate=cost_of(2e-6),
+        cost_estimate=cost_of(100e-6),
         name="add",
     )(*terms)
+
+
+def join_kernel(near_ref, own_ref, far_ref, near_out, own_out, scratch, sems):
+    near, own, *far = fetch((near_ref, own_ref, far_ref.at[0], far_ref.at[1]), scratch, sems)
+    near_out[...] = (near + far[0]).astype(near_out.dtype)
+    own_out[...] = (own + far[1]).astype(own_out.dtype)
+
+
+def join(near, own, far):
+    vmem = pl.BlockSpec(memory_space=pltpu.VMEM)
+    return pl.pallas_call(
+        join_kernel,
+        in_specs=[pl.BlockSpec(memory_space=pltpu.HBM)] * 3,
+        out_specs=[vmem] * 2,
+        out_shape=[jax.ShapeDtypeStruct(near.shape, near.dtype)] * 2,
+        scratch_shapes=[
+            pltpu.VMEM((4,) + near.shape, near.dtype),
+            pltpu.SemaphoreType.DMA((4,)),
+        ],
+        compiler_params=pltpu.CompilerParams(vmem_limit_bytes=VMEM_LIMIT),
+        cost_estimate=cost_of(2e-6),
+        name="join",
+    )(near, own, far)
+
+
+def finish_kernel(halves, side_ref, hidden_ref, *refs):
+    o_ref, scratch, sems = refs[-3:]
+    sources = [ref if half is None else ref.at[half] for ref, half in zip(refs, halves)]
+    received, *parts = fetch(sources, scratch, sems)
+    half = received.shape[2]
+    kept = pl.ds(pl.multiple_of(side_ref[0] * half, HD), half)
+    other = pl.ds(pl.multiple_of((1 - side_ref[0]) * half, HD), half)
+    o_ref[:, other] = (hidden_ref[:, other].astype(jnp.float32) + received[0]).astype(o_ref.dtype)
+    o_ref[:, kept] = (hidden_ref[:, kept].astype(jnp.float32) + sum(parts)[0]).astype(o_ref.dtype)
+
+
+def finish(side, hidden, received, parts):
+    terms = [received, *parts]
+    halves = tuple(term[1] if isinstance(term, tuple) else None for term in terms)
+    terms = [term[0] if isinstance(term, tuple) else term for term in terms]
+    vmem = pl.BlockSpec(memory_space=pltpu.VMEM)
+    hbm = pl.BlockSpec(memory_space=pltpu.HBM)
+    return pl.pallas_call(
+        functools.partial(finish_kernel, halves),
+        in_specs=[pl.BlockSpec(memory_space=pltpu.SMEM), vmem] + [hbm] * len(terms),
+        out_specs=vmem,
+        out_shape=jax.ShapeDtypeStruct(hidden.shape, hidden.dtype),
+        scratch_shapes=[
+            pltpu.VMEM((len(terms),) + received.shape, received.dtype),
+            pltpu.SemaphoreType.DMA((len(terms),)),
+        ],
+        compiler_params=pltpu.CompilerParams(vmem_limit_bytes=VMEM_LIMIT),
+        cost_estimate=cost_of(2e-6),
+        name="finish",
+    )(side.reshape(1), hidden, *terms)
 
 
 def to_tp(value, pairs):
@@ -466,8 +540,6 @@
                 if bit != 1:
                     pieces += [swap(piece, 2 << bit) for piece in pieces]
         spans = text_k.shape[:2]
-        prompts = read_prompts(prompt_of, asked, pieces[2:])
-
     across_passed = lax.ppermute(after(across, near), "req", list(zip(second_of, first_of)))
     held = [w_out, beside_passed, beside, across_passed]
     passed = [own_passed, beside, beside_passed, across]
@@ -479,25 +551,6 @@
     at = lax.axis_index("tp")
     order = jnp.stack([chip, holder, at]).astype(jnp.int32)
 
-    terms = project(tps, order, own, near, held, passed)
-
-    if split_heads and tps == 4 and chips == 4:
-        far = to_tp(terms[3], [(0, 1), (3, 2)])
-        inner = to_tp(terms[3], [(1, 2), (2, 1)])
-        joined = add(terms[2], after(far, inner, prompts), parted=False)
-        crossing = to_tp(joined, apart(4, 2))
-        outer, pieces = after((terms[1], pieces), joined)
-        outer = to_tp(outer, apart(4, 1))
-        pieces += [swap(piece, 1) for piece in pieces]
-        mine, others = cross_attention(prompts, text_side, q_cross, asked, pieces, spans)
-        outer, crossing = after((outer, crossing), mine)
-        given, kept = add(terms[0], inner, outer, crossing)
-    else:
-        given, kept = add(terms[0], *[to_tp(terms[d], apart(tps, d)) for d in range(1, tps)])
-        if split_heads:
-            pieces += [swap(piece, 1) for piece in pieces]
-            mine, others = cross_attention(prompts, text_side, q_cross, asked, pieces, spans)
-
     def in_order(side, kept, received, axis):
         return jnp.where(
             side == 0,
@@ -505,12 +558,46 @@
             jnp.concatenate([received, kept], axis=axis),
         )
 
-    if split_heads:
-        cross_heads = in_order(text_side, mine, swap(others, 4), 1)
+    line = split_heads and tps == 4 and chips == 4
+    terms = project(tps, order, own, near, held, passed, line)
+    if line:
+        near_terms, own_terms, last = terms[:3], terms[3:6], terms[6]
+        far, inner = to_tp(last, [(0, 1), (3, 2)]), to_tp(last, [(1, 2), (2, 1)])
+        prompts = read_prompts(prompt_of, asked, pieces[2:])
+        near_joined, own_joined = join(near_terms[2], own_terms[2], after(far, inner, prompts))
+        near_outer, own_outer, *late = after(
+            (near_terms[1], own_terms[1], *pieces), near_joined
+        )
+        near_outer, near_crossing = to_tp(near_outer, apart(4, 1)), to_tp(near_joined, apart(4, 2))
+        own_outer, own_crossing = to_tp(own_outer, apart(4, 1)), to_tp(own_joined, apart(4, 2))
+        pieces += [swap(piece, 1) for piece in late]
+        mine, others = cross_attention(prompts, text_side, q_cross, asked, pieces, spans)
+        answer = swap(others, 4)
+        near_outer = after(near_outer, mine)
+        given = add(near_terms[0], (inner, 0), near_outer, near_crossing)
+        own_parts = [own_terms[0], (inner, 1), own_outer, own_crossing]
+        cross_heads = in_order(text_side, mine, answer, 1)
+        side = gate(side, own_outer, own_crossing, cross_heads)
     else:
+        near_parts = [
+            [part[0]] + [to_tp(part[d], apart(tps, d)) for d in range(1, tps)]
+            for part in (terms[:tps], terms[tps:])
+        ]
+        given, own_parts = add(*near_parts[0]), near_parts[1]
+        if split_heads:
+            prompts = read_prompts(prompt_of, asked, [])
+            pieces += [swap(piece, 1) for piece in pieces]
+            mine, others = cross_attention(prompts, text_side, q_cross, asked, pieces, spans)
+            answer = swap(others, 4)
+            cross_heads = in_order(text_side, mine, answer, 1)
+
+    if not split_heads:
         cross_heads = whole_cross(q_cross, prompt_of, text_k, text_v)
 
-    ordered = in_order(side, kept, swap(given, 2), 2).transpose(1, 0, 2).reshape(rows, width)
+    received = swap(given, 2)
+    if received.shape[0] == 1 and received.shape[2] % HD == 0:
+        return finish(side, hidden, received, own_parts), cross_heads
+    ordered = in_order(side, add(*own_parts), received, 2).transpose(1, 0, 2).reshape(rows, width)
     hidden_out = (hidden.astype(jnp.float32) + ordered.astype(jnp.float32)).astype(jnp.bfloat16)
     return (hidden_out, cross_heads)
 

time: 140 us -> 130 us (0.929)
  waiting for transfers between devices: 55.6 us -> 39.9 us
  Pallas kernels: 35.4 us -> 49.3 us
  local copies, waits for them, and re-layouts: 6.32 us -> 1.24 us
  starting transfers between devices: 36.1 us -> 34.2 us
    pallas_call x1, Pallas kernels: 10.2 us -> 20.4 us  [self_attention(): pl.pallas_call(functools.partial(self_kernel, block_rows, heads), grid_sp...]
    ppermute x1, waiting for transfers between devices: 8.02 us -> 0.01 us  [per_device(): lax.ppermute(w_out, 'req', [(first_of[i], first_of[i ^ 2]) for i in range...]
    unnamed x34 -> x0, local copies, waits for them, and re-layouts: 5.08 us -> none
    ppermute x4 -> x6, waiting for transfers between devices: 20.6 us -> 16 us  [to_tp(): return lax.ppermute(value, 'tp', pairs)]
    pallas_call x3 -> x5, Pallas kernels: 14.6 us -> 18.4 us  [the longest x1 9.27 us: project(): pl.pallas_call(functools.partial(project_kernel, count, span, tps, joint)...]
    ppermute x11, waiting for transfers between devices: 27 us -> 23.9 us  [swap(): return lax.ppermute(array, 'req', [(i, i ^ distance) for i in range(reqs)])]
    ppermute x11, starting transfers between devices: 15.3 us -> 12.8 us  [swap(): return lax.ppermute(array, 'req', [(i, i ^ distance) for i in range(reqs)])]
    convert_element_type x1 -> x0, other arithmetic: 2.14 us -> none  [per_device(): (hidden.astype(jnp.float32) + ordered.astype(jnp.float32)).astype(jnp.bfl...]
  transfers between devices with their start and end apart: 19 -> 21, of which waited for: 8 -> 9; matrix products, arithmetic and copies ran while one was open for 3% -> 3% of each run, Pallas kernels for 22% -> 33%
where the time goes in v5:
time: 130 us; the launch traced here: 129 us
  Pallas kernels  49.3 us (38%)
  waiting for transfers between devices  39.9 us (31%)
  starting transfers between devices  34.2 us (26%)
  other arithmetic  2.87 us (2%)
  between operations  1.59 us (1%)
    ppermute x11, waiting for transfers between devices, swap(): return lax.ppermute(array, 'req', [(i, i ^ distance) for i in range(reqs)])  23.9 us
    pallas_call x1, Pallas kernels, self_attention(): pl.pallas_call(functools.partial(self_kernel, block_rows, heads), grid_sp...  20.4 us
    ppermute x6, waiting for transfers between devices, to_tp(): return lax.ppermute(value, 'tp', pairs)  16 us
    ppermute x11, starting transfers between devices, swap(): return lax.ppermute(array, 'req', [(i, i ^ distance) for i in range(reqs)])  12.8 us
    ppermute x6, starting transfers between devices, to_tp(): return lax.ppermute(value, 'tp', pairs)  12.6 us
    pallas_call x1, Pallas kernels, project(): pl.pallas_call(functools.partial(project_kernel, count, span, tps, joint)...  9.27 us
    pallas_call x1, Pallas kernels, cross_attention(): pl.pallas_call(functools.partial(cross_kernel, half // HD, len(pieces), s...  6.11 us
    pallas_call x1, Pallas kernels, finish(): pl.pallas_call(functools.partial(finish_kernel, halves), in_specs=[pl.Blo...  4.25 us
  transfers between devices with their start and end apart: 21, of which 9 were waited for; matrix products, arithmetic and copies ran while one was open for 3% of the time, Pallas kernels for 33%

profile of v5, /device:TPU:0, one launch (start us, length us, event | category | flops | bytes accessed | tf_op | source)
XLA Modules:
  0.0 129.1 jit_solution(14092336746185119377)
XLA Ops:
  0.6 3.0 %collective-permute-start.1 = (bf16[1280,640]{1,0:T(8,128)(2,1)}, bf16[1280,640]{1,0:T(8,128)(2,1)}, u32[]{:S(2)}, u32[]{:S(2)}) collective-permute-start(bf16[1280,640]{1,0:T(8,128)(2,1)} %refs_0_.1), channel_id=1, source_target_pairs={{0,16},{12,28},{16,0},{28,12},{4,8},{8,4},{20,24},{24,20},{1,17},{... | collective-permute-start | bytes 4915208 | tf_op jit(solution)/shard_map/ppermute | solution.py:514
  4.9 20.4 %self_attention.1.own_ref = bf16[256,1280]{1,0:T(8,128)(2,1)} custom-call(s32[1]{0:T(128)} %dynamic_slice.4.length_ref, bf16[256,1280]{1,0:T(8,128)(2,1)} %q_ref.2, bf16[256,1280]{1,0:T(8,128)(2,1)} %kn_ref.1, bf16[256,1280]{1,0:T(8,128)(2,1)} %vn_ref.1, bf16[4096,1280]{1,0:T(8,128)(2,1)} %bitcast.7, bf16[4096,1280]{1,0:T(8,128)(2,1)} %bitcast.8), custom_call_target="tpu_custom_call" | custom-call | flops 23069999104 | tf_op jit(solution)/shard_map/self_attention/pallas_call | solution.py:120
  25.3 1.8 %collective-permute-start.3 = (bf16[1280,640]{1,0:T(8,128)(2,1)}, bf16[1280,640]{1,0:T(8,128)(2,1)}, u32[]{:S(2)}, u32[]{:S(2)}) collective-permute-start(bf16[1280,640]{1,0:T(8,128)(2,1)} %collective-permute-done.1.refs_2_.refs_5_), channel_id=1, source_target_pairs={{4,20},{8,24},{20,4},{24,8},{5,21},{9,25},{21,5},{25,9},{6,22},{10... | collective-permute-start | bytes 4915208 | tf_op jit(solution)/shard_map/ppermute | solution.py:525
  28.0 2.5 %collective-permute-start.5 = (bf16[1280,640]{1,0:T(8,128)(2,1)}, bf16[1280,640]{1,0:T(8,128)(2,1)}, u32[]{:S(2)}, u32[]{:S(2)}) collective-permute-start(bf16[1280,640]{1,0:T(8,128)(2,1)} %refs_0_.1), channel_id=1, source_target_pairs={{0,4},{12,8},{16,20},{28,24},{1,5},{13,9},{17,21},{29,25},{2,6},{1... | collective-permute-start | bytes 4915208 | tf_op jit(solution)/shard_map/ppermute | solution.py:520
  31.1 3.0 %pack.1 = (bf16[512,640]{1,0:T(8,128)(2,1)}, bf16[512,640]{1,0:T(8,128)(2,1)}, bf16[784,640]{1,0:T(8,128)(2,1)}) custom-call(s32[1]{0:T(128)} %bitcast.6.side_ref, s32[1]{0:T(128)S(6)} %copy.14.prompt_ref, bf16[4,64,1280]{2,1,0:T(8,128)(2,1)} %k_ref.1, bf16[4,64,1280]{2,1,0:T(8,128)(2,1)} %v_ref.1, bf16[256,1280]{1,0:T(8,128)(2,1)} %q_ref.4), custom_call_target="tpu_custom_call" | custom-call | flops 3460499968 | tf_op jit(solution)/shard_map/pack/pallas_call | solution.py:246
  34.1 9.2 %collective-permute-done.near_ref = bf16[256,1280]{1,0:T(8,128)(2,1)} collective-permute-done((bf16[256,1280]{1,0:T(8,128)(2,1)}, bf16[256,1280]{1,0:T(8,128)(2,1)}, u32[]{:S(2)}, u32[]{:S(2)}) %collective-permute-start) | collective-permute-done | bytes 655392 | tf_op jit(solution)/shard_map/ppermute | solution.py:510
  45.9 8.3 %collective-permute-start.7 = (bf16[512,640]{1,0:T(8,128)(2,1)}, bf16[512,640]{1,0:T(8,128)(2,1)}, u32[]{:S(2)}, u32[]{:S(2)}) collective-permute-start(bf16[512,640]{1,0:T(8,128)(2,1)} %get-tuple-element.50.refs_0_), channel_id=1, source_target_pairs={{0,8},{4,12},{8,0},{12,4},{16,24},{20,28},{24,16},{28,20},{1,9},{5... | collective-permute-start | bytes 1966088 | tf_op jit(solution)/shard_map/ppermute | solution.py:510
  54.2 9.3 %project.1 = (bf16[1,256,640]{2,1,0:T(8,128)(2,1)}, bf16[1,256,640]{2,1,0:T(8,128)(2,1)}, bf16[1,256,640]{2,1,0:T(8,128)(2,1)}, bf16[1,256,640]{2,1,0:T(8,128)(2...) custom-call(s32[3]{0:T(128)} %pad_add_fusion.place_ref, ...), custom_call_target="tpu_custom_call" | custom-call | flops 11534999552 | tf_op jit(solution)/shard_map/project/pallas_call | solution.py:357
  63.5 4.4 %collective-permute-start.9 = (bf16[2,1,256,640]{3,2,1,0:T(8,128)(2,1)}, bf16[2,1,256,640]{3,2,1,0:T(8,128)(2,1)}, u32[]{:S(2)}, u32[]{:S(2)}) collective-permute-start(bf16[2,1,256,640]{3,2,1,0:T(8,128)(2,1)} %get-tuple-element.45), channel_id=1, source_target_pairs={{0,1},{3,2},{4,5},{7,6},{8,9},{11,10},{12,13},{15,14},{16,17},{19,... | collective-permute-start | bytes 1966088 | tf_op jit(solution)/shard_map/ppermute | solution.py:473
  70.2 10.5 %collective-permute-done.8.refs_1_.refs_3_ = bf16[512,640]{1,0:T(8,128)(2,1)} collective-permute-done((bf16[512,640]{1,0:T(8,128)(2,1)}, bf16[512,640]{1,0:T(8,128)(2,1)}, u32[]{:S(2)}, u32[]{:S(2)}) %collective-permute-start.8) | collective-permute-done | bytes 655392 | tf_op jit(solution)/shard_map/ppermute | solution.py:510
  80.7 2.1 %collective-permute-done.6.tag_ref.near_ref.refs_1_ = bf16[784,640]{1,0:T(8,128)(2,1)} collective-permute-done((bf16[784,640]{1,0:T(8,128)(2,1)}, bf16[784,640]{1,0:T(8,128)(2,1)}, u32[]{:S(2)}, u32[]{:S(2)}) %collective-permute-start.6) | collective-permute-done | bytes 1003552 | tf_op jit(solution)/shard_map/ppermute | solution.py:510
  84.1 2.2 %join.1 = (bf16[1,256,640]{2,1,0:T(8,128)(2,1)}, bf16[1,256,640]{2,1,0:T(8,128)(2,1)}) custom-call(bf16[1,256,640]{2,1,0:T(8,128)(2,1)} %get-tuple-element.43.near_ref, bf16[1,256,640]{2,1,0:T(8,128)(2,1)} %get-tuple-element.44.own_ref, bf16[2,1,256,640]{3,2,1,0:T(8,128)(2,1)} %collective-permute-done.9.far_ref), custom_call_target="tpu_custom_call" | custom-call | flops 2307000064 | tf_op jit(solution)/shard_map/join/pallas_call | solution.py:425
  86.3 2.0 %collective-permute-start.14 = (bf16[784,640]{1,0:T(8,128)(2,1)}, bf16[784,640]{1,0:T(8,128)(2,1)}, u32[]{:S(2)}, u32[]{:S(2)}) collective-permute-start(bf16[784,640]{1,0:T(8,128)(2,1)} %collective-permute-done.6.tag_ref.near_ref.refs_1_), channel_id=1, source_target_pairs={{0,4},{4,0},{8,12},{12,8},{16,20},{20,16},{24,28},{28,24},{1,5},{5... | collective-permute-start | bytes 3010568 | tf_op jit(solution)/shard_map/ppermute | solution.py:510
  88.9 1.6 %collective-permute-start.18 = (bf16[1,256,640]{2,1,0:T(8,128)(2,1)}, bf16[1,256,640]{2,1,0:T(8,128)(2,1)}, u32[]{:S(2)}, u32[]{:S(2)}) collective-permute-start(bf16[1,256,640]{2,1,0:T(8,128)(2,1)} %get-tuple-element.57), channel_id=1, source_target_pairs={{0,1},{1,0},{2,3},{3,2},{4,5},{5,4},{6,7},{7,6},{8,9},{9,8},{10,11... | collective-permute-start | bytes 983048 | tf_op jit(solution)/shard_map/ppermute | solution.py:473
  91.8 2.6 %collective-permute-start.19 = (bf16[1,256,640]{2,1,0:T(8,128)(2,1)}, bf16[1,256,640]{2,1,0:T(8,128)(2,1)}, u32[]{:S(2)}, u32[]{:S(2)}) collective-permute-start(bf16[1,256,640]{2,1,0:T(8,128)(2,1)} %get-tuple-element.47), channel_id=1, source_target_pairs={{0,2},{1,3},{2,0},{3,1},{4,6},{5,7},{6,4},{7,5},{8,10},{9,11},{10,... | collective-permute-start | bytes 983048 | tf_op jit(solution)/shard_map/ppermute | solution.py:473
  94.4 1.6 %collective-permute-start.11 = (bf16[1,256,640]{2,1,0:T(8,128)(2,1)}, bf16[1,256,640]{2,1,0:T(8,128)(2,1)}, u32[]{:S(2)}, u32[]{:S(2)}) collective-permute-start(bf16[1,256,640]{2,1,0:T(8,128)(2,1)} %get-tuple-element.48), channel_id=1, source_target_pairs={{0,1},{1,0},{2,3},{3,2},{4,5},{5,4},{6,7},{7,6},{8,9},{9,8},{10,11... | collective-permute-start | bytes 983048 | tf_op jit(solution)/shard_map/ppermute | solution.py:473
  97.0 6.1 %cross_attention.1 = (bf16[256,640]{1,0:T(8,128)(2,1)}, bf16[256,640]{1,0:T(8,128)(2,1)}) custom-call(s32[2]{0:T(128)} %read_prompts.1.prompts_ref, s32[1]{0:T(128)} %bitcast.6.side_ref, bf16[256,1280]{1,0:T(8,128)(2,1)} %q_ref.4, bf16[784,640]{1,0:T(8,128)(2,1)} %collective-permute-done.6.tag_ref.near_ref.refs_1_, ...), custom_call_target="tpu_custom_call" | custom-call | tf_op jit(solution)/shard_map/cross_attention/pallas_call | solution.py:174
  103.6 1.5 %collective-permute-done.18.refs_2_ = bf16[1,256,640]{2,1,0:T(8,128)(2,1)} collective-permute-done((bf16[1,256,640]{2,1,0:T(8,128)(2,1)}, bf16[1,256,640]{2,1,0:T(8,128)(2,1)}, u32[]{:S(2)}, u32[]{:S(2)}) %collective-permute-start.18) | collective-permute-done | bytes 327712 | tf_op jit(solution)/shard_map/ppermute | solution.py:473
  105.1 5.6 %collective-permute-done.19.refs_3_ = bf16[1,256,640]{2,1,0:T(8,128)(2,1)} collective-permute-done((bf16[1,256,640]{2,1,0:T(8,128)(2,1)}, bf16[1,256,640]{2,1,0:T(8,128)(2,1)}, u32[]{:S(2)}, u32[]{:S(2)}) %collective-permute-start.19) | collective-permute-done | bytes 327712 | tf_op jit(solution)/shard_map/ppermute | solution.py:473
  110.8 2.2 %add.25 = bf16[1,256,640]{2,1,0:T(8,128)(2,1)} custom-call(bf16[1,256,640]{2,1,0:T(8,128)(2,1)} %get-tuple-element.56.refs_0_, bf16[2,1,256,640]{3,2,1,0:T(8,128)(2,1)} %collective-permute-done.10.refs_1_.refs_2_, bf16[1,256,640]{2,1,0:T(8,128)(2,1)} %collective-permute-done.18.refs_2_, bf16[1,256,640]{2,1,0:T(8,128)(2,1)} %collective-permute-done.19.refs_3_), custom_call_target="tpu_custom_call" | custom-call | flops 115350003712 | tf_op jit(solution)/shard_map/add/pallas_call | solution.py:402
  113.0 2.3 %maximum_select_fusion.refs_2_ = bf16[256,1280]{1,0:T(8,128)(2,1)} fusion(bf16[256,640]{1,0:T(8,128)(2,1)} %collective-permute-done.17, bf16[256,640]{1,0:T(8,128)(2,1)} %get-tuple-element.54, pred[]{:T(512)S(6)} %eq.11), kind=kLoop, calls=%fused_computation | loop fusion | flops 2949120 | bytes 1310721 | tf_op jit(solution)/shard_map/jit(_where)/select_n | solution.py:555
  115.3 3.4 %collective-permute-done.11.refs_0_.refs_3_ = bf16[1,256,640]{2,1,0:T(8,128)(2,1)} collective-permute-done((bf16[1,256,640]{2,1,0:T(8,128)(2,1)}, bf16[1,256,640]{2,1,0:T(8,128)(2,1)}, u32[]{:S(2)}, u32[]{:S(2)}) %collective-permute-start.11) | collective-permute-done | bytes 327712 | tf_op jit(solution)/shard_map/ppermute | solution.py:473
  118.7 5.5 %collective-permute-done.12.refs_1_.refs_4_ = bf16[1,256,640]{2,1,0:T(8,128)(2,1)} collective-permute-done((bf16[1,256,640]{2,1,0:T(8,128)(2,1)}, bf16[1,256,640]{2,1,0:T(8,128)(2,1)}, u32[]{:S(2)}, u32[]{:S(2)}) %collective-permute-start.12) | collective-permute-done | bytes 327712 | tf_op jit(solution)/shard_map/ppermute | solution.py:473
  124.7 4.3 %finish.1 = bf16[256,1280]{1,0:T(8,128)(2,1)} custom-call(s32[1]{0:T(128)} %gate.1.side_ref, bf16[256,1280]{1,0:T(8,128)(2,1)} %hidden_ref.1, bf16[1,256,640]{2,1,0:T(8,128)(2,1)} %collective-permute-done.20.refs_0_, bf16[1,256,640]{2,1,0:T(8,128)(2,1)} %get-tuple-element.59.refs_1_, bf16[2,1,256,640]{3,2,1,0:T(8,128)(2,1)} %collective-permute-done.10.refs_1_.refs_2_, ...), custom_call_target="tpu_custom_call" | custom-call | flops 2307000064 | tf_op jit(solution)/shard_map/finish/pallas_call | solution.py:457
  (30 shorter events, 12.3 us)
Async XLA Ops:
  0.6 24.7 %collective-permute-start.1 = (bf16[1280,640]{1,0:T(8,128)(2,1)}, bf16[1280,640]{1,0:T(8,128)(2,1)}, u32[]{:S(2)}, u32[]{:S(2)}) collective-permute-start(bf16[1280,640]{1,0:T(8,128)(2,1)} %refs_0_.1), channel_id=1, source_target_pairs={{0,16},{12,28},{16,0},{28,12},{4,8},{8,4},{20,24},{24,20},{1,17},{... | collective-permute-start | bytes 4915208 | tf_op jit(solution)/shard_map/ppermute | solution.py:514
  25.3 8.9 %collective-permute-start.3 = (bf16[1280,640]{1,0:T(8,128)(2,1)}, bf16[1280,640]{1,0:T(8,128)(2,1)}, u32[]{:S(2)}, u32[]{:S(2)}) collective-permute-start(bf16[1280,640]{1,0:T(8,128)(2,1)} %collective-permute-done.1.refs_2_.refs_5_), channel_id=1, source_target_pairs={{4,20},{8,24},{20,4},{24,8},{5,21},{9,25},{21,5},{25,9},{6,22},{10... | collective-permute-start | bytes 4915208 | tf_op jit(solution)/shard_map/ppermute | solution.py:525
  27.1 16.2 %collective-permute-start = (bf16[256,1280]{1,0:T(8,128)(2,1)}, bf16[256,1280]{1,0:T(8,128)(2,1)}, u32[]{:S(2)}, u32[]{:S(2)}) collective-permute-start(bf16[256,1280]{1,0:T(8,128)(2,1)} %self_attention.1.own_ref), channel_id=1, source_target_pairs={{0,8},{4,12},{8,0},{12,4},{16,24},{20,28},{24,16},{28,20},{1,9},{5... | collective-permute-start | bytes 1966088 | tf_op jit(solution)/shard_map/ppermute | solution.py:510
  28.0 26.2 %collective-permute-start.5 = (bf16[1280,640]{1,0:T(8,128)(2,1)}, bf16[1280,640]{1,0:T(8,128)(2,1)}, u32[]{:S(2)}, u32[]{:S(2)}) collective-permute-start(bf16[1280,640]{1,0:T(8,128)(2,1)} %refs_0_.1), channel_id=1, source_target_pairs={{0,4},{12,8},{16,20},{28,24},{1,5},{13,9},{17,21},{29,25},{2,6},{1... | collective-permute-start | bytes 4915208 | tf_op jit(solution)/shard_map/ppermute | solution.py:520
  34.1 20.1 %collective-permute-start.2 = (bf16[1280,640]{1,0:T(8,128)(2,1)}, bf16[1280,640]{1,0:T(8,128)(2,1)}, u32[]{:S(2)}, u32[]{:S(2)}) collective-permute-start(bf16[1280,640]{1,0:T(8,128)(2,1)} %collective-permute-done.1.refs_2_.refs_5_), channel_id=1, source_target_pairs={{0,4},{4,0},{8,12},{12,8},{16,20},{20,16},{24,28},{28,24},{1,5},{5... | collective-permute-start | bytes 4915208 | tf_op jit(solution)/shard_map/ppermute | solution.py:510
  43.3 10.9 %collective-permute-start.4 = (bf16[1280,640]{1,0:T(8,128)(2,1)}, bf16[1280,640]{1,0:T(8,128)(2,1)}, u32[]{:S(2)}, u32[]{:S(2)}) collective-permute-start(bf16[1280,640]{1,0:T(8,128)(2,1)} %collective-permute-done.3.refs_7_), channel_id=1, source_target_pairs={{4,0},{8,12},{20,16},{24,28},{5,1},{9,13},{21,17},{25,29},{6,2},{1... | collective-permute-start | bytes 4915208 | tf_op jit(solution)/shard_map/ppermute | solution.py:543
  45.4 37.3 %collective-permute-start.6 = (bf16[784,640]{1,0:T(8,128)(2,1)}, bf16[784,640]{1,0:T(8,128)(2,1)}, u32[]{:S(2)}, u32[]{:S(2)}) collective-permute-start(bf16[784,640]{1,0:T(8,128)(2,1)} %get-tuple-element.41), channel_id=1, source_target_pairs={{0,16},{4,20},{8,24},{12,28},{16,0},{20,4},{24,8},{28,12},{1,17},{... | collective-permute-start | bytes 3010568 | tf_op jit(solution)/shard_map/ppermute | solution.py:510
  45.9 24.3 %collective-permute-start.7 = (bf16[512,640]{1,0:T(8,128)(2,1)}, bf16[512,640]{1,0:T(8,128)(2,1)}, u32[]{:S(2)}, u32[]{:S(2)}) collective-permute-start(bf16[512,640]{1,0:T(8,128)(2,1)} %get-tuple-element.50.refs_0_), channel_id=1, source_target_pairs={{0,8},{4,12},{8,0},{12,4},{16,24},{20,28},{24,16},{28,20},{1,9},{5... | collective-permute-start | bytes 1966088 | tf_op jit(solution)/shard_map/ppermute | solution.py:510
  54.2 26.5 %collective-permute-start.8 = (bf16[512,640]{1,0:T(8,128)(2,1)}, bf16[512,640]{1,0:T(8,128)(2,1)}, u32[]{:S(2)}, u32[]{:S(2)}) collective-permute-start(bf16[512,640]{1,0:T(8,128)(2,1)} %get-tuple-element.42), channel_id=1, source_target_pairs={{0,24},{4,28},{8,16},{12,20},{16,8},{20,12},{24,0},{28,4},{1,25},{... | collective-permute-start | bytes 1966088 | tf_op jit(solution)/shard_map/ppermute | solution.py:510
  63.5 20.6 %collective-permute-start.9 = (bf16[2,1,256,640]{3,2,1,0:T(8,128)(2,1)}, bf16[2,1,256,640]{3,2,1,0:T(8,128)(2,1)}, u32[]{:S(2)}, u32[]{:S(2)}) collective-permute-start(bf16[2,1,256,640]{3,2,1,0:T(8,128)(2,1)} %get-tuple-element.45), channel_id=1, source_target_pairs={{0,1},{3,2},{4,5},{7,6},{8,9},{11,10},{12,13},{15,14},{16,17},{19,... | collective-permute-start | bytes 1966088 | tf_op jit(solution)/shard_map/ppermute | solution.py:473
  67.8 16.3 %collective-permute-start.10 = (bf16[2,1,256,640]{3,2,1,0:T(8,128)(2,1)}, bf16[2,1,256,640]{3,2,1,0:T(8,128)(2,1)}, u32[]{:S(2)}, u32[]{:S(2)}) collective-permute-start(bf16[2,1,256,640]{3,2,1,0:T(8,128)(2,1)} %get-tuple-element.45), channel_id=1, source_target_pairs={{1,2},{2,1},{5,6},{6,5},{9,10},{10,9},{13,14},{14,13},{17,18},{18,... | collective-permute-start | bytes 1966088 | tf_op jit(solution)/shard_map/ppermute | solution.py:473
  86.3 10.6 %collective-permute-start.14 = (bf16[784,640]{1,0:T(8,128)(2,1)}, bf16[784,640]{1,0:T(8,128)(2,1)}, u32[]{:S(2)}, u32[]{:S(2)}) collective-permute-start(bf16[784,640]{1,0:T(8,128)(2,1)} %collective-permute-done.6.tag_ref.near_ref.refs_1_), channel_id=1, source_target_pairs={{0,4},{4,0},{8,12},{12,8},{16,20},{20,16},{24,28},{28,24},{1,5},{5... | collective-permute-start | bytes 3010568 | tf_op jit(solution)/shard_map/ppermute | solution.py:510
  88.3 3.5 %collective-permute-start.13 = (bf16[512,640]{1,0:T(8,128)(2,1)}, bf16[512,640]{1,0:T(8,128)(2,1)}, u32[]{:S(2)}, u32[]{:S(2)}) collective-permute-start(bf16[512,640]{1,0:T(8,128)(2,1)} %get-tuple-element.50.refs_0_), channel_id=1, source_target_pairs={{0,4},{4,0},{8,12},{12,8},{16,20},{20,16},{24,28},{28,24},{1,5},{5... | collective-permute-start | bytes 1966088 | tf_op jit(solution)/shard_map/ppermute | solution.py:510
  88.4 6.0 %collective-permute-start.15 = (bf16[512,640]{1,0:T(8,128)(2,1)}, bf16[512,640]{1,0:T(8,128)(2,1)}, u32[]{:S(2)}, u32[]{:S(2)}) collective-permute-start(bf16[512,640]{1,0:T(8,128)(2,1)} %collective-permute-done.7.refs_0_.refs_2_), channel_id=1, source_target_pairs={{0,4},{4,0},{8,12},{12,8},{16,20},{20,16},{24,28},{28,24},{1,5},{5... | collective-permute-start | bytes 1966088 | tf_op jit(solution)/shard_map/ppermute | solution.py:510
  88.8 7.2 %collective-permute-start.16 = (bf16[512,640]{1,0:T(8,128)(2,1)}, bf16[512,640]{1,0:T(8,128)(2,1)}, u32[]{:S(2)}, u32[]{:S(2)}) collective-permute-start(bf16[512,640]{1,0:T(8,128)(2,1)} %collective-permute-done.8.refs_1_.refs_3_), channel_id=1, source_target_pairs={{0,4},{4,0},{8,12},{12,8},{16,20},{20,16},{24,28},{28,24},{1,5},{5... | collective-permute-start | bytes 1966088 | tf_op jit(solution)/shard_map/ppermute | solution.py:510
  88.9 16.2 %collective-permute-start.18 = (bf16[1,256,640]{2,1,0:T(8,128)(2,1)}, bf16[1,256,640]{2,1,0:T(8,128)(2,1)}, u32[]{:S(2)}, u32[]{:S(2)}) collective-permute-start(bf16[1,256,640]{2,1,0:T(8,128)(2,1)} %get-tuple-element.57), channel_id=1, source_target_pairs={{0,1},{1,0},{2,3},{3,2},{4,5},{5,4},{6,7},{7,6},{8,9},{9,8},{10,11... | collective-permute-start | bytes 983048 | tf_op jit(solution)/shard_map/ppermute | solution.py:473
  91.8 18.9 %collective-permute-start.19 = (bf16[1,256,640]{2,1,0:T(8,128)(2,1)}, bf16[1,256,640]{2,1,0:T(8,128)(2,1)}, u32[]{:S(2)}, u32[]{:S(2)}) collective-permute-start(bf16[1,256,640]{2,1,0:T(8,128)(2,1)} %get-tuple-element.47), channel_id=1, source_target_pairs={{0,2},{1,3},{2,0},{3,1},{4,6},{5,7},{6,4},{7,5},{8,10},{9,11},{10,... | collective-permute-start | bytes 983048 | tf_op jit(solution)/shard_map/ppermute | solution.py:473
  94.4 24.3 %collective-permute-start.11 = (bf16[1,256,640]{2,1,0:T(8,128)(2,1)}, bf16[1,256,640]{2,1,0:T(8,128)(2,1)}, u32[]{:S(2)}, u32[]{:S(2)}) collective-permute-start(bf16[1,256,640]{2,1,0:T(8,128)(2,1)} %get-tuple-element.48), channel_id=1, source_target_pairs={{0,1},{1,0},{2,3},{3,2},{4,5},{5,4},{6,7},{7,6},{8,9},{9,8},{10,11... | collective-permute-start | bytes 983048 | tf_op jit(solution)/shard_map/ppermute | solution.py:473
  96.0 28.2 %collective-permute-start.12 = (bf16[1,256,640]{2,1,0:T(8,128)(2,1)}, bf16[1,256,640]{2,1,0:T(8,128)(2,1)}, u32[]{:S(2)}, u32[]{:S(2)}) collective-permute-start(bf16[1,256,640]{2,1,0:T(8,128)(2,1)} %get-tuple-element.49), channel_id=1, source_target_pairs={{0,2},{1,3},{2,0},{3,1},{4,6},{5,7},{6,4},{7,5},{8,10},{9,11},{10,... | collective-permute-start | bytes 983048 | tf_op jit(solution)/shard_map/ppermute | solution.py:473
  103.1 10.0 %collective-permute-start.17 = (bf16[256,640]{1,0:T(8,128)(2,1)}, bf16[256,640]{1,0:T(8,128)(2,1)}, u32[]{:S(2)}, u32[]{:S(2)}) collective-permute-start(bf16[256,640]{1,0:T(8,128)(2,1)} %get-tuple-element.55), channel_id=1, source_target_pairs={{0,16},{4,20},{8,24},{12,28},{16,0},{20,4},{24,8},{28,12},{1,17},{... | collective-permute-start | bytes 983048 | tf_op jit(solution)/shard_map/ppermute | solution.py:510
  112.9 11.8 %collective-permute-start.20 = (bf16[1,256,640]{2,1,0:T(8,128)(2,1)}, bf16[1,256,640]{2,1,0:T(8,128)(2,1)}, u32[]{:S(2)}, u32[]{:S(2)}) collective-permute-start(bf16[1,256,640]{2,1,0:T(8,128)(2,1)} %add.25), channel_id=1, source_target_pairs={{0,8},{4,12},{8,0},{12,4},{16,24},{20,28},{24,16},{28,20},{1,9},{5... | collective-permute-start | bytes 983048 | tf_op jit(solution)/shard_map/ppermute | solution.py:510

commit v6 on v5

--- a/solution.py
+++ b/solution.py
@@ -67,7 +67,7 @@
     block_rows, heads, length_ref, q_ref, kn_ref, vn_ref, kc_ref, vc_ref, o_ref, top_ref, total_ref
 ):
     step, steps = pl.program_id(0), pl.num_programs(0)
-    left = length_ref[0] - step * block_rows
+    left = length_ref[lax.axis_index("req")] - step * block_rows
     rows, new_rows = q_ref.shape[0], kn_ref.shape[0]
 
     @pl.when(step == 0)
@@ -107,16 +107,19 @@
         visit(kn_ref, vn_ref, key_ids <= query_ids, True)
 
 
-def self_attention(queries, new_keys, new_values, keys, values, length):
+def self_attention(queries, new_keys, new_values, keys, values, lengths):
     rows, width = queries.shape
     new_rows, capacity = new_keys.shape[0], keys.shape[0]
     block_rows = min(CACHE_BLOCK, capacity)
     heads = width // HD
     whole = pl.BlockSpec((rows, width), lambda i, n: (0, 0))
     new = pl.BlockSpec((new_rows, width), lambda i, n: (0, 0))
-    cached = pl.BlockSpec(
-        (block_rows, width), lambda i, n: (jnp.minimum(i, (n[0] - 1) // block_rows), 0)
-    )
+
+    def live_block(step, length_ref):
+        length = length_ref[lax.axis_index("req")]
+        return jnp.minimum(step, lax.div(length - 1, block_rows)), 0
+
+    cached = pl.BlockSpec((block_rows, width), live_block)
     return pl.pallas_call(
         functools.partial(self_kernel, block_rows, heads),
         grid_spec=pltpu.PrefetchScalarGridSpec(
@@ -133,7 +136,7 @@
         compiler_params=pltpu.CompilerParams(vmem_limit_bytes=VMEM_LIMIT),
         cost_estimate=cost_of(20e-6),
         name="self_attention",
-    )(length.reshape(1), queries, new_keys, new_values, keys, values)
+    )(lengths, queries, new_keys, new_values, keys, values)
 
 
 def cross_kernel(heads, pieces_count, spans, prompts_ref, side_ref, q_ref, near_ref, *refs):
@@ -282,11 +285,13 @@
     )(queries, keys, values)
 
 
-def project_kernel(count, span, places, joint, place_ref, own_ref, near_ref, *refs):
+def project_kernel(count, flat, places, joint, own_ref, near_ref, *refs):
     held, passed = refs[:count], refs[count : 2 * count]
     outs = refs[2 * count : -6]
     x_ref, weights, terms, x_sems, sems, out_sems = refs[-6:]
-    chip, holder, at_tp = place_ref[0], place_ref[1], place_ref[2]
+    place, at_tp = lax.axis_index("req"), lax.axis_index("tp")
+    chip = lax.div(place, 2)
+    holder = lax.rem(place, 2) == lax.rem(chip, 2)
     rows, columns = own_ref.shape[0], held[0].shape[1]
     blocks = outs[0].shape[0]
     if joint:
@@ -299,64 +304,77 @@
         )
 
     def weights_in(choice, at):
-        first = (at % span) * columns
-        place = weights.at[at // span, :, first : first + columns]
-        return pltpu.make_async_copy(choice[at], place, sems.at[at])
+        target = weights.at[:, at * columns : (at + 1) * columns] if flat else weights.at[at]
+        return pltpu.make_async_copy(choice[at], target, sems.at[at])
 
     def terms_out(at, part, distance, block):
+        if flat:
+            source = terms.at[part, :, at * columns : (at + 1) * columns]
+        else:
+            source = terms.at[at, part]
         target = outs[part * places + distance].at[block]
-        return pltpu.make_async_copy(terms.at[at, part], target, out_sems.at[at, part])
+        return pltpu.make_async_copy(source, target, out_sems.at[at, part])
+
+    def send(at):
+        source = chip ^ at
+        block = lax.rem(source, blocks)
+        away = lax.div(source, blocks) ^ at_tp
+        for distance in range(places):
+
+            @pl.when(away == distance)
+            def _(at=at, distance=distance, block=block):
+                for part in range(2):
+                    terms_out(at, part, distance, block).start()
 
     for part in range(2):
         rows_in(part).start()
 
-    @pl.when(holder == 1)
+    @pl.when(holder)
     def _():
         for at in range(count):
             weights_in(held, at).start()
 
-    @pl.when(holder == 0)
+    @pl.when(jnp.logical_not(holder))
     def _():
         for at in range(count):
             weights_in(passed, at).start()
 
     for part in range(2):
         rows_in(part).wait()
-    for first in range(0, count, span):
-        for at in range(first, first + span):
-            weights_in(held, at).wait()
-        product = jnp.dot(
-            x_ref[...], weights[first // span], preferred_element_type=jnp.float32
-        ).astype(terms.dtype)
-        for at in range(first, first + span):
-            cols = slice((at - first) * columns, (at - first + 1) * columns)
-            source = chip ^ at
-            block = lax.rem(source, blocks)
-            away = lax.div(source, blocks) ^ at_tp
-            for part in range(2):
-                terms[at, part] = product[part * rows : (part + 1) * rows, cols]
-            for distance in range(places):
-
-                @pl.when(away == distance)
-                def _(at=at, distance=distance, block=block):
-                    for part in range(2):
-                        terms_out(at, part, distance, block).start()
+    there = sent = 0
+    for first in range(0, count * columns, flat or columns):
+        last = first + (flat or columns)
+        while there * columns < last:
+            weights_in(held, there).wait()
+            there += 1
+        block_weights = weights[:, first:last] if flat else weights[first // columns]
+        product = jnp.dot(x_ref[...], block_weights, preferred_element_type=jnp.float32)
+        product = product.astype(terms.dtype)
+        for part in range(2):
+            piece = product[part * rows : (part + 1) * rows]
+            if flat:
+                terms[part, :, first:last] = piece
+            else:
+                terms[first // columns, part] = piece
+        while (sent + 1) * columns <= last:
+            send(sent)
+            sent += 1
 
     for at in range(count):
         for part in range(2):
             terms_out(at, part, 0, 0).wait()
 
 
-def project(tps, place, own, near, held, passed, joint):
+def project(tps, own, near, held, passed, joint):
     rows = own.shape[0]
     depth, columns = held[0].shape
     count = len(held)
-    span = 2 if columns % HD == 0 else 1
+    flat = 512 if columns % HD == 0 and count * columns % 512 == 0 else 0
     hbm = pl.BlockSpec(memory_space=pltpu.HBM)
     out = jax.ShapeDtypeStruct((count // tps, rows, columns), jnp.bfloat16)
     return pl.pallas_call(
-        functools.partial(project_kernel, count, span, tps, joint),
-        in_specs=[pl.BlockSpec(memory_space=pltpu.SMEM)] + [hbm] * (2 + 2 * count),
+        functools.partial(project_kernel, count, flat, tps, joint),
+        in_specs=[hbm] * (2 + 2 * count),
         out_specs=[hbm] * (2 * tps - joint),
         out_shape=(
             [out] * (2 * tps - 2) + [jax.ShapeDtypeStruct((2, *out.shape), out.dtype)]
@@ -365,8 +383,10 @@
         ),
         scratch_shapes=[
             pltpu.VMEM((2 * rows, depth), jnp.bfloat16),
-            pltpu.VMEM((count // span, depth, span * columns), jnp.bfloat16),
-            pltpu.VMEM((count, 2, rows, columns), jnp.bfloat16),
+            pltpu.VMEM((depth, count * columns) if flat else (count, depth, columns), jnp.bfloat16),
+            pltpu.VMEM(
+                (2, rows, count * columns) if flat else (count, 2, rows, columns), jnp.bfloat16
+            ),
             pltpu.SemaphoreType.DMA((2,)),
             pltpu.SemaphoreType.DMA((count,)),
             pltpu.SemaphoreType.DMA((count, 2)),
@@ -374,7 +394,7 @@
         compiler_params=pltpu.CompilerParams(vmem_limit_bytes=VMEM_LIMIT),
         cost_estimate=cost_of(10e-6),
         name="project",
-    )(place, own, near, *held, *passed)
+    )(own, near, *held, *passed)
 
 
 def fetch(sources, scratch, sems):
@@ -437,36 +457,63 @@
     )(near, own, far)
 
 
-def finish_kernel(halves, side_ref, hidden_ref, *refs):
-    o_ref, scratch, sems = refs[-3:]
+def finish_kernel(halves, side_ref, hidden_ref, received_ref, *refs):
+    o_ref, rest, kept_part, near_part, parts, sems, out_sems = refs[-7:]
     sources = [ref if half is None else ref.at[half] for ref, half in zip(refs, halves)]
-    received, *parts = fetch(sources, scratch, sems)
-    half = received.shape[2]
+    half = received_ref.shape[2]
     kept = pl.ds(pl.multiple_of(side_ref[0] * half, HD), half)
     other = pl.ds(pl.multiple_of((1 - side_ref[0]) * half, HD), half)
-    o_ref[:, other] = (hidden_ref[:, other].astype(jnp.float32) + received[0]).astype(o_ref.dtype)
-    o_ref[:, kept] = (hidden_ref[:, kept].astype(jnp.float32) + sum(parts)[0]).astype(o_ref.dtype)
+    copies = [
+        pltpu.make_async_copy(hidden_ref.at[:, other], rest.at[0], sems.at[0]),
+        pltpu.make_async_copy(received_ref.at[0], near_part, sems.at[1]),
+        pltpu.make_async_copy(hidden_ref.at[:, kept], rest.at[1], sems.at[2]),
+    ] + [
+        pltpu.make_async_copy(source.at[0], parts.at[at], sems.at[3 + at])
+        for at, source in enumerate(sources)
+    ]
+    for copy in copies:
+        copy.start()
+    for copy in copies[:2]:
+        copy.wait()
+    near_part[...] = (
+        rest[0].astype(jnp.float32) + near_part[...].astype(jnp.float32)
+    ).astype(near_part.dtype)
+    outs = [pltpu.make_async_copy(near_part, o_ref.at[:, other], out_sems.at[0])]
+    outs[0].start()
+    for copy in copies[2:]:
+        copy.wait()
+    total = rest[1].astype(jnp.float32)
+    for at in range(len(sources)):
+        total += parts[at].astype(jnp.float32)
+    kept_part[...] = total.astype(kept_part.dtype)
+    outs.append(pltpu.make_async_copy(kept_part, o_ref.at[:, kept], out_sems.at[1]))
+    outs[1].start()
+    for copy in outs:
+        copy.wait()
 
 
 def finish(side, hidden, received, parts):
-    terms = [received, *parts]
-    halves = tuple(term[1] if isinstance(term, tuple) else None for term in terms)
-    terms = [term[0] if isinstance(term, tuple) else term for term in terms]
-    vmem = pl.BlockSpec(memory_space=pltpu.VMEM)
+    halves = tuple(part[1] if isinstance(part, tuple) else None for part in parts)
+    parts = [part[0] if isinstance(part, tuple) else part for part in parts]
     hbm = pl.BlockSpec(memory_space=pltpu.HBM)
+    half = received.shape[1:]
     return pl.pallas_call(
         functools.partial(finish_kernel, halves),
-        in_specs=[pl.BlockSpec(memory_space=pltpu.SMEM), vmem] + [hbm] * len(terms),
-        out_specs=vmem,
+        in_specs=[pl.BlockSpec(memory_space=pltpu.SMEM)] + [hbm] * (2 + len(parts)),
+        out_specs=hbm,
         out_shape=jax.ShapeDtypeStruct(hidden.shape, hidden.dtype),
         scratch_shapes=[
-            pltpu.VMEM((len(terms),) + received.shape, received.dtype),
-            pltpu.SemaphoreType.DMA((len(terms),)),
+            pltpu.VMEM((2, *half), hidden.dtype),
+            pltpu.VMEM(half, hidden.dtype),
+            pltpu.VMEM(half, hidden.dtype),
+            pltpu.VMEM((len(parts), *half), hidden.dtype),
+            pltpu.SemaphoreType.DMA((3 + len(parts),)),
+            pltpu.SemaphoreType.DMA((2,)),
         ],
         compiler_params=pltpu.CompilerParams(vmem_limit_bytes=VMEM_LIMIT),
         cost_estimate=cost_of(2e-6),
         name="finish",
-    )(side.reshape(1), hidden, *terms)
+    )(side.reshape(1), hidden, received, *parts)
 
 
 def to_tp(value, pairs):
@@ -500,11 +547,9 @@
     rows, width = q_new.shape
     chips = reqs // 2
     place = lax.axis_index("req")
-    chip, core = place // 2, place % 2
+    chip = place // 2
     side = chip % 2
     text_side = (chip // 2) % 2
-    holder = core == side
-    length = lax.dynamic_index_in_dim(cache_len, place, 0, keepdims=False)
 
     def swap(array, distance):
         return lax.ppermute(array, "req", [(i, i ^ distance) for i in range(reqs)])
@@ -519,7 +564,7 @@
     )
     own_passed = lax.ppermute(w_out, "req", list(zip(first_of, second_of)))
 
-    own = self_attention(q_new, k_new, v_new, cache_k[0], cache_v[0], length)
+    own = self_attention(q_new, k_new, v_new, cache_k[0], cache_v[0], cache_len)
     near = swap(own, 2)
     beside = after(beside, own)
     across = lax.ppermute(
@@ -548,9 +593,6 @@
         held += [swap(block, 2 * bit) for block in held]
         passed += [swap(block, 2 * bit) for block in passed]
         bit *= 2
-    at = lax.axis_index("tp")
-    order = jnp.stack([chip, holder, at]).astype(jnp.int32)
-
     def in_order(side, kept, received, axis):
         return jnp.where(
             side == 0,
@@ -559,7 +601,7 @@
         )
 
     line = split_heads and tps == 4 and chips == 4
-    terms = project(tps, order, own, near, held, passed, line)
+    terms = project(tps, own, near, held, passed, line)
     if line:
         near_terms, own_terms, last = terms[:3], terms[3:6], terms[6]
         far, inner = to_tp(last, [(0, 1), (3, 2)]), to_tp(last, [(1, 2), (2, 1)])

time: 130 us -> 128 us (0.985)
  Pallas kernels: 49.3 us -> 35.9 us
  waiting for transfers between devices: 39.9 us -> 50.4 us
  starting transfers between devices: 34.2 us -> 37.3 us
    pallas_call x1, Pallas kernels: 20.4 us -> 10.4 us  [self_attention(): pl.pallas_call(functools.partial(self_kernel, block_rows, heads), grid_sp...]
    ppermute x1, waiting for transfers between devices: 0.01 us -> 9.01 us  [per_device(): lax.ppermute(w_out, 'req', [(first_of[i], first_of[i ^ 2]) for i in range...]
    ppermute x11, starting transfers between devices: 12.8 us -> 15.8 us  [swap(): return lax.ppermute(array, 'req', [(i, i ^ distance) for i in range(reqs)])]
    ppermute x11, waiting for transfers between devices: 23.9 us -> 26.5 us  [swap(): return lax.ppermute(array, 'req', [(i, i ^ distance) for i in range(reqs)])]
    pallas_call x1, Pallas kernels: 9.27 us -> 6.86 us  [project(): pl.pallas_call(functools.partial(project_kernel, count, flat, tps, joint)...]
  transfers between devices with their start and end apart: 21 -> 21, of which waited for: 9 -> 10; matrix products, arithmetic and copies ran while one was open for 3% -> 2% of each run, Pallas kernels for 33% -> 24%
where the time goes in v6:
time: 128 us
  waiting for transfers between devices  50.4 us (39%)
  starting transfers between devices  37.3 us (29%)
  Pallas kernels  35.9 us (28%)
  other arithmetic  2.3 us (2%)
  between operations  1.55 us (1%)
    ppermute x11, waiting for transfers between devices, swap(): return lax.ppermute(array, 'req', [(i, i ^ distance) for i in range(reqs)])  26.5 us
    ppermute x11, starting transfers between devices, swap(): return lax.ppermute(array, 'req', [(i, i ^ distance) for i in range(reqs)])  15.8 us
    ppermute x6, waiting for transfers between devices, to_tp(): return lax.ppermute(value, 'tp', pairs)  14.9 us
    ppermute x6, starting transfers between devices, to_tp(): return lax.ppermute(value, 'tp', pairs)  12.6 us
    pallas_call x1, Pallas kernels, self_attention(): pl.pallas_call(functools.partial(self_kernel, block_rows, heads), grid_sp...  10.4 us
    ppermute x1, waiting for transfers between devices, per_device(): lax.ppermute(w_out, 'req', [(first_of[i], first_of[i ^ 2]) for i in range...  9.01 us
    pallas_call x1, Pallas kernels, project(): pl.pallas_call(functools.partial(project_kernel, count, flat, tps, joint)...  6.86 us
    pallas_call x1, Pallas kernels, cross_attention(): pl.pallas_call(functools.partial(cross_kernel, half // HD, len(pieces), s...  6.11 us
  transfers between devices with their start and end apart: 21, of which 10 were waited for; matrix products, arithmetic and copies ran while one was open for 2% of the time, Pallas kernels for 24%

profile of v6, /device:TPU:0, one launch (start us, length us, event | category | flops | bytes accessed | tf_op | source)
XLA Modules:
  0.0 127.5 jit_solution(7394773746845616229)
XLA Ops:
  0.6 3.0 %collective-permute-start.1 = (bf16[1280,640]{1,0:T(8,128)(2,1)}, bf16[1280,640]{1,0:T(8,128)(2,1)}, u32[]{:S(2)}, u32[]{:S(2)}) collective-permute-start(bf16[1280,640]{1,0:T(8,128)(2,1)} %refs_0_.1), channel_id=1, source_target_pairs={{0,16},{12,28},{16,0},{28,12},{4,8},{8,4},{20,24},{24,20},{1,17},{... | collective-permute-start | bytes 4915208 | tf_op jit(solution)/shard_map/ppermute | solution.py:559
  3.7 10.4 %self_attention.1.own_ref = bf16[256,1280]{1,0:T(8,128)(2,1)} custom-call(s32[8]{0:T(128)} %length_ref.1, bf16[256,1280]{1,0:T(8,128)(2,1)} %q_ref.2, bf16[256,1280]{1,0:T(8,128)(2,1)} %kn_ref.1, bf16[256,1280]{1,0:T(8,128)(2,1)} %vn_ref.1, bf16[4096,1280]{1,0:T(8,128)(2,1)} %bitcast.4, bf16[4096,1280]{1,0:T(8,128)(2,1)} %bitcast.5), custom_call_target="tpu_custom_call" | custom-call | flops 23069999104 | tf_op jit(solution)/shard_map/self_attention/pallas_call | solution.py:123
  14.1 9.0 %collective-permute-done.1.refs_2_.refs_5_ = bf16[1280,640]{1,0:T(8,128)(2,1)} collective-permute-done((bf16[1280,640]{1,0:T(8,128)(2,1)}, bf16[1280,640]{1,0:T(8,128)(2,1)}, u32[]{:S(2)}, u32[]{:S(2)}) %collective-permute-start.1) | collective-permute-done | bytes 1638432 | tf_op jit(solution)/shard_map/ppermute | solution.py:559
  23.1 1.8 %collective-permute-start.3 = (bf16[1280,640]{1,0:T(8,128)(2,1)}, bf16[1280,640]{1,0:T(8,128)(2,1)}, u32[]{:S(2)}, u32[]{:S(2)}) collective-permute-start(bf16[1280,640]{1,0:T(8,128)(2,1)} %collective-permute-done.1.refs_2_.refs_5_), channel_id=1, source_target_pairs={{4,20},{8,24},{20,4},{24,8},{5,21},{9,25},{21,5},{25,9},{6,22},{10... | collective-permute-start | bytes 4915208 | tf_op jit(solution)/shard_map/ppermute | solution.py:570
  24.9 3.1 %collective-permute-start = (bf16[256,1280]{1,0:T(8,128)(2,1)}, bf16[256,1280]{1,0:T(8,128)(2,1)}, u32[]{:S(2)}, u32[]{:S(2)}) collective-permute-start(bf16[256,1280]{1,0:T(8,128)(2,1)} %self_attention.1.own_ref), channel_id=1, source_target_pairs={{0,8},{4,12},{8,0},{12,4},{16,24},{20,28},{24,16},{28,20},{1,9},{5... | collective-permute-start | bytes 1966088 | tf_op jit(solution)/shard_map/ppermute | solution.py:555
  28.0 2.7 %collective-permute-start.5 = (bf16[1280,640]{1,0:T(8,128)(2,1)}, bf16[1280,640]{1,0:T(8,128)(2,1)}, u32[]{:S(2)}, u32[]{:S(2)}) collective-permute-start(bf16[1280,640]{1,0:T(8,128)(2,1)} %refs_0_.1), channel_id=1, source_target_pairs={{0,4},{12,8},{16,20},{28,24},{1,5},{13,9},{17,21},{29,25},{2,6},{1... | collective-permute-start | bytes 4915208 | tf_op jit(solution)/shard_map/ppermute | solution.py:565
  31.3 3.0 %pack.1 = (bf16[512,640]{1,0:T(8,128)(2,1)}, bf16[512,640]{1,0:T(8,128)(2,1)}, bf16[784,640]{1,0:T(8,128)(2,1)}) custom-call(s32[1]{0:T(128)} %bitcast.3.side_ref, s32[1]{0:T(128)S(6)} %copy.14.prompt_ref, bf16[4,64,1280]{2,1,0:T(8,128)(2,1)} %k_ref.1, bf16[4,64,1280]{2,1,0:T(8,128)(2,1)} %v_ref.1, bf16[256,1280]{1,0:T(8,128)(2,1)} %q_ref.4), custom_call_target="tpu_custom_call" | custom-call | flops 3460499968 | tf_op jit(solution)/shard_map/pack/pallas_call | solution.py:249
  34.4 8.9 %collective-permute-done.near_ref = bf16[256,1280]{1,0:T(8,128)(2,1)} collective-permute-done((bf16[256,1280]{1,0:T(8,128)(2,1)}, bf16[256,1280]{1,0:T(8,128)(2,1)}, u32[]{:S(2)}, u32[]{:S(2)}) %collective-permute-start) | collective-permute-done | bytes 655392 | tf_op jit(solution)/shard_map/ppermute | solution.py:555
  44.8 1.6 %collective-permute-start.6 = (bf16[784,640]{1,0:T(8,128)(2,1)}, bf16[784,640]{1,0:T(8,128)(2,1)}, u32[]{:S(2)}, u32[]{:S(2)}) collective-permute-start(bf16[784,640]{1,0:T(8,128)(2,1)} %get-tuple-element.41), channel_id=1, source_target_pairs={{0,16},{4,20},{8,24},{12,28},{16,0},{20,4},{24,8},{28,12},{1,17},{... | collective-permute-start | bytes 3010568 | tf_op jit(solution)/shard_map/ppermute | solution.py:555
  46.4 5.8 %collective-permute-start.7 = (bf16[512,640]{1,0:T(8,128)(2,1)}, bf16[512,640]{1,0:T(8,128)(2,1)}, u32[]{:S(2)}, u32[]{:S(2)}) collective-permute-start(bf16[512,640]{1,0:T(8,128)(2,1)} %get-tuple-element.50.refs_0_), channel_id=1, source_target_pairs={{0,8},{4,12},{8,0},{12,4},{16,24},{20,28},{24,16},{28,20},{1,9},{5... | collective-permute-start | bytes 1966088 | tf_op jit(solution)/shard_map/ppermute | solution.py:555
  52.2 6.9 %project.1 = (bf16[1,256,640]{2,1,0:T(8,128)(2,1)}, bf16[1,256,640]{2,1,0:T(8,128)(2,1)}, bf16[1,256,640]{2,1,0:T(8,128)(2,1)}, bf16[1,256,640]{2,1,0:T(8,128)(2...) custom-call(bf16[256,1280]{1,0:T(8,128)(2,1)} %self_attention.1.own_ref, ...), custom_call_target="tpu_custom_call" | custom-call | flops 11534999552 | tf_op jit(solution)/shard_map/project/pallas_call | solution.py:375
  59.1 4.3 %collective-permute-start.9 = (bf16[2,1,256,640]{3,2,1,0:T(8,128)(2,1)}, bf16[2,1,256,640]{3,2,1,0:T(8,128)(2,1)}, u32[]{:S(2)}, u32[]{:S(2)}) collective-permute-start(bf16[2,1,256,640]{3,2,1,0:T(8,128)(2,1)} %get-tuple-element.45), channel_id=1, source_target_pairs={{0,1},{3,2},{4,5},{7,6},{8,9},{11,10},{12,13},{15,14},{16,17},{19,... | collective-permute-start | bytes 1966088 | tf_op jit(solution)/shard_map/ppermute | solution.py:520
  65.0 3.1 %collective-permute-done.7.refs_0_.refs_2_ = bf16[512,640]{1,0:T(8,128)(2,1)} collective-permute-done((bf16[512,640]{1,0:T(8,128)(2,1)}, bf16[512,640]{1,0:T(8,128)(2,1)}, u32[]{:S(2)}, u32[]{:S(2)}) %collective-permute-start.7) | collective-permute-done | bytes 655392 | tf_op jit(solution)/shard_map/ppermute | solution.py:555
  68.1 13.0 %collective-permute-done.8.refs_1_.refs_3_ = bf16[512,640]{1,0:T(8,128)(2,1)} collective-permute-done((bf16[512,640]{1,0:T(8,128)(2,1)}, bf16[512,640]{1,0:T(8,128)(2,1)}, u32[]{:S(2)}, u32[]{:S(2)}) %collective-permute-start.8) | collective-permute-done | bytes 655392 | tf_op jit(solution)/shard_map/ppermute | solution.py:555
  82.6 2.2 %join.1 = (bf16[1,256,640]{2,1,0:T(8,128)(2,1)}, bf16[1,256,640]{2,1,0:T(8,128)(2,1)}) custom-call(bf16[1,256,640]{2,1,0:T(8,128)(2,1)} %get-tuple-element.43.near_ref, bf16[1,256,640]{2,1,0:T(8,128)(2,1)} %get-tuple-element.44.own_ref, bf16[2,1,256,640]{3,2,1,0:T(8,128)(2,1)} %collective-permute-done.9.far_ref), custom_call_target="tpu_custom_call" | custom-call | flops 2307000064 | tf_op jit(solution)/shard_map/join/pallas_call | solution.py:445
  84.8 3.0 %collective-permute-start.14 = (bf16[784,640]{1,0:T(8,128)(2,1)}, bf16[784,640]{1,0:T(8,128)(2,1)}, u32[]{:S(2)}, u32[]{:S(2)}) collective-permute-start(bf16[784,640]{1,0:T(8,128)(2,1)} %collective-permute-done.6.tag_ref.near_ref.refs_1_), channel_id=1, source_target_pairs={{0,4},{4,0},{8,12},{12,8},{16,20},{20,16},{24,28},{28,24},{1,5},{5... | collective-permute-start | bytes 3010568 | tf_op jit(solution)/shard_map/ppermute | solution.py:555
  91.3 2.6 %collective-permute-start.19 = (bf16[1,256,640]{2,1,0:T(8,128)(2,1)}, bf16[1,256,640]{2,1,0:T(8,128)(2,1)}, u32[]{:S(2)}, u32[]{:S(2)}) collective-permute-start(bf16[1,256,640]{2,1,0:T(8,128)(2,1)} %get-tuple-element.47), channel_id=1, source_target_pairs={{0,2},{1,3},{2,0},{3,1},{4,6},{5,7},{6,4},{7,5},{8,10},{9,11},{10,... | collective-permute-start | bytes 983048 | tf_op jit(solution)/shard_map/ppermute | solution.py:520
  96.4 6.1 %cross_attention.1 = (bf16[256,640]{1,0:T(8,128)(2,1)}, bf16[256,640]{1,0:T(8,128)(2,1)}) custom-call(s32[2]{0:T(128)} %read_prompts.1.prompts_ref, s32[1]{0:T(128)} %bitcast.3.side_ref, bf16[256,1280]{1,0:T(8,128)(2,1)} %q_ref.4, bf16[784,640]{1,0:T(8,128)(2,1)} %collective-permute-done.6.tag_ref.near_ref.refs_1_, ...), custom_call_target="tpu_custom_call" | custom-call | tf_op jit(solution)/shard_map/cross_attention/pallas_call | solution.py:177
  104.6 5.7 %collective-permute-done.19.refs_3_ = bf16[1,256,640]{2,1,0:T(8,128)(2,1)} collective-permute-done((bf16[1,256,640]{2,1,0:T(8,128)(2,1)}, bf16[1,256,640]{2,1,0:T(8,128)(2,1)}, u32[]{:S(2)}, u32[]{:S(2)}) %collective-permute-start.19) | collective-permute-done | bytes 327712 | tf_op jit(solution)/shard_map/ppermute | solution.py:520
  110.2 2.2 %add.12 = bf16[1,256,640]{2,1,0:T(8,128)(2,1)} custom-call(bf16[1,256,640]{2,1,0:T(8,128)(2,1)} %get-tuple-element.56.refs_0_, bf16[2,1,256,640]{3,2,1,0:T(8,128)(2,1)} %collective-permute-done.10.refs_1_, bf16[1,256,640]{2,1,0:T(8,128)(2,1)} %collective-permute-done.18.refs_2_, bf16[1,256,640]{2,1,0:T(8,128)(2,1)} %collective-permute-done.19.refs_3_), custom_call_target="tpu_custom_call" | custom-call | flops 115350003712 | tf_op jit(solution)/shard_map/add/pallas_call | solution.py:422
  112.6 2.3 %maximum_select_fusion.refs_2_ = bf16[256,1280]{1,0:T(8,128)(2,1)} fusion(bf16[256,640]{1,0:T(8,128)(2,1)} %collective-permute-done.17, bf16[256,640]{1,0:T(8,128)(2,1)} %get-tuple-element.54, pred[]{:T(512)S(6)} %eq.6), kind=kLoop, calls=%fused_computation | loop fusion | flops 2949120 | bytes 1310721 | tf_op jit(solution)/shard_map/jit(_where)/select_n | solution.py:597
  114.9 3.3 %collective-permute-done.11.refs_0_.refs_2_ = bf16[1,256,640]{2,1,0:T(8,128)(2,1)} collective-permute-done((bf16[1,256,640]{2,1,0:T(8,128)(2,1)}, bf16[1,256,640]{2,1,0:T(8,128)(2,1)}, u32[]{:S(2)}, u32[]{:S(2)}) %collective-permute-start.11) | collective-permute-done | bytes 327712 | tf_op jit(solution)/shard_map/ppermute | solution.py:520
  118.1 5.5 %collective-permute-done.12.refs_1_.refs_3_ = bf16[1,256,640]{2,1,0:T(8,128)(2,1)} collective-permute-done((bf16[1,256,640]{2,1,0:T(8,128)(2,1)}, bf16[1,256,640]{2,1,0:T(8,128)(2,1)}, u32[]{:S(2)}, u32[]{:S(2)}) %collective-permute-start.12) | collective-permute-done | bytes 327712 | tf_op jit(solution)/shard_map/ppermute | solution.py:520
  124.2 3.2 %finish.1 = bf16[256,1280]{1,0:T(8,128)(2,1)} custom-call(s32[1]{0:T(128)} %gate.1.side_ref, bf16[256,1280]{1,0:T(8,128)(2,1)} %hidden_ref.1, bf16[1,256,640]{2,1,0:T(8,128)(2,1)} %collective-permute-done.20.received_ref, bf16[1,256,640]{2,1,0:T(8,128)(2,1)} %get-tuple-element.59.refs_0_, bf16[2,1,256,640]{3,2,1,0:T(8,128)(2,1)} %collective-permute-done.10.refs_1_, ...), custom_call_target="tpu_custom_call" | custom-call | flops 2307000064 | tf_op jit(solution)/shard_map/finish/pallas_call | solution.py:500
  (28 shorter events, 13.2 us)
Async XLA Ops:
  0.6 22.4 %collective-permute-start.1 = (bf16[1280,640]{1,0:T(8,128)(2,1)}, bf16[1280,640]{1,0:T(8,128)(2,1)}, u32[]{:S(2)}, u32[]{:S(2)}) collective-permute-start(bf16[1280,640]{1,0:T(8,128)(2,1)} %refs_0_.1), channel_id=1, source_target_pairs={{0,16},{12,28},{16,0},{28,12},{4,8},{8,4},{20,24},{24,20},{1,17},{... | collective-permute-start | bytes 4915208 | tf_op jit(solution)/shard_map/ppermute | solution.py:559
  23.1 11.3 %collective-permute-start.3 = (bf16[1280,640]{1,0:T(8,128)(2,1)}, bf16[1280,640]{1,0:T(8,128)(2,1)}, u32[]{:S(2)}, u32[]{:S(2)}) collective-permute-start(bf16[1280,640]{1,0:T(8,128)(2,1)} %collective-permute-done.1.refs_2_.refs_5_), channel_id=1, source_target_pairs={{4,20},{8,24},{20,4},{24,8},{5,21},{9,25},{21,5},{25,9},{6,22},{10... | collective-permute-start | bytes 4915208 | tf_op jit(solution)/shard_map/ppermute | solution.py:570
  24.9 18.4 %collective-permute-start = (bf16[256,1280]{1,0:T(8,128)(2,1)}, bf16[256,1280]{1,0:T(8,128)(2,1)}, u32[]{:S(2)}, u32[]{:S(2)}) collective-permute-start(bf16[256,1280]{1,0:T(8,128)(2,1)} %self_attention.1.own_ref), channel_id=1, source_target_pairs={{0,8},{4,12},{8,0},{12,4},{16,24},{20,28},{24,16},{28,20},{1,9},{5... | collective-permute-start | bytes 1966088 | tf_op jit(solution)/shard_map/ppermute | solution.py:555
  28.0 24.2 %collective-permute-start.5 = (bf16[1280,640]{1,0:T(8,128)(2,1)}, bf16[1280,640]{1,0:T(8,128)(2,1)}, u32[]{:S(2)}, u32[]{:S(2)}) collective-permute-start(bf16[1280,640]{1,0:T(8,128)(2,1)} %refs_0_.1), channel_id=1, source_target_pairs={{0,4},{12,8},{16,20},{28,24},{1,5},{13,9},{17,21},{29,25},{2,6},{1... | collective-permute-start | bytes 4915208 | tf_op jit(solution)/shard_map/ppermute | solution.py:565
  34.4 17.8 %collective-permute-start.2 = (bf16[1280,640]{1,0:T(8,128)(2,1)}, bf16[1280,640]{1,0:T(8,128)(2,1)}, u32[]{:S(2)}, u32[]{:S(2)}) collective-permute-start(bf16[1280,640]{1,0:T(8,128)(2,1)} %collective-permute-done.1.refs_2_.refs_5_), channel_id=1, source_target_pairs={{0,4},{4,0},{8,12},{12,8},{16,20},{20,16},{24,28},{28,24},{1,5},{5... | collective-permute-start | bytes 4915208 | tf_op jit(solution)/shard_map/ppermute | solution.py:555
  43.3 8.9 %collective-permute-start.4 = (bf16[1280,640]{1,0:T(8,128)(2,1)}, bf16[1280,640]{1,0:T(8,128)(2,1)}, u32[]{:S(2)}, u32[]{:S(2)}) collective-permute-start(bf16[1280,640]{1,0:T(8,128)(2,1)} %collective-permute-done.3.refs_7_), channel_id=1, source_target_pairs={{4,0},{8,12},{20,16},{24,28},{5,1},{9,13},{21,17},{25,29},{6,2},{1... | collective-permute-start | bytes 4915208 | tf_op jit(solution)/shard_map/ppermute | solution.py:588
  44.8 36.4 %collective-permute-start.6 = (bf16[784,640]{1,0:T(8,128)(2,1)}, bf16[784,640]{1,0:T(8,128)(2,1)}, u32[]{:S(2)}, u32[]{:S(2)}) collective-permute-start(bf16[784,640]{1,0:T(8,128)(2,1)} %get-tuple-element.41), channel_id=1, source_target_pairs={{0,16},{4,20},{8,24},{12,28},{16,0},{20,4},{24,8},{28,12},{1,17},{... | collective-permute-start | bytes 3010568 | tf_op jit(solution)/shard_map/ppermute | solution.py:555
  46.4 21.7 %collective-permute-start.7 = (bf16[512,640]{1,0:T(8,128)(2,1)}, bf16[512,640]{1,0:T(8,128)(2,1)}, u32[]{:S(2)}, u32[]{:S(2)}) collective-permute-start(bf16[512,640]{1,0:T(8,128)(2,1)} %get-tuple-element.50.refs_0_), channel_id=1, source_target_pairs={{0,8},{4,12},{8,0},{12,4},{16,24},{20,28},{24,16},{28,20},{1,9},{5... | collective-permute-start | bytes 1966088 | tf_op jit(solution)/shard_map/ppermute | solution.py:555
  52.2 28.9 %collective-permute-start.8 = (bf16[512,640]{1,0:T(8,128)(2,1)}, bf16[512,640]{1,0:T(8,128)(2,1)}, u32[]{:S(2)}, u32[]{:S(2)}) collective-permute-start(bf16[512,640]{1,0:T(8,128)(2,1)} %get-tuple-element.42), channel_id=1, source_target_pairs={{0,24},{4,28},{8,16},{12,20},{16,8},{20,12},{24,0},{28,4},{1,25},{... | collective-permute-start | bytes 1966088 | tf_op jit(solution)/shard_map/ppermute | solution.py:555
  59.1 23.5 %collective-permute-start.9 = (bf16[2,1,256,640]{3,2,1,0:T(8,128)(2,1)}, bf16[2,1,256,640]{3,2,1,0:T(8,128)(2,1)}, u32[]{:S(2)}, u32[]{:S(2)}) collective-permute-start(bf16[2,1,256,640]{3,2,1,0:T(8,128)(2,1)} %get-tuple-element.45), channel_id=1, source_target_pairs={{0,1},{3,2},{4,5},{7,6},{8,9},{11,10},{12,13},{15,14},{16,17},{19,... | collective-permute-start | bytes 1966088 | tf_op jit(solution)/shard_map/ppermute | solution.py:520
  63.4 19.2 %collective-permute-start.10 = (bf16[2,1,256,640]{3,2,1,0:T(8,128)(2,1)}, bf16[2,1,256,640]{3,2,1,0:T(8,128)(2,1)}, u32[]{:S(2)}, u32[]{:S(2)}) collective-permute-start(bf16[2,1,256,640]{3,2,1,0:T(8,128)(2,1)} %get-tuple-element.45), channel_id=1, source_target_pairs={{1,2},{2,1},{5,6},{6,5},{9,10},{10,9},{13,14},{14,13},{17,18},{18,... | collective-permute-start | bytes 1966088 | tf_op jit(solution)/shard_map/ppermute | solution.py:520
  84.8 11.6 %collective-permute-start.14 = (bf16[784,640]{1,0:T(8,128)(2,1)}, bf16[784,640]{1,0:T(8,128)(2,1)}, u32[]{:S(2)}, u32[]{:S(2)}) collective-permute-start(bf16[784,640]{1,0:T(8,128)(2,1)} %collective-permute-done.6.tag_ref.near_ref.refs_1_), channel_id=1, source_target_pairs={{0,4},{4,0},{8,12},{12,8},{16,20},{20,16},{24,28},{28,24},{1,5},{5... | collective-permute-start | bytes 3010568 | tf_op jit(solution)/shard_map/ppermute | solution.py:555
  87.8 3.5 %collective-permute-start.13 = (bf16[512,640]{1,0:T(8,128)(2,1)}, bf16[512,640]{1,0:T(8,128)(2,1)}, u32[]{:S(2)}, u32[]{:S(2)}) collective-permute-start(bf16[512,640]{1,0:T(8,128)(2,1)} %get-tuple-element.50.refs_0_), channel_id=1, source_target_pairs={{0,4},{4,0},{8,12},{12,8},{16,20},{20,16},{24,28},{28,24},{1,5},{5... | collective-permute-start | bytes 1966088 | tf_op jit(solution)/shard_map/ppermute | solution.py:555
  87.9 6.0 %collective-permute-start.15 = (bf16[512,640]{1,0:T(8,128)(2,1)}, bf16[512,640]{1,0:T(8,128)(2,1)}, u32[]{:S(2)}, u32[]{:S(2)}) collective-permute-start(bf16[512,640]{1,0:T(8,128)(2,1)} %collective-permute-done.7.refs_0_.refs_2_), channel_id=1, source_target_pairs={{0,4},{4,0},{8,12},{12,8},{16,20},{20,16},{24,28},{28,24},{1,5},{5... | collective-permute-start | bytes 1966088 | tf_op jit(solution)/shard_map/ppermute | solution.py:555
  88.3 7.2 %collective-permute-start.16 = (bf16[512,640]{1,0:T(8,128)(2,1)}, bf16[512,640]{1,0:T(8,128)(2,1)}, u32[]{:S(2)}, u32[]{:S(2)}) collective-permute-start(bf16[512,640]{1,0:T(8,128)(2,1)} %collective-permute-done.8.refs_1_.refs_3_), channel_id=1, source_target_pairs={{0,4},{4,0},{8,12},{12,8},{16,20},{20,16},{24,28},{28,24},{1,5},{5... | collective-permute-start | bytes 1966088 | tf_op jit(solution)/shard_map/ppermute | solution.py:555
  88.4 16.2 %collective-permute-start.18 = (bf16[1,256,640]{2,1,0:T(8,128)(2,1)}, bf16[1,256,640]{2,1,0:T(8,128)(2,1)}, u32[]{:S(2)}, u32[]{:S(2)}) collective-permute-start(bf16[1,256,640]{2,1,0:T(8,128)(2,1)} %get-tuple-element.57), channel_id=1, source_target_pairs={{0,1},{1,0},{2,3},{3,2},{4,5},{5,4},{6,7},{7,6},{8,9},{9,8},{10,11... | collective-permute-start | bytes 983048 | tf_op jit(solution)/shard_map/ppermute | solution.py:520
  91.3 18.9 %collective-permute-start.19 = (bf16[1,256,640]{2,1,0:T(8,128)(2,1)}, bf16[1,256,640]{2,1,0:T(8,128)(2,1)}, u32[]{:S(2)}, u32[]{:S(2)}) collective-permute-start(bf16[1,256,640]{2,1,0:T(8,128)(2,1)} %get-tuple-element.47), channel_id=1, source_target_pairs={{0,2},{1,3},{2,0},{3,1},{4,6},{5,7},{6,4},{7,5},{8,10},{9,11},{10,... | collective-permute-start | bytes 983048 | tf_op jit(solution)/shard_map/ppermute | solution.py:520
  93.9 24.3 %collective-permute-start.11 = (bf16[1,256,640]{2,1,0:T(8,128)(2,1)}, bf16[1,256,640]{2,1,0:T(8,128)(2,1)}, u32[]{:S(2)}, u32[]{:S(2)}) collective-permute-start(bf16[1,256,640]{2,1,0:T(8,128)(2,1)} %get-tuple-element.48), channel_id=1, source_target_pairs={{0,1},{1,0},{2,3},{3,2},{4,5},{5,4},{6,7},{7,6},{8,9},{9,8},{10,11... | collective-permute-start | bytes 983048 | tf_op jit(solution)/shard_map/ppermute | solution.py:520
  95.5 28.2 %collective-permute-start.12 = (bf16[1,256,640]{2,1,0:T(8,128)(2,1)}, bf16[1,256,640]{2,1,0:T(8,128)(2,1)}, u32[]{:S(2)}, u32[]{:S(2)}) collective-permute-start(bf16[1,256,640]{2,1,0:T(8,128)(2,1)} %get-tuple-element.49), channel_id=1, source_target_pairs={{0,2},{1,3},{2,0},{3,1},{4,6},{5,7},{6,4},{7,5},{8,10},{9,11},{10,... | collective-permute-start | bytes 983048 | tf_op jit(solution)/shard_map/ppermute | solution.py:520
  102.5 10.1 %collective-permute-start.17 = (bf16[256,640]{1,0:T(8,128)(2,1)}, bf16[256,640]{1,0:T(8,128)(2,1)}, u32[]{:S(2)}, u32[]{:S(2)}) collective-permute-start(bf16[256,640]{1,0:T(8,128)(2,1)} %get-tuple-element.55), channel_id=1, source_target_pairs={{0,16},{4,20},{8,24},{12,28},{16,0},{20,4},{24,8},{28,12},{1,17},{... | collective-permute-start | bytes 983048 | tf_op jit(solution)/shard_map/ppermute | solution.py:555
  112.4 11.8 %collective-permute-start.20 = (bf16[1,256,640]{2,1,0:T(8,128)(2,1)}, bf16[1,256,640]{2,1,0:T(8,128)(2,1)}, u32[]{:S(2)}, u32[]{:S(2)}) collective-permute-start(bf16[1,256,640]{2,1,0:T(8,128)(2,1)} %add.12), channel_id=1, source_target_pairs={{0,8},{4,12},{8,0},{12,4},{16,24},{20,28},{24,16},{28,20},{1,9},{5... | collective-permute-start | bytes 983048 | tf_op jit(solution)/shard_map/ppermute | solution.py:555

commit v7 on v6

--- a/solution.py
+++ b/solution.py
@@ -139,14 +139,14 @@
     )(lengths, queries, new_keys, new_values, keys, values)
 
 
-def cross_kernel(heads, pieces_count, spans, prompts_ref, side_ref, q_ref, near_ref, *refs):
+def cross_kernel(heads, pieces_count, spans, prompt_ref, side_ref, q_ref, near_ref, *refs):
     pieces, (own_ref, other_ref) = refs[:pieces_count], refs[pieces_count:]
     rows = q_ref.shape[0]
     width = heads * HD
     first = pl.multiple_of(side_ref[0] * width, HD)
-    asked = 2 * spans[0] * spans[1]
-    for part in range(2):
-        prompt = prompts_ref[part]
+    tag = near_ref[rows:, :HD].astype(jnp.float32)
+    prompts = prompt_ref[0], jnp.max(tag).astype(jnp.int32)
+    for part, prompt in enumerate(prompts):
         target = other_ref if part else own_ref
 
         def gathered(kind, head, prompt=prompt):
@@ -156,10 +156,8 @@
             return jnp.concatenate([piece[at, cols] for piece in pieces], axis=0)
 
         def scores_of(head, part=part, gathered=gathered):
-            if part == 0:
-                queries = q_ref[:, pl.ds(pl.multiple_of(first + head * HD, HD), HD)]
-            else:
-                queries = near_ref[asked : asked + rows, head * HD : (head + 1) * HD]
+            source = near_ref if part else q_ref
+            queries = source[:rows, pl.ds(pl.multiple_of(first + head * HD, HD), HD)]
             return score(queries, gathered(0, head))
 
         def use(head, scores, target=target, gathered=gathered):
@@ -169,7 +167,7 @@
         visit_heads(heads, scores_of, use)
 
 
-def cross_attention(prompts, side, queries, near, pieces, spans):
+def cross_attention(prompt, side, queries, near, pieces, spans):
     rows, width = queries.shape
     half = width // 2
     scalars = pl.BlockSpec(memory_space=pltpu.SMEM)
@@ -180,29 +178,9 @@
         out_specs=[vmem, vmem],
         out_shape=[jax.ShapeDtypeStruct((rows, half), jnp.bfloat16)] * 2,
         compiler_params=pltpu.CompilerParams(vmem_limit_bytes=VMEM_LIMIT),
-        cost_estimate=cost_of(0),
+        cost_estimate=cost_of(2e-6),
         name="cross_attention",
-    )(prompts, side.reshape(1), queries, near, *pieces)
-
-
-def prompts_kernel(prompt_ref, tag_ref, *refs):
-    refs[-1][0] = prompt_ref[0]
-    refs[-1][1] = jnp.max(tag_ref[...].astype(jnp.float32)).astype(jnp.int32)
-
-
-def read_prompts(prompt_of, asked, gates):
-    rows, half = asked.shape
-    scalars = pl.BlockSpec(memory_space=pltpu.SMEM)
-    return pl.pallas_call(
-        prompts_kernel,
-        grid=(1,),
-        in_specs=[scalars, pl.BlockSpec((TAG_ROWS, half), lambda i: (rows // TAG_ROWS - 1, 0))]
-        + [pl.BlockSpec(memory_space=pl.ANY)] * len(gates),
-        out_specs=scalars,
-        out_shape=jax.ShapeDtypeStruct((2,), jnp.int32),
-        cost_estimate=cost_of(100e-6),
-        name="read_prompts",
-    )(prompt_of, asked, *gates)
+    )(prompt, side.reshape(1), queries, near, *pieces)
 
 
 def gate_kernel(value_ref, *refs):
@@ -218,7 +196,7 @@
         out_shape=jax.ShapeDtypeStruct((1,), jnp.int32),
         cost_estimate=cost_of(100e-6),
         name="gate",
-    )(value.reshape(1), *waited)[0]
+    )(value.reshape(1), *waited)
 
 
 def pack_kernel(side_ref, prompt_ref, k_ref, v_ref, q_ref, keep_ref, give_ref, ask_ref):
@@ -232,18 +210,17 @@
             at = slice(first, first + text_rows)
             keep_ref[at, :] = source[prompt, :, kept]
             give_ref[at, :] = source[prompt, :, given]
-            ask_ref[at, :] = source[prompt, :, given]
-    first, rows = give_ref.shape[0], q_ref.shape[0]
-    ask_ref[first : first + rows, :] = q_ref[:, given]
-    tag = jnp.full((TAG_ROWS, half), prompt_ref[0], jnp.int32)
-    ask_ref[first + rows :, :] = tag.astype(jnp.float32).astype(ask_ref.dtype)
+    rows = q_ref.shape[0]
+    ask_ref[:rows, :] = q_ref[...]
+    tag = jnp.full((TAG_ROWS, 2 * half), prompt_ref[0], jnp.int32)
+    ask_ref[rows:, :] = tag.astype(jnp.float32).astype(ask_ref.dtype)
 
 
 def pack(side, prompt_of, text_k, text_v, queries):
     prompts, text_rows, width = text_k.shape
     rows, half = queries.shape[0], width // 2
     text = jax.ShapeDtypeStruct((2 * prompts * text_rows, half), text_k.dtype)
-    ask = jax.ShapeDtypeStruct((text.shape[0] + rows + TAG_ROWS, half), queries.dtype)
+    ask = jax.ShapeDtypeStruct((rows + TAG_ROWS, width), queries.dtype)
     scalars = pl.BlockSpec(memory_space=pltpu.SMEM)
     vmem = pl.BlockSpec(memory_space=pltpu.VMEM)
     return pl.pallas_call(
@@ -576,11 +553,10 @@
         keep, give, ask = pack(text_side, prompt_of, text_k, text_v, after(q_cross, own))
         across = after(across, keep)
         give, keep, ask = after((give, keep, ask), near)
-        asked = swap(ask, 4)
         if chips == 4:
-            pieces = [keep, asked, swap(keep, 2), swap(give, 6)]
+            pieces = [keep, swap(give, 4), swap(keep, 2), swap(give, 6)]
         else:
-            pieces = [keep, asked[: give.shape[0]]]
+            pieces = [keep, swap(give, 4)]
             for bit in range(chips.bit_length() - 1):
                 if bit != 1:
                     pieces += [swap(piece, 2 << bit) for piece in pieces]
@@ -605,15 +581,16 @@
     if line:
         near_terms, own_terms, last = terms[:3], terms[3:6], terms[6]
         far, inner = to_tp(last, [(0, 1), (3, 2)]), to_tp(last, [(1, 2), (2, 1)])
-        prompts = read_prompts(prompt_of, asked, pieces[2:])
-        near_joined, own_joined = join(near_terms[2], own_terms[2], after(far, inner, prompts))
-        near_outer, own_outer, *late = after(
-            (near_terms[1], own_terms[1], *pieces), near_joined
+        prompt = gate(prompt_of, *pieces[1:])
+        near_joined, own_joined = join(near_terms[2], own_terms[2], after(far, inner, prompt))
+        near_outer, own_outer, ask, *late = after(
+            (near_terms[1], own_terms[1], ask, *pieces), near_joined
         )
         near_outer, near_crossing = to_tp(near_outer, apart(4, 1)), to_tp(near_joined, apart(4, 2))
         own_outer, own_crossing = to_tp(own_outer, apart(4, 1)), to_tp(own_joined, apart(4, 2))
         pieces += [swap(piece, 1) for piece in late]
-        mine, others = cross_attention(prompts, text_side, q_cross, asked, pieces, spans)
+        asked = swap(ask, 4)
+        mine, others = cross_attention(prompt, text_side, q_cross, asked, pieces, spans)
         answer = swap(others, 4)
         near_outer = after(near_outer, mine)
         given = add(near_terms[0], (inner, 0), near_outer, near_crossing)
@@ -627,9 +604,9 @@
         ]
         given, own_parts = add(*near_parts[0]), near_parts[1]
         if split_heads:
-            prompts = read_prompts(prompt_of, asked, [])
             pieces += [swap(piece, 1) for piece in pieces]
-            mine, others = cross_attention(prompts, text_side, q_cross, asked, pieces, spans)
+            asked = swap(ask, 4)
+            mine, others = cross_attention(prompt_of, text_side, q_cross, asked, pieces, spans)
             answer = swap(others, 4)
             cross_heads = in_order(text_side, mine, answer, 1)
 

time: 128 us -> 124 us (0.969)
  waiting for transfers between devices: 50.4 us -> 38.5 us
  Pallas kernels: 35.9 us -> 45.4 us
  starting transfers between devices: 37.3 us -> 36 us
    ppermute x6, waiting for transfers between devices: 14.9 us -> 0.02 us  [to_tp(): return lax.ppermute(value, 'tp', pairs)]
    ppermute x11 -> x12, waiting for transfers between devices: 26.5 us -> 38.4 us  [swap(): return lax.ppermute(array, 'req', [(i, i ^ distance) for i in range(reqs)])]
    pallas_call x1, Pallas kernels: 10.4 us -> 20.6 us  [self_attention(): pl.pallas_call(functools.partial(self_kernel, block_rows, heads), grid_sp...]
    ppermute x1, waiting for transfers between devices: 9.01 us -> 0.01 us  [per_device(): lax.ppermute(w_out, 'req', [(first_of[i], first_of[i ^ 2]) for i in range...]
    pallas_call x1 -> x0, Pallas kernels: 1.37 us -> none  [read_prompts(): pl.pallas_call(prompts_kernel, grid=(1,), in_specs=[scalars, pl.BlockSpec...]
    ppermute x11 -> x12, starting transfers between devices: 15.8 us -> 15.3 us  [swap(): return lax.ppermute(array, 'req', [(i, i ^ distance) for i in range(reqs)])]
  transfers between devices with their start and end apart: 21 -> 22, of which waited for: 10 -> 6; matrix products, arithmetic and copies ran while one was open for 2% -> 2% of each run, Pallas kernels for 24% -> 32%
where the time goes in v7:
time: 124 us
  Pallas kernels  45.4 us (37%)
  waiting for transfers between devices  38.5 us (31%)
  starting transfers between devices  36 us (29%)
  other arithmetic  2.27 us (2%)
  between operations  1.55 us (1%)
    ppermute x12, waiting for transfers between devices, swap(): return lax.ppermute(array, 'req', [(i, i ^ distance) for i in range(reqs)])  38.4 us
    pallas_call x1, Pallas kernels, self_attention(): pl.pallas_call(functools.partial(self_kernel, block_rows, heads), grid_sp...  20.6 us
    ppermute x12, starting transfers between devices, swap(): return lax.ppermute(array, 'req', [(i, i ^ distance) for i in range(reqs)])  15.3 us
    ppermute x6, starting transfers between devices, to_tp(): return lax.ppermute(value, 'tp', pairs)  12 us
    pallas_call x1, Pallas kernels, project(): pl.pallas_call(functools.partial(project_kernel, count, flat, tps, joint)...  6.84 us
    pallas_call x1, Pallas kernels, cross_attention(): pl.pallas_call(functools.partial(cross_kernel, half // HD, len(pieces), s...  6.35 us
    pallas_call x1, Pallas kernels, finish(): pl.pallas_call(functools.partial(finish_kernel, halves), in_specs=[pl.Blo...  3.26 us
    ppermute x1, starting transfers between devices, per_device(): lax.ppermute(w_out, 'req', [(first_of[i], first_of[i ^ 2]) for i in range...  3.03 us
  transfers between devices with their start and end apart: 22, of which 6 were waited for; matrix products, arithmetic and copies ran while one was open for 2% of the time, Pallas kernels for 32%

profile of v7, /device:TPU:0, one launch (start us, length us, event | category | flops | bytes accessed | tf_op | source)
XLA Modules:
  0.0 123.7 jit_solution(7860271699628896142)
XLA Ops:
  0.6 3.0 %collective-permute-start.1 = (bf16[1280,640]{1,0:T(8,128)(2,1)}, bf16[1280,640]{1,0:T(8,128)(2,1)}, u32[]{:S(2)}, u32[]{:S(2)}) collective-permute-start(bf16[1280,640]{1,0:T(8,128)(2,1)} %refs_0_.1), channel_id=1, source_target_pairs={{0,16},{12,28},{16,0},{28,12},{4,8},{8,4},{20,24},{24,20},{1,17},{... | collective-permute-start | bytes 4915208 | tf_op jit(solution)/shard_map/ppermute | solution.py:536
  3.7 20.6 %self_attention.1.own_ref = bf16[256,1280]{1,0:T(8,128)(2,1)} custom-call(s32[8]{0:T(128)} %length_ref.1, bf16[256,1280]{1,0:T(8,128)(2,1)} %q_ref.2, bf16[256,1280]{1,0:T(8,128)(2,1)} %kn_ref.1, bf16[256,1280]{1,0:T(8,128)(2,1)} %vn_ref.1, bf16[4096,1280]{1,0:T(8,128)(2,1)} %bitcast.4, bf16[4096,1280]{1,0:T(8,128)(2,1)} %bitcast.5), custom_call_target="tpu_custom_call" | custom-call | flops 23069999104 | tf_op jit(solution)/shard_map/self_attention/pallas_call | solution.py:123
  24.3 1.8 %collective-permute-start.3 = (bf16[1280,640]{1,0:T(8,128)(2,1)}, bf16[1280,640]{1,0:T(8,128)(2,1)}, u32[]{:S(2)}, u32[]{:S(2)}) collective-permute-start(bf16[1280,640]{1,0:T(8,128)(2,1)} %collective-permute-done.1.refs_2_.refs_5_), channel_id=1, source_target_pairs={{4,20},{8,24},{20,4},{24,8},{5,21},{9,25},{21,5},{25,9},{6,22},{10... | collective-permute-start | bytes 4915208 | tf_op jit(solution)/shard_map/ppermute | solution.py:547
  26.1 1.9 %collective-permute-start = (bf16[256,1280]{1,0:T(8,128)(2,1)}, bf16[256,1280]{1,0:T(8,128)(2,1)}, u32[]{:S(2)}, u32[]{:S(2)}) collective-permute-start(bf16[256,1280]{1,0:T(8,128)(2,1)} %self_attention.1.own_ref), channel_id=1, source_target_pairs={{0,8},{4,12},{8,0},{12,4},{16,24},{20,28},{24,16},{28,20},{1,9},{5... | collective-permute-start | bytes 1966088 | tf_op jit(solution)/shard_map/ppermute | solution.py:532
  28.0 2.5 %collective-permute-start.5 = (bf16[1280,640]{1,0:T(8,128)(2,1)}, bf16[1280,640]{1,0:T(8,128)(2,1)}, u32[]{:S(2)}, u32[]{:S(2)}) collective-permute-start(bf16[1280,640]{1,0:T(8,128)(2,1)} %refs_0_.1), channel_id=1, source_target_pairs={{0,4},{12,8},{16,20},{28,24},{1,5},{13,9},{17,21},{29,25},{2,6},{1... | collective-permute-start | bytes 4915208 | tf_op jit(solution)/shard_map/ppermute | solution.py:542
  31.1 2.9 %pack.1 = (bf16[512,640]{1,0:T(8,128)(2,1)}, bf16[512,640]{1,0:T(8,128)(2,1)}, bf16[272,1280]{1,0:T(8,128)(2,1)}) custom-call(s32[1]{0:T(128)} %bitcast.3.side_ref, s32[1]{0:T(128)S(6)} %copy.14.prompt_ref.value_ref, bf16[4,64,1280]{2,1,0:T(8,128)(2,1)} %k_ref.1, bf16[4,64,1280]{2,1,0:T(8,128)(2,1)} %v_ref.1, bf16[256,1280]{1,0:T(8,128)(2,1)} %q_ref.4), custom_call_target="tpu_custom_call" | custom-call | flops 3460499968 | tf_op jit(solution)/shard_map/pack/pallas_call | solution.py:226
  34.0 9.3 %collective-permute-done.near_ref = bf16[256,1280]{1,0:T(8,128)(2,1)} collective-permute-done((bf16[256,1280]{1,0:T(8,128)(2,1)}, bf16[256,1280]{1,0:T(8,128)(2,1)}, u32[]{:S(2)}, u32[]{:S(2)}) %collective-permute-start) | collective-permute-done | bytes 655392 | tf_op jit(solution)/shard_map/ppermute | solution.py:532
  45.4 8.1 %collective-permute-start.8 = (bf16[512,640]{1,0:T(8,128)(2,1)}, bf16[512,640]{1,0:T(8,128)(2,1)}, u32[]{:S(2)}, u32[]{:S(2)}) collective-permute-start(bf16[512,640]{1,0:T(8,128)(2,1)} %get-tuple-element.43), channel_id=1, source_target_pairs={{0,24},{4,28},{8,16},{12,20},{16,8},{20,12},{24,0},{28,4},{1,25},{... | collective-permute-start | bytes 1966088 | tf_op jit(solution)/shard_map/ppermute | solution.py:532
  54.0 6.8 %project.1 = (bf16[1,256,640]{2,1,0:T(8,128)(2,1)}, bf16[1,256,640]{2,1,0:T(8,128)(2,1)}, bf16[1,256,640]{2,1,0:T(8,128)(2,1)}, bf16[1,256,640]{2,1,0:T(8,128)(2...) custom-call(bf16[256,1280]{1,0:T(8,128)(2,1)} %self_attention.1.own_ref, ...), custom_call_target="tpu_custom_call" | custom-call | flops 11534999552 | tf_op jit(solution)/shard_map/project/pallas_call | solution.py:352
  60.9 4.4 %collective-permute-start.9 = (bf16[2,1,256,640]{3,2,1,0:T(8,128)(2,1)}, bf16[2,1,256,640]{3,2,1,0:T(8,128)(2,1)}, u32[]{:S(2)}, u32[]{:S(2)}) collective-permute-start(bf16[2,1,256,640]{3,2,1,0:T(8,128)(2,1)} %get-tuple-element.46), channel_id=1, source_target_pairs={{0,1},{3,2},{4,5},{7,6},{8,9},{11,10},{12,13},{15,14},{16,17},{19,... | collective-permute-start | bytes 1966088 | tf_op jit(solution)/shard_map/ppermute | solution.py:497
  65.2 1.5 %collective-permute-start.10 = (bf16[2,1,256,640]{3,2,1,0:T(8,128)(2,1)}, bf16[2,1,256,640]{3,2,1,0:T(8,128)(2,1)}, u32[]{:S(2)}, u32[]{:S(2)}) collective-permute-start(bf16[2,1,256,640]{3,2,1,0:T(8,128)(2,1)} %get-tuple-element.46), channel_id=1, source_target_pairs={{1,2},{2,1},{5,6},{6,5},{9,10},{10,9},{13,14},{14,13},{17,18},{18,... | collective-permute-start | bytes 1966088 | tf_op jit(solution)/shard_map/ppermute | solution.py:497
  66.8 8.0 %collective-permute-done.6.refs_0_.refs_1_ = bf16[512,640]{1,0:T(8,128)(2,1)} collective-permute-done((bf16[512,640]{1,0:T(8,128)(2,1)}, bf16[512,640]{1,0:T(8,128)(2,1)}, u32[]{:S(2)}, u32[]{:S(2)}) %collective-permute-start.6) | collective-permute-done | bytes 655392 | tf_op jit(solution)/shard_map/ppermute | solution.py:532
  74.8 5.3 %collective-permute-done.7.refs_1_.refs_2_ = bf16[512,640]{1,0:T(8,128)(2,1)} collective-permute-done((bf16[512,640]{1,0:T(8,128)(2,1)}, bf16[512,640]{1,0:T(8,128)(2,1)}, u32[]{:S(2)}, u32[]{:S(2)}) %collective-permute-start.7) | collective-permute-done | bytes 655392 | tf_op jit(solution)/shard_map/ppermute | solution.py:532
  80.6 2.2 %join.1 = (bf16[1,256,640]{2,1,0:T(8,128)(2,1)}, bf16[1,256,640]{2,1,0:T(8,128)(2,1)}) custom-call(bf16[1,256,640]{2,1,0:T(8,128)(2,1)} %get-tuple-element.44.near_ref, bf16[1,256,640]{2,1,0:T(8,128)(2,1)} %get-tuple-element.45.own_ref, bf16[2,1,256,640]{3,2,1,0:T(8,128)(2,1)} %collective-permute-done.9.far_ref), custom_call_target="tpu_custom_call" | custom-call | flops 2307000064 | tf_op jit(solution)/shard_map/join/pallas_call | solution.py:422
  83.4 1.5 %collective-permute-start.13 = (bf16[272,1280]{1,0:T(8,128)(2,1)}, bf16[272,1280]{1,0:T(8,128)(2,1)}, u32[]{:S(2)}, u32[]{:S(2)}) collective-permute-start(bf16[272,1280]{1,0:T(8,128)(2,1)} %get-tuple-element.51), channel_id=1, source_target_pairs={{0,16},{4,20},{8,24},{12,28},{16,0},{20,4},{24,8},{28,12},{1,17},{... | collective-permute-start | bytes 2088968 | tf_op jit(solution)/shard_map/ppermute | solution.py:532
  85.4 1.6 %collective-permute-start.19 = (bf16[1,256,640]{2,1,0:T(8,128)(2,1)}, bf16[1,256,640]{2,1,0:T(8,128)(2,1)}, u32[]{:S(2)}, u32[]{:S(2)}) collective-permute-start(bf16[1,256,640]{2,1,0:T(8,128)(2,1)} %get-tuple-element.59), channel_id=1, source_target_pairs={{0,1},{1,0},{2,3},{3,2},{4,5},{5,4},{6,7},{7,6},{8,9},{9,8},{10,11... | collective-permute-start | bytes 983048 | tf_op jit(solution)/shard_map/ppermute | solution.py:497
  87.0 2.6 %collective-permute-start.20 = (bf16[1,256,640]{2,1,0:T(8,128)(2,1)}, bf16[1,256,640]{2,1,0:T(8,128)(2,1)}, u32[]{:S(2)}, u32[]{:S(2)}) collective-permute-start(bf16[1,256,640]{2,1,0:T(8,128)(2,1)} %get-tuple-element.48), channel_id=1, source_target_pairs={{0,2},{1,3},{2,0},{3,1},{4,6},{5,7},{6,4},{7,5},{8,10},{9,11},{10,... | collective-permute-start | bytes 983048 | tf_op jit(solution)/shard_map/ppermute | solution.py:497
  91.5 9.8 %collective-permute-done.13.near_ref = bf16[272,1280]{1,0:T(8,128)(2,1)} collective-permute-done((bf16[272,1280]{1,0:T(8,128)(2,1)}, bf16[272,1280]{1,0:T(8,128)(2,1)}, u32[]{:S(2)}, u32[]{:S(2)}) %collective-permute-start.13) | collective-permute-done | bytes 696352 | tf_op jit(solution)/shard_map/ppermute | solution.py:532
  101.3 6.4 %cross_attention.1 = (bf16[256,640]{1,0:T(8,128)(2,1)}, bf16[256,640]{1,0:T(8,128)(2,1)}) custom-call(s32[1]{0:T(128)} %gate.2.prompt_ref, s32[1]{0:T(128)} %bitcast.3.side_ref, bf16[256,1280]{1,0:T(8,128)(2,1)} %q_ref.4, bf16[272,1280]{1,0:T(8,128)(2,1)} %collective-permute-done.13.near_ref, bf16[512,640]{1,0:T(8,128)(2,1)} %get-tuple-element.52.refs_0_, ...), custom_call_target="tpu_custom_call" | custom-call | flops 2307000064 | tf_op jit(solution)/shard_map/cross_attention/pallas_call | solution.py:175
  107.7 1.5 %collective-permute-start.18 = (bf16[256,640]{1,0:T(8,128)(2,1)}, bf16[256,640]{1,0:T(8,128)(2,1)}, u32[]{:S(2)}, u32[]{:S(2)}) collective-permute-start(bf16[256,640]{1,0:T(8,128)(2,1)} %get-tuple-element.57), channel_id=1, source_target_pairs={{0,16},{4,20},{8,24},{12,28},{16,0},{20,4},{24,8},{28,12},{1,17},{... | collective-permute-start | bytes 983048 | tf_op jit(solution)/shard_map/ppermute | solution.py:532
  109.2 2.2 %add.12 = bf16[1,256,640]{2,1,0:T(8,128)(2,1)} custom-call(bf16[1,256,640]{2,1,0:T(8,128)(2,1)} %get-tuple-element.58.refs_0_, bf16[2,1,256,640]{3,2,1,0:T(8,128)(2,1)} %collective-permute-done.10.refs_1_, bf16[1,256,640]{2,1,0:T(8,128)(2,1)} %collective-permute-done.19.refs_2_, bf16[1,256,640]{2,1,0:T(8,128)(2,1)} %collective-permute-done.20.refs_3_), custom_call_target="tpu_custom_call" | custom-call | flops 115350003712 | tf_op jit(solution)/shard_map/add/pallas_call | solution.py:399
  111.4 5.4 %collective-permute-done.18 = bf16[256,640]{1,0:T(8,128)(2,1)} collective-permute-done((bf16[256,640]{1,0:T(8,128)(2,1)}, bf16[256,640]{1,0:T(8,128)(2,1)}, u32[]{:S(2)}, u32[]{:S(2)}) %collective-permute-start.18) | collective-permute-done | bytes 327712 | tf_op jit(solution)/shard_map/ppermute | solution.py:532
  116.8 2.3 %maximum_select_fusion.refs_2_ = bf16[256,1280]{1,0:T(8,128)(2,1)} fusion(bf16[256,640]{1,0:T(8,128)(2,1)} %collective-permute-done.18, bf16[256,640]{1,0:T(8,128)(2,1)} %get-tuple-element.56, pred[]{:T(512)S(6)} %eq.6), kind=kLoop, calls=%fused_computation | loop fusion | flops 2949120 | bytes 1310721 | tf_op jit(solution)/shard_map/jit(_where)/select_n | solution.py:573
  120.3 3.3 %finish.1 = bf16[256,1280]{1,0:T(8,128)(2,1)} custom-call(s32[1]{0:T(128)} %gate.3.side_ref, bf16[256,1280]{1,0:T(8,128)(2,1)} %hidden_ref.1, bf16[1,256,640]{2,1,0:T(8,128)(2,1)} %collective-permute-done.21.received_ref, bf16[1,256,640]{2,1,0:T(8,128)(2,1)} %get-tuple-element.61.refs_0_, bf16[2,1,256,640]{3,2,1,0:T(8,128)(2,1)} %collective-permute-done.10.refs_1_, ...), custom_call_target="tpu_custom_call" | custom-call | flops 2307000064 | tf_op jit(solution)/shard_map/finish/pallas_call | solution.py:477
  (30 shorter events, 7.4 us)
Async XLA Ops:
  0.6 23.6 %collective-permute-start.1 = (bf16[1280,640]{1,0:T(8,128)(2,1)}, bf16[1280,640]{1,0:T(8,128)(2,1)}, u32[]{:S(2)}, u32[]{:S(2)}) collective-permute-start(bf16[1280,640]{1,0:T(8,128)(2,1)} %refs_0_.1), channel_id=1, source_target_pairs={{0,16},{12,28},{16,0},{28,12},{4,8},{8,4},{20,24},{24,20},{1,17},{... | collective-permute-start | bytes 4915208 | tf_op jit(solution)/shard_map/ppermute | solution.py:536
  24.3 9.7 %collective-permute-start.3 = (bf16[1280,640]{1,0:T(8,128)(2,1)}, bf16[1280,640]{1,0:T(8,128)(2,1)}, u32[]{:S(2)}, u32[]{:S(2)}) collective-permute-start(bf16[1280,640]{1,0:T(8,128)(2,1)} %collective-permute-done.1.refs_2_.refs_5_), channel_id=1, source_target_pairs={{4,20},{8,24},{20,4},{24,8},{5,21},{9,25},{21,5},{25,9},{6,22},{10... | collective-permute-start | bytes 4915208 | tf_op jit(solution)/shard_map/ppermute | solution.py:547
  26.1 17.2 %collective-permute-start = (bf16[256,1280]{1,0:T(8,128)(2,1)}, bf16[256,1280]{1,0:T(8,128)(2,1)}, u32[]{:S(2)}, u32[]{:S(2)}) collective-permute-start(bf16[256,1280]{1,0:T(8,128)(2,1)} %self_attention.1.own_ref), channel_id=1, source_target_pairs={{0,8},{4,12},{8,0},{12,4},{16,24},{20,28},{24,16},{28,20},{1,9},{5... | collective-permute-start | bytes 1966088 | tf_op jit(solution)/shard_map/ppermute | solution.py:532
  28.0 25.5 %collective-permute-start.5 = (bf16[1280,640]{1,0:T(8,128)(2,1)}, bf16[1280,640]{1,0:T(8,128)(2,1)}, u32[]{:S(2)}, u32[]{:S(2)}) collective-permute-start(bf16[1280,640]{1,0:T(8,128)(2,1)} %refs_0_.1), channel_id=1, source_target_pairs={{0,4},{12,8},{16,20},{28,24},{1,5},{13,9},{17,21},{29,25},{2,6},{1... | collective-permute-start | bytes 4915208 | tf_op jit(solution)/shard_map/ppermute | solution.py:542
  34.0 20.0 %collective-permute-start.2 = (bf16[1280,640]{1,0:T(8,128)(2,1)}, bf16[1280,640]{1,0:T(8,128)(2,1)}, u32[]{:S(2)}, u32[]{:S(2)}) collective-permute-start(bf16[1280,640]{1,0:T(8,128)(2,1)} %collective-permute-done.1.refs_2_.refs_5_), channel_id=1, source_target_pairs={{0,4},{4,0},{8,12},{12,8},{16,20},{20,16},{24,28},{28,24},{1,5},{5... | collective-permute-start | bytes 4915208 | tf_op jit(solution)/shard_map/ppermute | solution.py:532
  43.3 10.7 %collective-permute-start.4 = (bf16[1280,640]{1,0:T(8,128)(2,1)}, bf16[1280,640]{1,0:T(8,128)(2,1)}, u32[]{:S(2)}, u32[]{:S(2)}) collective-permute-start(bf16[1280,640]{1,0:T(8,128)(2,1)} %collective-permute-done.3.refs_7_), channel_id=1, source_target_pairs={{4,0},{8,12},{20,16},{24,28},{5,1},{9,13},{21,17},{25,29},{6,2},{1... | collective-permute-start | bytes 4915208 | tf_op jit(solution)/shard_map/ppermute | solution.py:564
  44.8 30.0 %collective-permute-start.6 = (bf16[512,640]{1,0:T(8,128)(2,1)}, bf16[512,640]{1,0:T(8,128)(2,1)}, u32[]{:S(2)}, u32[]{:S(2)}) collective-permute-start(bf16[512,640]{1,0:T(8,128)(2,1)} %get-tuple-element.43), channel_id=1, source_target_pairs={{0,16},{4,20},{8,24},{12,28},{16,0},{20,4},{24,8},{28,12},{1,17},{... | collective-permute-start | bytes 1966088 | tf_op jit(solution)/shard_map/ppermute | solution.py:532
  45.4 34.7 %collective-permute-start.8 = (bf16[512,640]{1,0:T(8,128)(2,1)}, bf16[512,640]{1,0:T(8,128)(2,1)}, u32[]{:S(2)}, u32[]{:S(2)}) collective-permute-start(bf16[512,640]{1,0:T(8,128)(2,1)} %get-tuple-element.43), channel_id=1, source_target_pairs={{0,24},{4,28},{8,16},{12,20},{16,8},{20,12},{24,0},{28,4},{1,25},{... | collective-permute-start | bytes 1966088 | tf_op jit(solution)/shard_map/ppermute | solution.py:532
  53.5 26.6 %collective-permute-start.7 = (bf16[512,640]{1,0:T(8,128)(2,1)}, bf16[512,640]{1,0:T(8,128)(2,1)}, u32[]{:S(2)}, u32[]{:S(2)}) collective-permute-start(bf16[512,640]{1,0:T(8,128)(2,1)} %get-tuple-element.52.refs_0_), channel_id=1, source_target_pairs={{0,8},{4,12},{8,0},{12,4},{16,24},{20,28},{24,16},{28,20},{1,9},{5... | collective-permute-start | bytes 1966088 | tf_op jit(solution)/shard_map/ppermute | solution.py:532
  60.9 19.7 %collective-permute-start.9 = (bf16[2,1,256,640]{3,2,1,0:T(8,128)(2,1)}, bf16[2,1,256,640]{3,2,1,0:T(8,128)(2,1)}, u32[]{:S(2)}, u32[]{:S(2)}) collective-permute-start(bf16[2,1,256,640]{3,2,1,0:T(8,128)(2,1)} %get-tuple-element.46), channel_id=1, source_target_pairs={{0,1},{3,2},{4,5},{7,6},{8,9},{11,10},{12,13},{15,14},{16,17},{19,... | collective-permute-start | bytes 1966088 | tf_op jit(solution)/shard_map/ppermute | solution.py:497
  65.2 15.3 %collective-permute-start.10 = (bf16[2,1,256,640]{3,2,1,0:T(8,128)(2,1)}, bf16[2,1,256,640]{3,2,1,0:T(8,128)(2,1)}, u32[]{:S(2)}, u32[]{:S(2)}) collective-permute-start(bf16[2,1,256,640]{3,2,1,0:T(8,128)(2,1)} %get-tuple-element.46), channel_id=1, source_target_pairs={{1,2},{2,1},{5,6},{6,5},{9,10},{10,9},{13,14},{14,13},{17,18},{18,... | collective-permute-start | bytes 1966088 | tf_op jit(solution)/shard_map/ppermute | solution.py:497
  82.8 2.6 %collective-permute-start.14 = (bf16[512,640]{1,0:T(8,128)(2,1)}, bf16[512,640]{1,0:T(8,128)(2,1)}, u32[]{:S(2)}, u32[]{:S(2)}) collective-permute-start(bf16[512,640]{1,0:T(8,128)(2,1)} %get-tuple-element.52.refs_0_), channel_id=1, source_target_pairs={{0,4},{4,0},{8,12},{12,8},{16,20},{20,16},{24,28},{28,24},{1,5},{5... | collective-permute-start | bytes 1966088 | tf_op jit(solution)/shard_map/ppermute | solution.py:532
  82.9 4.1 %collective-permute-start.15 = (bf16[512,640]{1,0:T(8,128)(2,1)}, bf16[512,640]{1,0:T(8,128)(2,1)}, u32[]{:S(2)}, u32[]{:S(2)}) collective-permute-start(bf16[512,640]{1,0:T(8,128)(2,1)} %collective-permute-done.6.refs_0_.refs_1_), channel_id=1, source_target_pairs={{0,4},{4,0},{8,12},{12,8},{16,20},{20,16},{24,28},{28,24},{1,5},{5... | collective-permute-start | bytes 1966088 | tf_op jit(solution)/shard_map/ppermute | solution.py:532
  83.4 17.9 %collective-permute-start.13 = (bf16[272,1280]{1,0:T(8,128)(2,1)}, bf16[272,1280]{1,0:T(8,128)(2,1)}, u32[]{:S(2)}, u32[]{:S(2)}) collective-permute-start(bf16[272,1280]{1,0:T(8,128)(2,1)} %get-tuple-element.51), channel_id=1, source_target_pairs={{0,16},{4,20},{8,24},{12,28},{16,0},{20,4},{24,8},{28,12},{1,17},{... | collective-permute-start | bytes 2088968 | tf_op jit(solution)/shard_map/ppermute | solution.py:532
  84.9 4.7 %collective-permute-start.16 = (bf16[512,640]{1,0:T(8,128)(2,1)}, bf16[512,640]{1,0:T(8,128)(2,1)}, u32[]{:S(2)}, u32[]{:S(2)}) collective-permute-start(bf16[512,640]{1,0:T(8,128)(2,1)} %collective-permute-done.7.refs_1_.refs_2_), channel_id=1, source_target_pairs={{0,4},{4,0},{8,12},{12,8},{16,20},{20,16},{24,28},{28,24},{1,5},{5... | collective-permute-start | bytes 1966088 | tf_op jit(solution)/shard_map/ppermute | solution.py:532
  84.9 5.5 %collective-permute-start.17 = (bf16[512,640]{1,0:T(8,128)(2,1)}, bf16[512,640]{1,0:T(8,128)(2,1)}, u32[]{:S(2)}, u32[]{:S(2)}) collective-permute-start(bf16[512,640]{1,0:T(8,128)(2,1)} %collective-permute-done.8.refs_2_.refs_3_), channel_id=1, source_target_pairs={{0,4},{4,0},{8,12},{12,8},{16,20},{20,16},{24,28},{28,24},{1,5},{5... | collective-permute-start | bytes 1966088 | tf_op jit(solution)/shard_map/ppermute | solution.py:532
  85.4 23.7 %collective-permute-start.19 = (bf16[1,256,640]{2,1,0:T(8,128)(2,1)}, bf16[1,256,640]{2,1,0:T(8,128)(2,1)}, u32[]{:S(2)}, u32[]{:S(2)}) collective-permute-start(bf16[1,256,640]{2,1,0:T(8,128)(2,1)} %get-tuple-element.59), channel_id=1, source_target_pairs={{0,1},{1,0},{2,3},{3,2},{4,5},{5,4},{6,7},{7,6},{8,9},{9,8},{10,11... | collective-permute-start | bytes 983048 | tf_op jit(solution)/shard_map/ppermute | solution.py:497
  87.0 22.2 %collective-permute-start.20 = (bf16[1,256,640]{2,1,0:T(8,128)(2,1)}, bf16[1,256,640]{2,1,0:T(8,128)(2,1)}, u32[]{:S(2)}, u32[]{:S(2)}) collective-permute-start(bf16[1,256,640]{2,1,0:T(8,128)(2,1)} %get-tuple-element.48), channel_id=1, source_target_pairs={{0,2},{1,3},{2,0},{3,1},{4,6},{5,7},{6,4},{7,5},{8,10},{9,11},{10,... | collective-permute-start | bytes 983048 | tf_op jit(solution)/shard_map/ppermute | solution.py:497
  89.6 29.5 %collective-permute-start.11 = (bf16[1,256,640]{2,1,0:T(8,128)(2,1)}, bf16[1,256,640]{2,1,0:T(8,128)(2,1)}, u32[]{:S(2)}, u32[]{:S(2)}) collective-permute-start(bf16[1,256,640]{2,1,0:T(8,128)(2,1)} %get-tuple-element.49), channel_id=1, source_target_pairs={{0,1},{1,0},{2,3},{3,2},{4,5},{5,4},{6,7},{7,6},{8,9},{9,8},{10,11... | collective-permute-start | bytes 983048 | tf_op jit(solution)/shard_map/ppermute | solution.py:497
  90.4 28.7 %collective-permute-start.12 = (bf16[1,256,640]{2,1,0:T(8,128)(2,1)}, bf16[1,256,640]{2,1,0:T(8,128)(2,1)}, u32[]{:S(2)}, u32[]{:S(2)}) collective-permute-start(bf16[1,256,640]{2,1,0:T(8,128)(2,1)} %get-tuple-element.50), channel_id=1, source_target_pairs={{0,2},{1,3},{2,0},{3,1},{4,6},{5,7},{6,4},{7,5},{8,10},{9,11},{10,... | collective-permute-start | bytes 983048 | tf_op jit(solution)/shard_map/ppermute | solution.py:497
  107.7 9.2 %collective-permute-start.18 = (bf16[256,640]{1,0:T(8,128)(2,1)}, bf16[256,640]{1,0:T(8,128)(2,1)}, u32[]{:S(2)}, u32[]{:S(2)}) collective-permute-start(bf16[256,640]{1,0:T(8,128)(2,1)} %get-tuple-element.57), channel_id=1, source_target_pairs={{0,16},{4,20},{8,24},{12,28},{16,0},{20,4},{24,8},{28,12},{1,17},{... | collective-permute-start | bytes 983048 | tf_op jit(solution)/shard_map/ppermute | solution.py:532
  111.4 9.0 %collective-permute-start.21 = (bf16[1,256,640]{2,1,0:T(8,128)(2,1)}, bf16[1,256,640]{2,1,0:T(8,128)(2,1)}, u32[]{:S(2)}, u32[]{:S(2)}) collective-permute-start(bf16[1,256,640]{2,1,0:T(8,128)(2,1)} %add.12), channel_id=1, source_target_pairs={{0,8},{4,12},{8,0},{12,4},{16,24},{20,28},{24,16},{28,20},{1,9},{5... | collective-permute-start | bytes 983048 | tf_op jit(solution)/shard_map/ppermute | solution.py:532

commit v8 on v7

--- a/solution.py
+++ b/solution.py
@@ -429,7 +429,7 @@
             pltpu.SemaphoreType.DMA((4,)),
         ],
         compiler_params=pltpu.CompilerParams(vmem_limit_bytes=VMEM_LIMIT),
-        cost_estimate=cost_of(2e-6),
+        cost_estimate=cost_of(100e-6),
         name="join",
     )(near, own, far)
 
@@ -581,8 +581,8 @@
     if line:
         near_terms, own_terms, last = terms[:3], terms[3:6], terms[6]
         far, inner = to_tp(last, [(0, 1), (3, 2)]), to_tp(last, [(1, 2), (2, 1)])
-        prompt = gate(prompt_of, *pieces[1:])
-        near_joined, own_joined = join(near_terms[2], own_terms[2], after(far, inner, prompt))
+        prompt = prompt_of
+        near_joined, own_joined = join(near_terms[2], own_terms[2], after(far, inner, *pieces[1:]))
         near_outer, own_outer, ask, *late = after(
             (near_terms[1], own_terms[1], ask, *pieces), near_joined
         )

time: 124 us -> 123 us (level)
  Pallas kernels: 45.4 us -> 34.2 us
  waiting for transfers between devices: 38.5 us -> 47.6 us
    pallas_call x1, Pallas kernels: 20.6 us -> 10.4 us  [self_attention(): pl.pallas_call(functools.partial(self_kernel, block_rows, heads), grid_sp...]
    ppermute x1, waiting for transfers between devices: 0.01 us -> 9.01 us  [per_device(): lax.ppermute(w_out, 'req', [(first_of[i], first_of[i ^ 2]) for i in range...]
  transfers between devices with their start and end apart: 22 -> 22, of which waited for: 6 -> 8; matrix products, arithmetic and copies ran while one was open for 2% -> 2% of each run, Pallas kernels for 32% -> 23%
where the time goes in v8:
time: 123 us
  waiting for transfers between devices  47.6 us (39%)
  starting transfers between devices  37.1 us (30%)
  Pallas kernels  34.2 us (28%)
  other arithmetic  2.27 us (2%)
  between operations  1.53 us (1%)
    ppermute x12, waiting for transfers between devices, swap(): return lax.ppermute(array, 'req', [(i, i ^ distance) for i in range(reqs)])  38.4 us
    ppermute x12, starting transfers between devices, swap(): return lax.ppermute(array, 'req', [(i, i ^ distance) for i in range(reqs)])  16.3 us
    ppermute x6, starting transfers between devices, to_tp(): return lax.ppermute(value, 'tp', pairs)  12 us
    pallas_call x1, Pallas kernels, self_attention(): pl.pallas_call(functools.partial(self_kernel, block_rows, heads), grid_sp...  10.4 us
    ppermute x1, waiting for transfers between devices, per_device(): lax.ppermute(w_out, 'req', [(first_of[i], first_of[i ^ 2]) for i in range...  9.01 us
    pallas_call x1, Pallas kernels, project(): pl.pallas_call(functools.partial(project_kernel, count, flat, tps, joint)...  6.85 us
    pallas_call x1, Pallas kernels, cross_attention(): pl.pallas_call(functools.partial(cross_kernel, half // HD, len(pieces), s...  5.81 us
    pallas_call x1, Pallas kernels, finish(): pl.pallas_call(functools.partial(finish_kernel, halves), in_specs=[pl.Blo...  3.26 us
  transfers between devices with their start and end apart: 22, of which 8 were waited for; matrix products, arithmetic and copies ran while one was open for 2% of the time, Pallas kernels for 23%

profile of v8, /device:TPU:0, one launch (start us, length us, event | category | flops | bytes accessed | tf_op | source)
XLA Modules:
  0.0 122.7 jit_solution(3804049308085424019)
XLA Ops:
  0.6 3.0 %collective-permute-start.1 = (bf16[1280,640]{1,0:T(8,128)(2,1)}, bf16[1280,640]{1,0:T(8,128)(2,1)}, u32[]{:S(2)}, u32[]{:S(2)}) collective-permute-start(bf16[1280,640]{1,0:T(8,128)(2,1)} %refs_0_.1), channel_id=1, source_target_pairs={{0,16},{12,28},{16,0},{28,12},{4,8},{8,4},{20,24},{24,20},{1,17},{... | collective-permute-start | bytes 4915208 | tf_op jit(solution)/shard_map/ppermute | solution.py:536
  3.7 10.4 %self_attention.1.own_ref = bf16[256,1280]{1,0:T(8,128)(2,1)} custom-call(s32[8]{0:T(128)} %length_ref.1, bf16[256,1280]{1,0:T(8,128)(2,1)} %q_ref.2, bf16[256,1280]{1,0:T(8,128)(2,1)} %kn_ref.1, bf16[256,1280]{1,0:T(8,128)(2,1)} %vn_ref.1, bf16[4096,1280]{1,0:T(8,128)(2,1)} %bitcast.4, bf16[4096,1280]{1,0:T(8,128)(2,1)} %bitcast.5), custom_call_target="tpu_custom_call" | custom-call | flops 23069999104 | tf_op jit(solution)/shard_map/self_attention/pallas_call | solution.py:123
  14.1 9.0 %collective-permute-done.1.refs_2_.refs_5_ = bf16[1280,640]{1,0:T(8,128)(2,1)} collective-permute-done((bf16[1280,640]{1,0:T(8,128)(2,1)}, bf16[1280,640]{1,0:T(8,128)(2,1)}, u32[]{:S(2)}, u32[]{:S(2)}) %collective-permute-start.1) | collective-permute-done | bytes 1638432 | tf_op jit(solution)/shard_map/ppermute | solution.py:536
  23.1 1.8 %collective-permute-start.3 = (bf16[1280,640]{1,0:T(8,128)(2,1)}, bf16[1280,640]{1,0:T(8,128)(2,1)}, u32[]{:S(2)}, u32[]{:S(2)}) collective-permute-start(bf16[1280,640]{1,0:T(8,128)(2,1)} %collective-permute-done.1.refs_2_.refs_5_), channel_id=1, source_target_pairs={{4,20},{8,24},{20,4},{24,8},{5,21},{9,25},{21,5},{25,9},{6,22},{10... | collective-permute-start | bytes 4915208 | tf_op jit(solution)/shard_map/ppermute | solution.py:547
  24.9 3.1 %collective-permute-start = (bf16[256,1280]{1,0:T(8,128)(2,1)}, bf16[256,1280]{1,0:T(8,128)(2,1)}, u32[]{:S(2)}, u32[]{:S(2)}) collective-permute-start(bf16[256,1280]{1,0:T(8,128)(2,1)} %self_attention.1.own_ref), channel_id=1, source_target_pairs={{0,8},{4,12},{8,0},{12,4},{16,24},{20,28},{24,16},{28,20},{1,9},{5... | collective-permute-start | bytes 1966088 | tf_op jit(solution)/shard_map/ppermute | solution.py:532
  28.0 2.5 %collective-permute-start.5 = (bf16[1280,640]{1,0:T(8,128)(2,1)}, bf16[1280,640]{1,0:T(8,128)(2,1)}, u32[]{:S(2)}, u32[]{:S(2)}) collective-permute-start(bf16[1280,640]{1,0:T(8,128)(2,1)} %refs_0_.1), channel_id=1, source_target_pairs={{0,4},{12,8},{16,20},{28,24},{1,5},{13,9},{17,21},{29,25},{2,6},{1... | collective-permute-start | bytes 4915208 | tf_op jit(solution)/shard_map/ppermute | solution.py:542
  31.1 2.9 %pack.1 = (bf16[512,640]{1,0:T(8,128)(2,1)}, bf16[512,640]{1,0:T(8,128)(2,1)}, bf16[272,1280]{1,0:T(8,128)(2,1)}) custom-call(s32[1]{0:T(128)} %bitcast.3.side_ref, s32[1]{0:T(128)S(6)} %copy.14.prompt_ref, bf16[4,64,1280]{2,1,0:T(8,128)(2,1)} %k_ref.1, bf16[4,64,1280]{2,1,0:T(8,128)(2,1)} %v_ref.1, bf16[256,1280]{1,0:T(8,128)(2,1)} %q_ref.4), custom_call_target="tpu_custom_call" | custom-call | flops 3460499968 | tf_op jit(solution)/shard_map/pack/pallas_call | solution.py:226
  34.0 9.3 %collective-permute-done.near_ref = bf16[256,1280]{1,0:T(8,128)(2,1)} collective-permute-done((bf16[256,1280]{1,0:T(8,128)(2,1)}, bf16[256,1280]{1,0:T(8,128)(2,1)}, u32[]{:S(2)}, u32[]{:S(2)}) %collective-permute-start) | collective-permute-done | bytes 655392 | tf_op jit(solution)/shard_map/ppermute | solution.py:532
  45.4 7.9 %collective-permute-start.8 = (bf16[512,640]{1,0:T(8,128)(2,1)}, bf16[512,640]{1,0:T(8,128)(2,1)}, u32[]{:S(2)}, u32[]{:S(2)}) collective-permute-start(bf16[512,640]{1,0:T(8,128)(2,1)} %get-tuple-element.43), channel_id=1, source_target_pairs={{0,24},{4,28},{8,16},{12,20},{16,8},{20,12},{24,0},{28,4},{1,25},{... | collective-permute-start | bytes 1966088 | tf_op jit(solution)/shard_map/ppermute | solution.py:532
  53.9 6.8 %project.1 = (bf16[1,256,640]{2,1,0:T(8,128)(2,1)}, bf16[1,256,640]{2,1,0:T(8,128)(2,1)}, bf16[1,256,640]{2,1,0:T(8,128)(2,1)}, bf16[1,256,640]{2,1,0:T(8,128)(2...) custom-call(bf16[256,1280]{1,0:T(8,128)(2,1)} %self_attention.1.own_ref, ...), custom_call_target="tpu_custom_call" | custom-call | flops 11534999552 | tf_op jit(solution)/shard_map/project/pallas_call | solution.py:352
  60.7 4.4 %collective-permute-start.9 = (bf16[2,1,256,640]{3,2,1,0:T(8,128)(2,1)}, bf16[2,1,256,640]{3,2,1,0:T(8,128)(2,1)}, u32[]{:S(2)}, u32[]{:S(2)}) collective-permute-start(bf16[2,1,256,640]{3,2,1,0:T(8,128)(2,1)} %get-tuple-element.46), channel_id=1, source_target_pairs={{0,1},{3,2},{4,5},{7,6},{8,9},{11,10},{12,13},{15,14},{16,17},{19,... | collective-permute-start | bytes 1966088 | tf_op jit(solution)/shard_map/ppermute | solution.py:497
  65.1 1.5 %collective-permute-start.10 = (bf16[2,1,256,640]{3,2,1,0:T(8,128)(2,1)}, bf16[2,1,256,640]{3,2,1,0:T(8,128)(2,1)}, u32[]{:S(2)}, u32[]{:S(2)}) collective-permute-start(bf16[2,1,256,640]{3,2,1,0:T(8,128)(2,1)} %get-tuple-element.46), channel_id=1, source_target_pairs={{1,2},{2,1},{5,6},{6,5},{9,10},{10,9},{13,14},{14,13},{17,18},{18,... | collective-permute-start | bytes 1966088 | tf_op jit(solution)/shard_map/ppermute | solution.py:497
  66.6 8.2 %collective-permute-done.6.refs_1_ = bf16[512,640]{1,0:T(8,128)(2,1)} collective-permute-done((bf16[512,640]{1,0:T(8,128)(2,1)}, bf16[512,640]{1,0:T(8,128)(2,1)}, u32[]{:S(2)}, u32[]{:S(2)}) %collective-permute-start.6) | collective-permute-done | bytes 655392 | tf_op jit(solution)/shard_map/ppermute | solution.py:532
  74.8 5.3 %collective-permute-done.7.refs_2_ = bf16[512,640]{1,0:T(8,128)(2,1)} collective-permute-done((bf16[512,640]{1,0:T(8,128)(2,1)}, bf16[512,640]{1,0:T(8,128)(2,1)}, u32[]{:S(2)}, u32[]{:S(2)}) %collective-permute-start.7) | collective-permute-done | bytes 655392 | tf_op jit(solution)/shard_map/ppermute | solution.py:532
  80.1 2.2 %join.1 = (bf16[1,256,640]{2,1,0:T(8,128)(2,1)}, bf16[1,256,640]{2,1,0:T(8,128)(2,1)}) custom-call(bf16[1,256,640]{2,1,0:T(8,128)(2,1)} %get-tuple-element.44.near_ref, bf16[1,256,640]{2,1,0:T(8,128)(2,1)} %get-tuple-element.45.own_ref, bf16[2,1,256,640]{3,2,1,0:T(8,128)(2,1)} %collective-permute-done.9.far_ref), custom_call_target="tpu_custom_call" | custom-call | flops 115350003712 | tf_op jit(solution)/shard_map/join/pallas_call | solution.py:422
  82.9 1.5 %collective-permute-start.13 = (bf16[272,1280]{1,0:T(8,128)(2,1)}, bf16[272,1280]{1,0:T(8,128)(2,1)}, u32[]{:S(2)}, u32[]{:S(2)}) collective-permute-start(bf16[272,1280]{1,0:T(8,128)(2,1)} %get-tuple-element.51), channel_id=1, source_target_pairs={{0,16},{4,20},{8,24},{12,28},{16,0},{20,4},{24,8},{28,12},{1,17},{... | collective-permute-start | bytes 2088968 | tf_op jit(solution)/shard_map/ppermute | solution.py:532
  84.9 1.6 %collective-permute-start.19 = (bf16[1,256,640]{2,1,0:T(8,128)(2,1)}, bf16[1,256,640]{2,1,0:T(8,128)(2,1)}, u32[]{:S(2)}, u32[]{:S(2)}) collective-permute-start(bf16[1,256,640]{2,1,0:T(8,128)(2,1)} %get-tuple-element.59), channel_id=1, source_target_pairs={{0,1},{1,0},{2,3},{3,2},{4,5},{5,4},{6,7},{7,6},{8,9},{9,8},{10,11... | collective-permute-start | bytes 983048 | tf_op jit(solution)/shard_map/ppermute | solution.py:497
  86.5 2.6 %collective-permute-start.20 = (bf16[1,256,640]{2,1,0:T(8,128)(2,1)}, bf16[1,256,640]{2,1,0:T(8,128)(2,1)}, u32[]{:S(2)}, u32[]{:S(2)}) collective-permute-start(bf16[1,256,640]{2,1,0:T(8,128)(2,1)} %get-tuple-element.48), channel_id=1, source_target_pairs={{0,2},{1,3},{2,0},{3,1},{4,6},{5,7},{6,4},{7,5},{8,10},{9,11},{10,... | collective-permute-start | bytes 983048 | tf_op jit(solution)/shard_map/ppermute | solution.py:497
  91.0 9.8 %collective-permute-done.13.near_ref = bf16[272,1280]{1,0:T(8,128)(2,1)} collective-permute-done((bf16[272,1280]{1,0:T(8,128)(2,1)}, bf16[272,1280]{1,0:T(8,128)(2,1)}, u32[]{:S(2)}, u32[]{:S(2)}) %collective-permute-start.13) | collective-permute-done | bytes 696352 | tf_op jit(solution)/shard_map/ppermute | solution.py:532
  100.8 5.8 %cross_attention.1 = (bf16[256,640]{1,0:T(8,128)(2,1)}, bf16[256,640]{1,0:T(8,128)(2,1)}) custom-call(s32[1]{0:T(128)S(6)} %copy.14.prompt_ref, s32[1]{0:T(128)} %bitcast.3.side_ref, bf16[256,1280]{1,0:T(8,128)(2,1)} %q_ref.4, bf16[272,1280]{1,0:T(8,128)(2,1)} %collective-permute-done.13.near_ref, bf16[512,640]{1,0:T(8,128)(2,1)} %get-tuple-element.52.refs_0_, ...), custom_call_target="tpu_custom_call" | custom-call | flops 2307000064 | tf_op jit(solution)/shard_map/cross_attention/pallas_call | solution.py:175
  108.1 2.2 %add.12 = bf16[1,256,640]{2,1,0:T(8,128)(2,1)} custom-call(bf16[1,256,640]{2,1,0:T(8,128)(2,1)} %get-tuple-element.58.refs_0_, bf16[2,1,256,640]{3,2,1,0:T(8,128)(2,1)} %collective-permute-done.10.refs_1_, bf16[1,256,640]{2,1,0:T(8,128)(2,1)} %collective-permute-done.19.refs_2_, bf16[1,256,640]{2,1,0:T(8,128)(2,1)} %collective-permute-done.20.refs_3_), custom_call_target="tpu_custom_call" | custom-call | flops 115350003712 | tf_op jit(solution)/shard_map/add/pallas_call | solution.py:399
  110.4 5.4 %collective-permute-done.18 = bf16[256,640]{1,0:T(8,128)(2,1)} collective-permute-done((bf16[256,640]{1,0:T(8,128)(2,1)}, bf16[256,640]{1,0:T(8,128)(2,1)}, u32[]{:S(2)}, u32[]{:S(2)}) %collective-permute-start.18) | collective-permute-done | bytes 327712 | tf_op jit(solution)/shard_map/ppermute | solution.py:532
  115.8 2.3 %maximum_select_fusion.refs_2_ = bf16[256,1280]{1,0:T(8,128)(2,1)} fusion(bf16[256,640]{1,0:T(8,128)(2,1)} %collective-permute-done.18, bf16[256,640]{1,0:T(8,128)(2,1)} %get-tuple-element.56, pred[]{:T(512)S(6)} %eq.6), kind=kLoop, calls=%fused_computation | loop fusion | flops 2949120 | bytes 1310721 | tf_op jit(solution)/shard_map/jit(_where)/select_n | solution.py:573
  119.2 3.3 %finish.1 = bf16[256,1280]{1,0:T(8,128)(2,1)} custom-call(s32[1]{0:T(128)} %gate.1.side_ref, bf16[256,1280]{1,0:T(8,128)(2,1)} %hidden_ref.1, bf16[1,256,640]{2,1,0:T(8,128)(2,1)} %collective-permute-done.21.received_ref, bf16[1,256,640]{2,1,0:T(8,128)(2,1)} %get-tuple-element.61.refs_0_, bf16[2,1,256,640]{3,2,1,0:T(8,128)(2,1)} %collective-permute-done.10.refs_1_, ...), custom_call_target="tpu_custom_call" | custom-call | flops 2307000064 | tf_op jit(solution)/shard_map/finish/pallas_call | solution.py:477
  (29 shorter events, 8.4 us)
Async XLA Ops:
  0.6 22.4 %collective-permute-start.1 = (bf16[1280,640]{1,0:T(8,128)(2,1)}, bf16[1280,640]{1,0:T(8,128)(2,1)}, u32[]{:S(2)}, u32[]{:S(2)}) collective-permute-start(bf16[1280,640]{1,0:T(8,128)(2,1)} %refs_0_.1), channel_id=1, source_target_pairs={{0,16},{12,28},{16,0},{28,12},{4,8},{8,4},{20,24},{24,20},{1,17},{... | collective-permute-start | bytes 4915208 | tf_op jit(solution)/shard_map/ppermute | solution.py:536
  23.1 10.9 %collective-permute-start.3 = (bf16[1280,640]{1,0:T(8,128)(2,1)}, bf16[1280,640]{1,0:T(8,128)(2,1)}, u32[]{:S(2)}, u32[]{:S(2)}) collective-permute-start(bf16[1280,640]{1,0:T(8,128)(2,1)} %collective-permute-done.1.refs_2_.refs_5_), channel_id=1, source_target_pairs={{4,20},{8,24},{20,4},{24,8},{5,21},{9,25},{21,5},{25,9},{6,22},{10... | collective-permute-start | bytes 4915208 | tf_op jit(solution)/shard_map/ppermute | solution.py:547
  24.9 18.4 %collective-permute-start = (bf16[256,1280]{1,0:T(8,128)(2,1)}, bf16[256,1280]{1,0:T(8,128)(2,1)}, u32[]{:S(2)}, u32[]{:S(2)}) collective-permute-start(bf16[256,1280]{1,0:T(8,128)(2,1)} %self_attention.1.own_ref), channel_id=1, source_target_pairs={{0,8},{4,12},{8,0},{12,4},{16,24},{20,28},{24,16},{28,20},{1,9},{5... | collective-permute-start | bytes 1966088 | tf_op jit(solution)/shard_map/ppermute | solution.py:532
  28.0 25.3 %collective-permute-start.5 = (bf16[1280,640]{1,0:T(8,128)(2,1)}, bf16[1280,640]{1,0:T(8,128)(2,1)}, u32[]{:S(2)}, u32[]{:S(2)}) collective-permute-start(bf16[1280,640]{1,0:T(8,128)(2,1)} %refs_0_.1), channel_id=1, source_target_pairs={{0,4},{12,8},{16,20},{28,24},{1,5},{13,9},{17,21},{29,25},{2,6},{1... | collective-permute-start | bytes 4915208 | tf_op jit(solution)/shard_map/ppermute | solution.py:542
  34.0 19.8 %collective-permute-start.2 = (bf16[1280,640]{1,0:T(8,128)(2,1)}, bf16[1280,640]{1,0:T(8,128)(2,1)}, u32[]{:S(2)}, u32[]{:S(2)}) collective-permute-start(bf16[1280,640]{1,0:T(8,128)(2,1)} %collective-permute-done.1.refs_2_.refs_5_), channel_id=1, source_target_pairs={{0,4},{4,0},{8,12},{12,8},{16,20},{20,16},{24,28},{28,24},{1,5},{5... | collective-permute-start | bytes 4915208 | tf_op jit(solution)/shard_map/ppermute | solution.py:532
  43.3 10.5 %collective-permute-start.4 = (bf16[1280,640]{1,0:T(8,128)(2,1)}, bf16[1280,640]{1,0:T(8,128)(2,1)}, u32[]{:S(2)}, u32[]{:S(2)}) collective-permute-start(bf16[1280,640]{1,0:T(8,128)(2,1)} %collective-permute-done.3.refs_7_), channel_id=1, source_target_pairs={{4,0},{8,12},{20,16},{24,28},{5,1},{9,13},{21,17},{25,29},{6,2},{1... | collective-permute-start | bytes 4915208 | tf_op jit(solution)/shard_map/ppermute | solution.py:564
  44.8 30.0 %collective-permute-start.6 = (bf16[512,640]{1,0:T(8,128)(2,1)}, bf16[512,640]{1,0:T(8,128)(2,1)}, u32[]{:S(2)}, u32[]{:S(2)}) collective-permute-start(bf16[512,640]{1,0:T(8,128)(2,1)} %get-tuple-element.43), channel_id=1, source_target_pairs={{0,16},{4,20},{8,24},{12,28},{16,0},{20,4},{24,8},{28,12},{1,17},{... | collective-permute-start | bytes 1966088 | tf_op jit(solution)/shard_map/ppermute | solution.py:532
  45.4 34.7 %collective-permute-start.8 = (bf16[512,640]{1,0:T(8,128)(2,1)}, bf16[512,640]{1,0:T(8,128)(2,1)}, u32[]{:S(2)}, u32[]{:S(2)}) collective-permute-start(bf16[512,640]{1,0:T(8,128)(2,1)} %get-tuple-element.43), channel_id=1, source_target_pairs={{0,24},{4,28},{8,16},{12,20},{16,8},{20,12},{24,0},{28,4},{1,25},{... | collective-permute-start | bytes 1966088 | tf_op jit(solution)/shard_map/ppermute | solution.py:532
  53.3 26.8 %collective-permute-start.7 = (bf16[512,640]{1,0:T(8,128)(2,1)}, bf16[512,640]{1,0:T(8,128)(2,1)}, u32[]{:S(2)}, u32[]{:S(2)}) collective-permute-start(bf16[512,640]{1,0:T(8,128)(2,1)} %get-tuple-element.52.refs_0_), channel_id=1, source_target_pairs={{0,8},{4,12},{8,0},{12,4},{16,24},{20,28},{24,16},{28,20},{1,9},{5... | collective-permute-start | bytes 1966088 | tf_op jit(solution)/shard_map/ppermute | solution.py:532
  60.7 19.3 %collective-permute-start.9 = (bf16[2,1,256,640]{3,2,1,0:T(8,128)(2,1)}, bf16[2,1,256,640]{3,2,1,0:T(8,128)(2,1)}, u32[]{:S(2)}, u32[]{:S(2)}) collective-permute-start(bf16[2,1,256,640]{3,2,1,0:T(8,128)(2,1)} %get-tuple-element.46), channel_id=1, source_target_pairs={{0,1},{3,2},{4,5},{7,6},{8,9},{11,10},{12,13},{15,14},{16,17},{19,... | collective-permute-start | bytes 1966088 | tf_op jit(solution)/shard_map/ppermute | solution.py:497
  65.1 15.0 %collective-permute-start.10 = (bf16[2,1,256,640]{3,2,1,0:T(8,128)(2,1)}, bf16[2,1,256,640]{3,2,1,0:T(8,128)(2,1)}, u32[]{:S(2)}, u32[]{:S(2)}) collective-permute-start(bf16[2,1,256,640]{3,2,1,0:T(8,128)(2,1)} %get-tuple-element.46), channel_id=1, source_target_pairs={{1,2},{2,1},{5,6},{6,5},{9,10},{10,9},{13,14},{14,13},{17,18},{18,... | collective-permute-start | bytes 1966088 | tf_op jit(solution)/shard_map/ppermute | solution.py:497
  82.3 2.6 %collective-permute-start.14 = (bf16[512,640]{1,0:T(8,128)(2,1)}, bf16[512,640]{1,0:T(8,128)(2,1)}, u32[]{:S(2)}, u32[]{:S(2)}) collective-permute-start(bf16[512,640]{1,0:T(8,128)(2,1)} %get-tuple-element.52.refs_0_), channel_id=1, source_target_pairs={{0,4},{4,0},{8,12},{12,8},{16,20},{20,16},{24,28},{28,24},{1,5},{5... | collective-permute-start | bytes 1966088 | tf_op jit(solution)/shard_map/ppermute | solution.py:532
  82.4 4.1 %collective-permute-start.15 = (bf16[512,640]{1,0:T(8,128)(2,1)}, bf16[512,640]{1,0:T(8,128)(2,1)}, u32[]{:S(2)}, u32[]{:S(2)}) collective-permute-start(bf16[512,640]{1,0:T(8,128)(2,1)} %collective-permute-done.6.refs_1_), channel_id=1, source_target_pairs={{0,4},{4,0},{8,12},{12,8},{16,20},{20,16},{24,28},{28,24},{1,5},{5... | collective-permute-start | bytes 1966088 | tf_op jit(solution)/shard_map/ppermute | solution.py:532
  82.9 17.9 %collective-permute-start.13 = (bf16[272,1280]{1,0:T(8,128)(2,1)}, bf16[272,1280]{1,0:T(8,128)(2,1)}, u32[]{:S(2)}, u32[]{:S(2)}) collective-permute-start(bf16[272,1280]{1,0:T(8,128)(2,1)} %get-tuple-element.51), channel_id=1, source_target_pairs={{0,16},{4,20},{8,24},{12,28},{16,0},{20,4},{24,8},{28,12},{1,17},{... | collective-permute-start | bytes 2088968 | tf_op jit(solution)/shard_map/ppermute | solution.py:532
  84.4 4.7 %collective-permute-start.16 = (bf16[512,640]{1,0:T(8,128)(2,1)}, bf16[512,640]{1,0:T(8,128)(2,1)}, u32[]{:S(2)}, u32[]{:S(2)}) collective-permute-start(bf16[512,640]{1,0:T(8,128)(2,1)} %collective-permute-done.7.refs_2_), channel_id=1, source_target_pairs={{0,4},{4,0},{8,12},{12,8},{16,20},{20,16},{24,28},{28,24},{1,5},{5... | collective-permute-start | bytes 1966088 | tf_op jit(solution)/shard_map/ppermute | solution.py:532
  84.4 5.5 %collective-permute-start.17 = (bf16[512,640]{1,0:T(8,128)(2,1)}, bf16[512,640]{1,0:T(8,128)(2,1)}, u32[]{:S(2)}, u32[]{:S(2)}) collective-permute-start(bf16[512,640]{1,0:T(8,128)(2,1)} %collective-permute-done.8.refs_3_), channel_id=1, source_target_pairs={{0,4},{4,0},{8,12},{12,8},{16,20},{20,16},{24,28},{28,24},{1,5},{5... | collective-permute-start | bytes 1966088 | tf_op jit(solution)/shard_map/ppermute | solution.py:532
  84.9 23.2 %collective-permute-start.19 = (bf16[1,256,640]{2,1,0:T(8,128)(2,1)}, bf16[1,256,640]{2,1,0:T(8,128)(2,1)}, u32[]{:S(2)}, u32[]{:S(2)}) collective-permute-start(bf16[1,256,640]{2,1,0:T(8,128)(2,1)} %get-tuple-element.59), channel_id=1, source_target_pairs={{0,1},{1,0},{2,3},{3,2},{4,5},{5,4},{6,7},{7,6},{8,9},{9,8},{10,11... | collective-permute-start | bytes 983048 | tf_op jit(solution)/shard_map/ppermute | solution.py:497
  86.5 21.6 %collective-permute-start.20 = (bf16[1,256,640]{2,1,0:T(8,128)(2,1)}, bf16[1,256,640]{2,1,0:T(8,128)(2,1)}, u32[]{:S(2)}, u32[]{:S(2)}) collective-permute-start(bf16[1,256,640]{2,1,0:T(8,128)(2,1)} %get-tuple-element.48), channel_id=1, source_target_pairs={{0,2},{1,3},{2,0},{3,1},{4,6},{5,7},{6,4},{7,5},{8,10},{9,11},{10,... | collective-permute-start | bytes 983048 | tf_op jit(solution)/shard_map/ppermute | solution.py:497
  89.1 29.0 %collective-permute-start.11 = (bf16[1,256,640]{2,1,0:T(8,128)(2,1)}, bf16[1,256,640]{2,1,0:T(8,128)(2,1)}, u32[]{:S(2)}, u32[]{:S(2)}) collective-permute-start(bf16[1,256,640]{2,1,0:T(8,128)(2,1)} %get-tuple-element.49), channel_id=1, source_target_pairs={{0,1},{1,0},{2,3},{3,2},{4,5},{5,4},{6,7},{7,6},{8,9},{9,8},{10,11... | collective-permute-start | bytes 983048 | tf_op jit(solution)/shard_map/ppermute | solution.py:497
  89.9 28.3 %collective-permute-start.12 = (bf16[1,256,640]{2,1,0:T(8,128)(2,1)}, bf16[1,256,640]{2,1,0:T(8,128)(2,1)}, u32[]{:S(2)}, u32[]{:S(2)}) collective-permute-start(bf16[1,256,640]{2,1,0:T(8,128)(2,1)} %get-tuple-element.50), channel_id=1, source_target_pairs={{0,2},{1,3},{2,0},{3,1},{4,6},{5,7},{6,4},{7,5},{8,10},{9,11},{10,... | collective-permute-start | bytes 983048 | tf_op jit(solution)/shard_map/ppermute | solution.py:497
  106.6 9.2 %collective-permute-start.18 = (bf16[256,640]{1,0:T(8,128)(2,1)}, bf16[256,640]{1,0:T(8,128)(2,1)}, u32[]{:S(2)}, u32[]{:S(2)}) collective-permute-start(bf16[256,640]{1,0:T(8,128)(2,1)} %get-tuple-element.57), channel_id=1, source_target_pairs={{0,16},{4,20},{8,24},{12,28},{16,0},{20,4},{24,8},{28,12},{1,17},{... | collective-permute-start | bytes 983048 | tf_op jit(solution)/shard_map/ppermute | solution.py:532
  110.3 9.0 %collective-permute-start.21 = (bf16[1,256,640]{2,1,0:T(8,128)(2,1)}, bf16[1,256,640]{2,1,0:T(8,128)(2,1)}, u32[]{:S(2)}, u32[]{:S(2)}) collective-permute-start(bf16[1,256,640]{2,1,0:T(8,128)(2,1)} %add.12), channel_id=1, source_target_pairs={{0,8},{4,12},{8,0},{12,4},{16,24},{20,28},{24,16},{28,20},{1,9},{5... | collective-permute-start | bytes 983048 | tf_op jit(solution)/shard_map/ppermute | solution.py:532

commit v9 on v8

--- a/solution.py
+++ b/solution.py
@@ -183,20 +183,20 @@
     )(prompt, side.reshape(1), queries, near, *pieces)
 
 
-def gate_kernel(value_ref, *refs):
-    refs[-1][0] = value_ref[0]
-
-
-def gate(value, *waited):
-    scalars = pl.BlockSpec(memory_space=pltpu.SMEM)
+def gate_kernel(*refs):
+    refs[-1][...] = jnp.zeros_like(refs[-1])
+
+
+def gate(*waited):
     return pl.pallas_call(
         gate_kernel,
-        in_specs=[scalars] + [pl.BlockSpec(memory_space=pltpu.HBM)] * len(waited),
-        out_specs=scalars,
-        out_shape=jax.ShapeDtypeStruct((1,), jnp.int32),
+        in_specs=[pl.BlockSpec(memory_space=pltpu.HBM)] * len(waited),
+        out_specs=pl.BlockSpec(memory_space=pltpu.VMEM),
+        out_shape=jax.ShapeDtypeStruct((8, HD), jnp.float32),
+        compiler_params=pltpu.CompilerParams(vmem_limit_bytes=VMEM_LIMIT),
         cost_estimate=cost_of(100e-6),
         name="gate",
-    )(value.reshape(1), *waited)
+    )(*waited)
 
 
 def pack_kernel(side_ref, prompt_ref, k_ref, v_ref, q_ref, keep_ref, give_ref, ask_ref):
@@ -434,12 +434,14 @@
     )(near, own, far)
 
 
-def finish_kernel(halves, side_ref, hidden_ref, received_ref, *refs):
+def finish_kernel(halves, gates, *refs):
+    hidden_ref, received_ref, *refs = refs[gates:]
+    side = lax.rem(lax.div(lax.axis_index("req"), 2), 2)
     o_ref, rest, kept_part, near_part, parts, sems, out_sems = refs[-7:]
     sources = [ref if half is None else ref.at[half] for ref, half in zip(refs, halves)]
     half = received_ref.shape[2]
-    kept = pl.ds(pl.multiple_of(side_ref[0] * half, HD), half)
-    other = pl.ds(pl.multiple_of((1 - side_ref[0]) * half, HD), half)
+    kept = pl.ds(pl.multiple_of(side * half, HD), half)
+    other = pl.ds(pl.multiple_of((1 - side) * half, HD), half)
     copies = [
         pltpu.make_async_copy(hidden_ref.at[:, other], rest.at[0], sems.at[0]),
         pltpu.make_async_copy(received_ref.at[0], near_part, sems.at[1]),
@@ -469,14 +471,14 @@
         copy.wait()
 
 
-def finish(side, hidden, received, parts):
+def finish(hidden, received, parts, waited):
     halves = tuple(part[1] if isinstance(part, tuple) else None for part in parts)
     parts = [part[0] if isinstance(part, tuple) else part for part in parts]
     hbm = pl.BlockSpec(memory_space=pltpu.HBM)
     half = received.shape[1:]
     return pl.pallas_call(
-        functools.partial(finish_kernel, halves),
-        in_specs=[pl.BlockSpec(memory_space=pltpu.SMEM)] + [hbm] * (2 + len(parts)),
+        functools.partial(finish_kernel, halves, len(waited)),
+        in_specs=[hbm] * (2 + len(parts) + len(waited)),
         out_specs=hbm,
         out_shape=jax.ShapeDtypeStruct(hidden.shape, hidden.dtype),
         scratch_shapes=[
@@ -490,7 +492,7 @@
         compiler_params=pltpu.CompilerParams(vmem_limit_bytes=VMEM_LIMIT),
         cost_estimate=cost_of(2e-6),
         name="finish",
-    )(side.reshape(1), hidden, received, *parts)
+    )(*waited, hidden, received, *parts)
 
 
 def to_tp(value, pairs):
@@ -596,13 +598,13 @@
         given = add(near_terms[0], (inner, 0), near_outer, near_crossing)
         own_parts = [own_terms[0], (inner, 1), own_outer, own_crossing]
         cross_heads = in_order(text_side, mine, answer, 1)
-        side = gate(side, own_outer, own_crossing, cross_heads)
+        waited = [gate(own_outer, own_crossing, cross_heads)]
     else:
         near_parts = [
             [part[0]] + [to_tp(part[d], apart(tps, d)) for d in range(1, tps)]
             for part in (terms[:tps], terms[tps:])
         ]
-        given, own_parts = add(*near_parts[0]), near_parts[1]
+        given, own_parts, waited = add(*near_parts[0]), near_parts[1], []
         if split_heads:
             pieces += [swap(piece, 1) for piece in pieces]
             asked = swap(ask, 4)
@@ -615,7 +617,7 @@
 
     received = swap(given, 2)
     if received.shape[0] == 1 and received.shape[2] % HD == 0:
-        return finish(side, hidden, received, own_parts), cross_heads
+        return finish(hidden, received, own_parts, waited), cross_heads
     ordered = in_order(side, add(*own_parts), received, 2).transpose(1, 0, 2).reshape(rows, width)
     hidden_out = (hidden.astype(jnp.float32) + ordered.astype(jnp.float32)).astype(jnp.bfloat16)
     return (hidden_out, cross_heads)

time: 123 us -> 122 us (level)
  transfers between devices with their start and end apart: 22 -> 22, of which waited for: 8 -> 8; matrix products, arithmetic and copies ran while one was open for 2% -> 2% of each run, Pallas kernels for 23% -> 24%
where the time goes in v9:
time: 122 us
  waiting for transfers between devices  47.6 us (39%)
  starting transfers between devices  37.1 us (30%)
  Pallas kernels  33.6 us (28%)
  other arithmetic  2.27 us (2%)
  between operations  1.52 us (1%)
    ppermute x12, waiting for transfers between devices, swap(): return lax.ppermute(array, 'req', [(i, i ^ distance) for i in range(reqs)])  38.3 us
    ppermute x12, starting transfers between devices, swap(): return lax.ppermute(array, 'req', [(i, i ^ distance) for i in range(reqs)])  16.3 us
    ppermute x6, starting transfers between devices, to_tp(): return lax.ppermute(value, 'tp', pairs)  12 us
    pallas_call x1, Pallas kernels, self_attention(): pl.pallas_call(functools.partial(self_kernel, block_rows, heads), grid_sp...  10.4 us
    ppermute x1, waiting for transfers between devices, per_device(): lax.ppermute(w_out, 'req', [(first_of[i], first_of[i ^ 2]) for i in range...  9.01 us
    pallas_call x1, Pallas kernels, project(): pl.pallas_call(functools.partial(project_kernel, count, flat, tps, joint)...  6.85 us
    pallas_call x1, Pallas kernels, cross_attention(): pl.pallas_call(functools.partial(cross_kernel, half // HD, len(pieces), s...  5.81 us
    ppermute x1, starting transfers between devices, per_device(): lax.ppermute(w_out, 'req', [(first_of[i], first_of[i ^ 2]) for i in range...  3.03 us
  transfers between devices with their start and end apart: 22, of which 8 were waited for; matrix products, arithmetic and copies ran while one was open for 2% of the time, Pallas kernels for 24%

profile of v9, /device:TPU:0, one launch (start us, length us, event | category | flops | bytes accessed | tf_op | source)
XLA Modules:
  0.0 122.0 jit_solution(14501538324287604335)
XLA Ops:
  0.6 3.0 %collective-permute-start.1 = (bf16[1280,640]{1,0:T(8,128)(2,1)}, bf16[1280,640]{1,0:T(8,128)(2,1)}, u32[]{:S(2)}, u32[]{:S(2)}) collective-permute-start(bf16[1280,640]{1,0:T(8,128)(2,1)} %refs_0_.1), channel_id=1, source_target_pairs={{0,16},{12,28},{16,0},{28,12},{4,8},{8,4},{20,24},{24,20},{1,17},{... | collective-permute-start | bytes 4915208 | tf_op jit(solution)/shard_map/ppermute | solution.py:538
  3.7 10.4 %self_attention.1.own_ref = bf16[256,1280]{1,0:T(8,128)(2,1)} custom-call(s32[8]{0:T(128)} %length_ref.1, bf16[256,1280]{1,0:T(8,128)(2,1)} %q_ref.2, bf16[256,1280]{1,0:T(8,128)(2,1)} %kn_ref.1, bf16[256,1280]{1,0:T(8,128)(2,1)} %vn_ref.1, bf16[4096,1280]{1,0:T(8,128)(2,1)} %bitcast.3, bf16[4096,1280]{1,0:T(8,128)(2,1)} %bitcast.4), custom_call_target="tpu_custom_call" | custom-call | flops 23069999104 | tf_op jit(solution)/shard_map/self_attention/pallas_call | solution.py:123
  14.1 9.0 %collective-permute-done.1.refs_2_.refs_5_ = bf16[1280,640]{1,0:T(8,128)(2,1)} collective-permute-done((bf16[1280,640]{1,0:T(8,128)(2,1)}, bf16[1280,640]{1,0:T(8,128)(2,1)}, u32[]{:S(2)}, u32[]{:S(2)}) %collective-permute-start.1) | collective-permute-done | bytes 1638432 | tf_op jit(solution)/shard_map/ppermute | solution.py:538
  23.1 1.8 %collective-permute-start.3 = (bf16[1280,640]{1,0:T(8,128)(2,1)}, bf16[1280,640]{1,0:T(8,128)(2,1)}, u32[]{:S(2)}, u32[]{:S(2)}) collective-permute-start(bf16[1280,640]{1,0:T(8,128)(2,1)} %collective-permute-done.1.refs_2_.refs_5_), channel_id=1, source_target_pairs={{4,20},{8,24},{20,4},{24,8},{5,21},{9,25},{21,5},{25,9},{6,22},{10... | collective-permute-start | bytes 4915208 | tf_op jit(solution)/shard_map/ppermute | solution.py:549
  24.9 3.1 %collective-permute-start = (bf16[256,1280]{1,0:T(8,128)(2,1)}, bf16[256,1280]{1,0:T(8,128)(2,1)}, u32[]{:S(2)}, u32[]{:S(2)}) collective-permute-start(bf16[256,1280]{1,0:T(8,128)(2,1)} %self_attention.1.own_ref), channel_id=1, source_target_pairs={{0,8},{4,12},{8,0},{12,4},{16,24},{20,28},{24,16},{28,20},{1,9},{5... | collective-permute-start | bytes 1966088 | tf_op jit(solution)/shard_map/ppermute | solution.py:534
  28.0 2.5 %collective-permute-start.5 = (bf16[1280,640]{1,0:T(8,128)(2,1)}, bf16[1280,640]{1,0:T(8,128)(2,1)}, u32[]{:S(2)}, u32[]{:S(2)}) collective-permute-start(bf16[1280,640]{1,0:T(8,128)(2,1)} %refs_0_.1), channel_id=1, source_target_pairs={{0,4},{12,8},{16,20},{28,24},{1,5},{13,9},{17,21},{29,25},{2,6},{1... | collective-permute-start | bytes 4915208 | tf_op jit(solution)/shard_map/ppermute | solution.py:544
  31.1 2.9 %pack.1 = (bf16[512,640]{1,0:T(8,128)(2,1)}, bf16[512,640]{1,0:T(8,128)(2,1)}, bf16[272,1280]{1,0:T(8,128)(2,1)}) custom-call(s32[1]{0:T(128)} %bitcast.2.side_ref, s32[1]{0:T(128)S(6)} %copy.14.prompt_ref, bf16[4,64,1280]{2,1,0:T(8,128)(2,1)} %k_ref.1, bf16[4,64,1280]{2,1,0:T(8,128)(2,1)} %v_ref.1, bf16[256,1280]{1,0:T(8,128)(2,1)} %q_ref.4), custom_call_target="tpu_custom_call" | custom-call | flops 3460499968 | tf_op jit(solution)/shard_map/pack/pallas_call | solution.py:226
  34.0 9.3 %collective-permute-done.near_ref = bf16[256,1280]{1,0:T(8,128)(2,1)} collective-permute-done((bf16[256,1280]{1,0:T(8,128)(2,1)}, bf16[256,1280]{1,0:T(8,128)(2,1)}, u32[]{:S(2)}, u32[]{:S(2)}) %collective-permute-start) | collective-permute-done | bytes 655392 | tf_op jit(solution)/shard_map/ppermute | solution.py:534
  45.4 7.9 %collective-permute-start.8 = (bf16[512,640]{1,0:T(8,128)(2,1)}, bf16[512,640]{1,0:T(8,128)(2,1)}, u32[]{:S(2)}, u32[]{:S(2)}) collective-permute-start(bf16[512,640]{1,0:T(8,128)(2,1)} %get-tuple-element.43), channel_id=1, source_target_pairs={{0,24},{4,28},{8,16},{12,20},{16,8},{20,12},{24,0},{28,4},{1,25},{... | collective-permute-start | bytes 1966088 | tf_op jit(solution)/shard_map/ppermute | solution.py:534
  53.9 6.8 %project.1 = (bf16[1,256,640]{2,1,0:T(8,128)(2,1)}, bf16[1,256,640]{2,1,0:T(8,128)(2,1)}, bf16[1,256,640]{2,1,0:T(8,128)(2,1)}, bf16[1,256,640]{2,1,0:T(8,128)(2...) custom-call(bf16[256,1280]{1,0:T(8,128)(2,1)} %self_attention.1.own_ref, ...), custom_call_target="tpu_custom_call" | custom-call | flops 11534999552 | tf_op jit(solution)/shard_map/project/pallas_call | solution.py:352
  60.7 4.4 %collective-permute-start.9 = (bf16[2,1,256,640]{3,2,1,0:T(8,128)(2,1)}, bf16[2,1,256,640]{3,2,1,0:T(8,128)(2,1)}, u32[]{:S(2)}, u32[]{:S(2)}) collective-permute-start(bf16[2,1,256,640]{3,2,1,0:T(8,128)(2,1)} %get-tuple-element.46), channel_id=1, source_target_pairs={{0,1},{3,2},{4,5},{7,6},{8,9},{11,10},{12,13},{15,14},{16,17},{19,... | collective-permute-start | bytes 1966088 | tf_op jit(solution)/shard_map/ppermute | solution.py:499
  65.1 1.5 %collective-permute-start.10 = (bf16[2,1,256,640]{3,2,1,0:T(8,128)(2,1)}, bf16[2,1,256,640]{3,2,1,0:T(8,128)(2,1)}, u32[]{:S(2)}, u32[]{:S(2)}) collective-permute-start(bf16[2,1,256,640]{3,2,1,0:T(8,128)(2,1)} %get-tuple-element.46), channel_id=1, source_target_pairs={{1,2},{2,1},{5,6},{6,5},{9,10},{10,9},{13,14},{14,13},{17,18},{18,... | collective-permute-start | bytes 1966088 | tf_op jit(solution)/shard_map/ppermute | solution.py:499
  66.6 8.2 %collective-permute-done.6.refs_1_ = bf16[512,640]{1,0:T(8,128)(2,1)} collective-permute-done((bf16[512,640]{1,0:T(8,128)(2,1)}, bf16[512,640]{1,0:T(8,128)(2,1)}, u32[]{:S(2)}, u32[]{:S(2)}) %collective-permute-start.6) | collective-permute-done | bytes 655392 | tf_op jit(solution)/shard_map/ppermute | solution.py:534
  74.8 5.3 %collective-permute-done.7.refs_2_ = bf16[512,640]{1,0:T(8,128)(2,1)} collective-permute-done((bf16[512,640]{1,0:T(8,128)(2,1)}, bf16[512,640]{1,0:T(8,128)(2,1)}, u32[]{:S(2)}, u32[]{:S(2)}) %collective-permute-start.7) | collective-permute-done | bytes 655392 | tf_op jit(solution)/shard_map/ppermute | solution.py:534
  80.1 2.2 %join.1 = (bf16[1,256,640]{2,1,0:T(8,128)(2,1)}, bf16[1,256,640]{2,1,0:T(8,128)(2,1)}) custom-call(bf16[1,256,640]{2,1,0:T(8,128)(2,1)} %get-tuple-element.44.near_ref, bf16[1,256,640]{2,1,0:T(8,128)(2,1)} %get-tuple-element.45.own_ref, bf16[2,1,256,640]{3,2,1,0:T(8,128)(2,1)} %collective-permute-done.9.far_ref), custom_call_target="tpu_custom_call" | custom-call | flops 115350003712 | tf_op jit(solution)/shard_map/join/pallas_call | solution.py:422
  82.9 1.5 %collective-permute-start.13 = (bf16[272,1280]{1,0:T(8,128)(2,1)}, bf16[272,1280]{1,0:T(8,128)(2,1)}, u32[]{:S(2)}, u32[]{:S(2)}) collective-permute-start(bf16[272,1280]{1,0:T(8,128)(2,1)} %get-tuple-element.51), channel_id=1, source_target_pairs={{0,16},{4,20},{8,24},{12,28},{16,0},{20,4},{24,8},{28,12},{1,17},{... | collective-permute-start | bytes 2088968 | tf_op jit(solution)/shard_map/ppermute | solution.py:534
  84.9 1.6 %collective-permute-start.19 = (bf16[1,256,640]{2,1,0:T(8,128)(2,1)}, bf16[1,256,640]{2,1,0:T(8,128)(2,1)}, u32[]{:S(2)}, u32[]{:S(2)}) collective-permute-start(bf16[1,256,640]{2,1,0:T(8,128)(2,1)} %get-tuple-element.59), channel_id=1, source_target_pairs={{0,1},{1,0},{2,3},{3,2},{4,5},{5,4},{6,7},{7,6},{8,9},{9,8},{10,11... | collective-permute-start | bytes 983048 | tf_op jit(solution)/shard_map/ppermute | solution.py:499
  86.5 2.6 %collective-permute-start.20 = (bf16[1,256,640]{2,1,0:T(8,128)(2,1)}, bf16[1,256,640]{2,1,0:T(8,128)(2,1)}, u32[]{:S(2)}, u32[]{:S(2)}) collective-permute-start(bf16[1,256,640]{2,1,0:T(8,128)(2,1)} %get-tuple-element.48), channel_id=1, source_target_pairs={{0,2},{1,3},{2,0},{3,1},{4,6},{5,7},{6,4},{7,5},{8,10},{9,11},{10,... | collective-permute-start | bytes 983048 | tf_op jit(solution)/shard_map/ppermute | solution.py:499
  91.0 9.8 %collective-permute-done.13.near_ref = bf16[272,1280]{1,0:T(8,128)(2,1)} collective-permute-done((bf16[272,1280]{1,0:T(8,128)(2,1)}, bf16[272,1280]{1,0:T(8,128)(2,1)}, u32[]{:S(2)}, u32[]{:S(2)}) %collective-permute-start.13) | collective-permute-done | bytes 696352 | tf_op jit(solution)/shard_map/ppermute | solution.py:534
  100.8 5.8 %cross_attention.1 = (bf16[256,640]{1,0:T(8,128)(2,1)}, bf16[256,640]{1,0:T(8,128)(2,1)}) custom-call(s32[1]{0:T(128)S(6)} %copy.14.prompt_ref, s32[1]{0:T(128)} %bitcast.2.side_ref, bf16[256,1280]{1,0:T(8,128)(2,1)} %q_ref.4, bf16[272,1280]{1,0:T(8,128)(2,1)} %collective-permute-done.13.near_ref, bf16[512,640]{1,0:T(8,128)(2,1)} %get-tuple-element.52.refs_0_, ...), custom_call_target="tpu_custom_call" | custom-call | flops 2307000064 | tf_op jit(solution)/shard_map/cross_attention/pallas_call | solution.py:175
  108.1 2.2 %add.8 = bf16[1,256,640]{2,1,0:T(8,128)(2,1)} custom-call(bf16[1,256,640]{2,1,0:T(8,128)(2,1)} %get-tuple-element.58.refs_0_, bf16[2,1,256,640]{3,2,1,0:T(8,128)(2,1)} %collective-permute-done.10.refs_1_.refs_4_, bf16[1,256,640]{2,1,0:T(8,128)(2,1)} %collective-permute-done.19.refs_2_, bf16[1,256,640]{2,1,0:T(8,128)(2,1)} %collective-permute-done.20.refs_3_), custom_call_target="tpu_custom_call" | custom-call | flops 115350003712 | tf_op jit(solution)/shard_map/add/pallas_call | solution.py:399
  110.4 5.4 %collective-permute-done.18 = bf16[256,640]{1,0:T(8,128)(2,1)} collective-permute-done((bf16[256,640]{1,0:T(8,128)(2,1)}, bf16[256,640]{1,0:T(8,128)(2,1)}, u32[]{:S(2)}, u32[]{:S(2)}) %collective-permute-start.18) | collective-permute-done | bytes 327712 | tf_op jit(solution)/shard_map/ppermute | solution.py:534
  115.8 2.3 %maximum_select_fusion.refs_2_ = bf16[256,1280]{1,0:T(8,128)(2,1)} fusion(bf16[256,640]{1,0:T(8,128)(2,1)} %collective-permute-done.18, bf16[256,640]{1,0:T(8,128)(2,1)} %get-tuple-element.56, pred[]{:T(512)S(6)} %eq.5), kind=kLoop, calls=%fused_computation | loop fusion | flops 2949120 | bytes 1310721 | tf_op jit(solution)/shard_map/jit(_where)/select_n | solution.py:575
  119.2 2.6 %finish.1 = bf16[256,1280]{1,0:T(8,128)(2,1)} custom-call(f32[8,128]{1,0:T(8,128)} %gate.1.refs_0_, bf16[256,1280]{1,0:T(8,128)(2,1)} %refs_1_.1, bf16[1,256,640]{2,1,0:T(8,128)(2,1)} %collective-permute-done.21.refs_2_, bf16[1,256,640]{2,1,0:T(8,128)(2,1)} %get-tuple-element.61.refs_3_, bf16[2,1,256,640]{3,2,1,0:T(8,128)(2,1)} %collective-permute-done.10.refs_1_.refs_4_, ...), custom_call_target="tpu_custom_call" | custom-call | flops 2307000064 | tf_op jit(solution)/shard_map/finish/pallas_call | solution.py:479
  (29 shorter events, 8.4 us)
Async XLA Ops:
  0.6 22.4 %collective-permute-start.1 = (bf16[1280,640]{1,0:T(8,128)(2,1)}, bf16[1280,640]{1,0:T(8,128)(2,1)}, u32[]{:S(2)}, u32[]{:S(2)}) collective-permute-start(bf16[1280,640]{1,0:T(8,128)(2,1)} %refs_0_.1), channel_id=1, source_target_pairs={{0,16},{12,28},{16,0},{28,12},{4,8},{8,4},{20,24},{24,20},{1,17},{... | collective-permute-start | bytes 4915208 | tf_op jit(solution)/shard_map/ppermute | solution.py:538
  23.1 10.9 %collective-permute-start.3 = (bf16[1280,640]{1,0:T(8,128)(2,1)}, bf16[1280,640]{1,0:T(8,128)(2,1)}, u32[]{:S(2)}, u32[]{:S(2)}) collective-permute-start(bf16[1280,640]{1,0:T(8,128)(2,1)} %collective-permute-done.1.refs_2_.refs_5_), channel_id=1, source_target_pairs={{4,20},{8,24},{20,4},{24,8},{5,21},{9,25},{21,5},{25,9},{6,22},{10... | collective-permute-start | bytes 4915208 | tf_op jit(solution)/shard_map/ppermute | solution.py:549
  24.9 18.4 %collective-permute-start = (bf16[256,1280]{1,0:T(8,128)(2,1)}, bf16[256,1280]{1,0:T(8,128)(2,1)}, u32[]{:S(2)}, u32[]{:S(2)}) collective-permute-start(bf16[256,1280]{1,0:T(8,128)(2,1)} %self_attention.1.own_ref), channel_id=1, source_target_pairs={{0,8},{4,12},{8,0},{12,4},{16,24},{20,28},{24,16},{28,20},{1,9},{5... | collective-permute-start | bytes 1966088 | tf_op jit(solution)/shard_map/ppermute | solution.py:534
  28.0 25.3 %collective-permute-start.5 = (bf16[1280,640]{1,0:T(8,128)(2,1)}, bf16[1280,640]{1,0:T(8,128)(2,1)}, u32[]{:S(2)}, u32[]{:S(2)}) collective-permute-start(bf16[1280,640]{1,0:T(8,128)(2,1)} %refs_0_.1), channel_id=1, source_target_pairs={{0,4},{12,8},{16,20},{28,24},{1,5},{13,9},{17,21},{29,25},{2,6},{1... | collective-permute-start | bytes 4915208 | tf_op jit(solution)/shard_map/ppermute | solution.py:544
  34.0 19.8 %collective-permute-start.2 = (bf16[1280,640]{1,0:T(8,128)(2,1)}, bf16[1280,640]{1,0:T(8,128)(2,1)}, u32[]{:S(2)}, u32[]{:S(2)}) collective-permute-start(bf16[1280,640]{1,0:T(8,128)(2,1)} %collective-permute-done.1.refs_2_.refs_5_), channel_id=1, source_target_pairs={{0,4},{4,0},{8,12},{12,8},{16,20},{20,16},{24,28},{28,24},{1,5},{5... | collective-permute-start | bytes 4915208 | tf_op jit(solution)/shard_map/ppermute | solution.py:534
  43.3 10.5 %collective-permute-start.4 = (bf16[1280,640]{1,0:T(8,128)(2,1)}, bf16[1280,640]{1,0:T(8,128)(2,1)}, u32[]{:S(2)}, u32[]{:S(2)}) collective-permute-start(bf16[1280,640]{1,0:T(8,128)(2,1)} %collective-permute-done.3.refs_7_), channel_id=1, source_target_pairs={{4,0},{8,12},{20,16},{24,28},{5,1},{9,13},{21,17},{25,29},{6,2},{1... | collective-permute-start | bytes 4915208 | tf_op jit(solution)/shard_map/ppermute | solution.py:566
  44.8 30.0 %collective-permute-start.6 = (bf16[512,640]{1,0:T(8,128)(2,1)}, bf16[512,640]{1,0:T(8,128)(2,1)}, u32[]{:S(2)}, u32[]{:S(2)}) collective-permute-start(bf16[512,640]{1,0:T(8,128)(2,1)} %get-tuple-element.43), channel_id=1, source_target_pairs={{0,16},{4,20},{8,24},{12,28},{16,0},{20,4},{24,8},{28,12},{1,17},{... | collective-permute-start | bytes 1966088 | tf_op jit(solution)/shard_map/ppermute | solution.py:534
  45.4 34.7 %collective-permute-start.8 = (bf16[512,640]{1,0:T(8,128)(2,1)}, bf16[512,640]{1,0:T(8,128)(2,1)}, u32[]{:S(2)}, u32[]{:S(2)}) collective-permute-start(bf16[512,640]{1,0:T(8,128)(2,1)} %get-tuple-element.43), channel_id=1, source_target_pairs={{0,24},{4,28},{8,16},{12,20},{16,8},{20,12},{24,0},{28,4},{1,25},{... | collective-permute-start | bytes 1966088 | tf_op jit(solution)/shard_map/ppermute | solution.py:534
  53.3 26.8 %collective-permute-start.7 = (bf16[512,640]{1,0:T(8,128)(2,1)}, bf16[512,640]{1,0:T(8,128)(2,1)}, u32[]{:S(2)}, u32[]{:S(2)}) collective-permute-start(bf16[512,640]{1,0:T(8,128)(2,1)} %get-tuple-element.52.refs_0_), channel_id=1, source_target_pairs={{0,8},{4,12},{8,0},{12,4},{16,24},{20,28},{24,16},{28,20},{1,9},{5... | collective-permute-start | bytes 1966088 | tf_op jit(solution)/shard_map/ppermute | solution.py:534
  60.7 19.3 %collective-permute-start.9 = (bf16[2,1,256,640]{3,2,1,0:T(8,128)(2,1)}, bf16[2,1,256,640]{3,2,1,0:T(8,128)(2,1)}, u32[]{:S(2)}, u32[]{:S(2)}) collective-permute-start(bf16[2,1,256,640]{3,2,1,0:T(8,128)(2,1)} %get-tuple-element.46), channel_id=1, source_target_pairs={{0,1},{3,2},{4,5},{7,6},{8,9},{11,10},{12,13},{15,14},{16,17},{19,... | collective-permute-start | bytes 1966088 | tf_op jit(solution)/shard_map/ppermute | solution.py:499
  65.1 15.0 %collective-permute-start.10 = (bf16[2,1,256,640]{3,2,1,0:T(8,128)(2,1)}, bf16[2,1,256,640]{3,2,1,0:T(8,128)(2,1)}, u32[]{:S(2)}, u32[]{:S(2)}) collective-permute-start(bf16[2,1,256,640]{3,2,1,0:T(8,128)(2,1)} %get-tuple-element.46), channel_id=1, source_target_pairs={{1,2},{2,1},{5,6},{6,5},{9,10},{10,9},{13,14},{14,13},{17,18},{18,... | collective-permute-start | bytes 1966088 | tf_op jit(solution)/shard_map/ppermute | solution.py:499
  82.3 2.6 %collective-permute-start.14 = (bf16[512,640]{1,0:T(8,128)(2,1)}, bf16[512,640]{1,0:T(8,128)(2,1)}, u32[]{:S(2)}, u32[]{:S(2)}) collective-permute-start(bf16[512,640]{1,0:T(8,128)(2,1)} %get-tuple-element.52.refs_0_), channel_id=1, source_target_pairs={{0,4},{4,0},{8,12},{12,8},{16,20},{20,16},{24,28},{28,24},{1,5},{5... | collective-permute-start | bytes 1966088 | tf_op jit(solution)/shard_map/ppermute | solution.py:534
  82.4 4.1 %collective-permute-start.15 = (bf16[512,640]{1,0:T(8,128)(2,1)}, bf16[512,640]{1,0:T(8,128)(2,1)}, u32[]{:S(2)}, u32[]{:S(2)}) collective-permute-start(bf16[512,640]{1,0:T(8,128)(2,1)} %collective-permute-done.6.refs_1_), channel_id=1, source_target_pairs={{0,4},{4,0},{8,12},{12,8},{16,20},{20,16},{24,28},{28,24},{1,5},{5... | collective-permute-start | bytes 1966088 | tf_op jit(solution)/shard_map/ppermute | solution.py:534
  82.9 17.9 %collective-permute-start.13 = (bf16[272,1280]{1,0:T(8,128)(2,1)}, bf16[272,1280]{1,0:T(8,128)(2,1)}, u32[]{:S(2)}, u32[]{:S(2)}) collective-permute-start(bf16[272,1280]{1,0:T(8,128)(2,1)} %get-tuple-element.51), channel_id=1, source_target_pairs={{0,16},{4,20},{8,24},{12,28},{16,0},{20,4},{24,8},{28,12},{1,17},{... | collective-permute-start | bytes 2088968 | tf_op jit(solution)/shard_map/ppermute | solution.py:534
  84.4 4.7 %collective-permute-start.16 = (bf16[512,640]{1,0:T(8,128)(2,1)}, bf16[512,640]{1,0:T(8,128)(2,1)}, u32[]{:S(2)}, u32[]{:S(2)}) collective-permute-start(bf16[512,640]{1,0:T(8,128)(2,1)} %collective-permute-done.7.refs_2_), channel_id=1, source_target_pairs={{0,4},{4,0},{8,12},{12,8},{16,20},{20,16},{24,28},{28,24},{1,5},{5... | collective-permute-start | bytes 1966088 | tf_op jit(solution)/shard_map/ppermute | solution.py:534
  84.4 5.5 %collective-permute-start.17 = (bf16[512,640]{1,0:T(8,128)(2,1)}, bf16[512,640]{1,0:T(8,128)(2,1)}, u32[]{:S(2)}, u32[]{:S(2)}) collective-permute-start(bf16[512,640]{1,0:T(8,128)(2,1)} %collective-permute-done.8.refs_3_), channel_id=1, source_target_pairs={{0,4},{4,0},{8,12},{12,8},{16,20},{20,16},{24,28},{28,24},{1,5},{5... | collective-permute-start | bytes 1966088 | tf_op jit(solution)/shard_map/ppermute | solution.py:534
  84.9 23.2 %collective-permute-start.19 = (bf16[1,256,640]{2,1,0:T(8,128)(2,1)}, bf16[1,256,640]{2,1,0:T(8,128)(2,1)}, u32[]{:S(2)}, u32[]{:S(2)}) collective-permute-start(bf16[1,256,640]{2,1,0:T(8,128)(2,1)} %get-tuple-element.59), channel_id=1, source_target_pairs={{0,1},{1,0},{2,3},{3,2},{4,5},{5,4},{6,7},{7,6},{8,9},{9,8},{10,11... | collective-permute-start | bytes 983048 | tf_op jit(solution)/shard_map/ppermute | solution.py:499
  86.5 21.6 %collective-permute-start.20 = (bf16[1,256,640]{2,1,0:T(8,128)(2,1)}, bf16[1,256,640]{2,1,0:T(8,128)(2,1)}, u32[]{:S(2)}, u32[]{:S(2)}) collective-permute-start(bf16[1,256,640]{2,1,0:T(8,128)(2,1)} %get-tuple-element.48), channel_id=1, source_target_pairs={{0,2},{1,3},{2,0},{3,1},{4,6},{5,7},{6,4},{7,5},{8,10},{9,11},{10,... | collective-permute-start | bytes 983048 | tf_op jit(solution)/shard_map/ppermute | solution.py:499
  89.1 29.0 %collective-permute-start.11 = (bf16[1,256,640]{2,1,0:T(8,128)(2,1)}, bf16[1,256,640]{2,1,0:T(8,128)(2,1)}, u32[]{:S(2)}, u32[]{:S(2)}) collective-permute-start(bf16[1,256,640]{2,1,0:T(8,128)(2,1)} %get-tuple-element.49), channel_id=1, source_target_pairs={{0,1},{1,0},{2,3},{3,2},{4,5},{5,4},{6,7},{7,6},{8,9},{9,8},{10,11... | collective-permute-start | bytes 983048 | tf_op jit(solution)/shard_map/ppermute | solution.py:499
  89.9 28.3 %collective-permute-start.12 = (bf16[1,256,640]{2,1,0:T(8,128)(2,1)}, bf16[1,256,640]{2,1,0:T(8,128)(2,1)}, u32[]{:S(2)}, u32[]{:S(2)}) collective-permute-start(bf16[1,256,640]{2,1,0:T(8,128)(2,1)} %get-tuple-element.50), channel_id=1, source_target_pairs={{0,2},{1,3},{2,0},{3,1},{4,6},{5,7},{6,4},{7,5},{8,10},{9,11},{10,... | collective-permute-start | bytes 983048 | tf_op jit(solution)/shard_map/ppermute | solution.py:499
  106.6 9.2 %collective-permute-start.18 = (bf16[256,640]{1,0:T(8,128)(2,1)}, bf16[256,640]{1,0:T(8,128)(2,1)}, u32[]{:S(2)}, u32[]{:S(2)}) collective-permute-start(bf16[256,640]{1,0:T(8,128)(2,1)} %get-tuple-element.57), channel_id=1, source_target_pairs={{0,16},{4,20},{8,24},{12,28},{16,0},{20,4},{24,8},{28,12},{1,17},{... | collective-permute-start | bytes 983048 | tf_op jit(solution)/shard_map/ppermute | solution.py:534
  110.3 9.0 %collective-permute-start.21 = (bf16[1,256,640]{2,1,0:T(8,128)(2,1)}, bf16[1,256,640]{2,1,0:T(8,128)(2,1)}, u32[]{:S(2)}, u32[]{:S(2)}) collective-permute-start(bf16[1,256,640]{2,1,0:T(8,128)(2,1)} %add.8), channel_id=1, source_target_pairs={{0,8},{4,12},{8,0},{12,4},{16,24},{20,28},{24,16},{28,20},{1,9},{5... | collective-permute-start | bytes 983048 | tf_op jit(solution)/shard_map/ppermute | solution.py:534
